TPU v7x, 128 devices: a whole 4x4x4 slice. The times are simulated.
128 devices in a mesh: row: 8 (over x, core), col: 16 (over y, z).
Axes of the slice: x: 4, y: 4, z: 4, core: 2. Of those that a mesh axis runs over, the one named last changes fastest.
Arguments:
- hamiltonian: bfloat16 [5824, 5824], P('row', 'col'), may hold values from -6 to 6
- new_atom: int32 [448], replicated, may hold values from 0 to 447, as said below
- pattern: int32 [448, 448], P('row', 'col'), may hold values 0 or 1
Outputs:
- sign_matrix: float32 [5824, 5824], P('row', 'col')
Inputs may be any that keep to these rules, and one draw needn't show every extreme that they name: `new_atom`: each old atom appears once. Block column b holds atoms b * 28 to (b + 1) * 28 - 1 in both orders. For each new block column d and each v from 0 to 27, exactly one atom of new block column d comes from old block column (d - 1 - (v mod 16)) mod 16, so the number of atoms that old block column b sends to new block column (b + k) mod 16 is the number of such v with (1 + v) mod 16 = k.
All inputs are finite; a program needn't handle non-finite values. No bound on the sum of `pattern` on one device may be relied on, other than what follows from the above.
Results may differ from a plain program's by a relative error of at most 0.0029.
Values may be sent and summed in bfloat16 or wider, within the bound.
No kernel may reach another device: no remote copies, remote signals or barrier semaphores. Data moves between devices by JAX's collectives and lax.ppermute only.
A program may use at most 64 MiB of HBM per device.

v0:
```python
import functools

import jax
import jax.numpy as jnp
import numpy as np
from jax import lax
from jax.experimental import pallas as pl
from jax.experimental.pallas import tpu as pltpu
from jax.sharding import Mesh
from jax.sharding import PartitionSpec as P

NBF = 13
ROW = ("x", "c")
COL = ("y", "z")
BF = jnp.bfloat16
F32 = jnp.float32


def shift(n, by):
    return [(i, (i + by) % n) for i in range(n)]


def eq(left, right):
    return (left == right).astype(BF)


def exact(left, right, dims=(((1,), (0,)), ((), ()))):
    return lax.dot_general(left, right, dims, preferred_element_type=F32).astype(BF)


def slots_of(source, groups, per_group):
    same = source[:, :, None] == source[:, None, :]
    earlier = np.tril(np.ones((per_group, per_group), bool), -1)
    return jnp.sum((same & earlier[None]).astype(jnp.int32), axis=2)


def packed(new_atom, here, per_block, groups, slots):
    table = new_atom.reshape(groups, per_block)
    source = table // per_block
    rank = slots_of(source, groups, per_block)
    hit = (source == here)[:, None, :] & (rank[:, None, :] == np.arange(slots)[None, :, None])
    return jnp.sum(jnp.where(hit, (table - here * per_block)[:, None, :] + 1000, 0), axis=2) - 1000


def arrivals(new_atom, here, per_block):
    table = lax.dynamic_slice_in_dim(new_atom, here * per_block, per_block)
    source = table // per_block
    return source, slots_of(source[None], 1, per_block)[0]


TALL = 368
WIDE = 384


def multiply(panel, tall, wide, scale, index, blocks, scaled, epilogue, extra, out_shape, start=None):
    count = len(blocks)
    rows = panel.shape[1]

    def body(index_ref, scale_ref, panel_ref, tall_ref, wide_ref, *refs):
        block_refs = refs[: 2 * count]
        out_refs, acc = refs[-1 - len(out_shape) : -1], refs[-1]
        rest = refs[2 * count : -1 - len(out_shape)]
        if start is not None:
            start_ref, rest = rest[0], rest[1:]
        step = pl.program_id(0)
        by = scale_ref[0, 0]

        @pl.when(step == 0)
        def _():
            acc[...] = jnp.zeros_like(acc) if start is None else start_ref[...]

        kept = jnp.dot(tall_ref[...], wide_ref[0], preferred_element_type=F32) * by
        left = jnp.concatenate([panel_ref[0], panel_ref[1]], axis=1)
        left = (left.astype(F32) * kept).astype(BF)
        gap = jnp.zeros((WIDE - TALL, WIDE), BF)
        for j in range(count):

            @pl.when(step == j)
            def _(j=j):
                top, bottom = block_refs[2 * j][...], block_refs[2 * j + 1][...]
                if scaled:
                    top = (top.astype(F32) * by).astype(BF)
                    bottom = (bottom.astype(F32) * by).astype(BF)
                right = jnp.concatenate([top, gap, bottom, gap], axis=0)
                acc[...] += jnp.dot(left, right, preferred_element_type=F32)

        @pl.when(step == count - 1)
        def _():
            epilogue(acc, by, out_refs, *rest)

    whole = pl.BlockSpec(memory_space=pltpu.VMEM)
    operands = [b for pair in blocks for b in pair] + ([] if start is None else [start]) + extra
    return pl.pallas_call(
        body,
        out_shape=out_shape,
        grid_spec=pltpu.PrefetchScalarGridSpec(
            num_scalar_prefetch=1,
            grid=(count,),
            in_specs=[
                pl.BlockSpec(memory_space=pltpu.SMEM),
                pl.BlockSpec((2, rows, WIDE), lambda g, index: (index[g], 0, 0)),
                whole,
                pl.BlockSpec((1,) + wide.shape[1:], lambda g, index: (index[g], 0, 0)),
            ]
            + [whole] * len(operands),
            out_specs=[whole] * len(out_shape),
            scratch_shapes=[pltpu.VMEM((rows, WIDE), F32)],
        ),
        compiler_params=pltpu.CompilerParams(vmem_limit_bytes=40 * 2**20),
        cost_estimate=pl.CostEstimate(
            flops=2 * rows * 2 * WIDE * WIDE * count,
            bytes_accessed=count * 3 * rows * WIDE * 2,
            transcendentals=0,
        ),
    )(index, scale, panel, tall, wide, *operands)


def square_end(acc, by, out_refs, keep_ref):
    for part in range(2):
        at = pl.ds(part * TALL, TALL)
        out_refs[part][...] = (acc[at, :] * keep_ref[at, :].astype(F32)).astype(BF)


def keep_sum(acc, by, out_refs):
    out_refs[0][...] = acc[...]


def sign_end(acc, by, out_refs, keep_ref, top_ref, bottom_ref, pack_ref):
    first = jnp.concatenate([top_ref[...], bottom_ref[...]], axis=0)
    first = (first.astype(F32) * by).astype(BF).astype(F32)
    value = (keep_ref[...].astype(F32) * (1.5 * first - 0.5 * acc[...])).astype(BF)
    out_refs[0][...] = jnp.dot(pack_ref[...], value, preferred_element_type=F32).astype(BF)


def unpack_body(place_ref, arrived_ref, out_ref):
    value = jnp.dot(place_ref[...], arrived_ref[...], preferred_element_type=F32)
    out_ref[...] = value[:, : out_ref.shape[1]]


def send(array, axis, by):
    return lax.ppermute(array, axis, shift(2 if axis == "c" else 4, by))


def around(array, axis):
    return [array] + [send(array, axis, by) for by in (1, 2, 3)]


def column_panel(top, bottom):
    before = (send(top, "x", 1), send(bottom, "x", 1))
    after = (send(top, "x", 3), send(bottom, "x", 3))
    opposite = (send(before[0], "x", 1), send(after[1], "x", 3))
    near = [(top, bottom), before, after]
    near = near + [tuple(send(half, "c", 1) for half in pair) for pair in near]
    far = [opposite, tuple(send(half, "c", 1) for half in opposite)]
    return near, far


def on_device(hamiltonian, new_atom, pattern):
    rows_here, cols_here = hamiltonian.shape
    row_count, col_count = 8, 16
    atoms_row, atoms_col = pattern.shape
    order_all = rows_here * row_count
    slots_col = -(-atoms_col // col_count)
    counts = np.bincount((1 + np.arange(atoms_col)) % col_count, minlength=col_count)
    targets = (np.arange(2)[:, None] + np.arange(col_count)[None, :]) % col_count // 2
    slots_row = max(int(np.sum((targets == t) * counts[None, :])) for t in range(row_count))
    x, c = lax.axis_index("x"), lax.axis_index("c")
    y, z = lax.axis_index("y"), lax.axis_index("z")
    row_here, col_here = 2 * x + c, 4 * y + z
    half = rows_here // 2
    pads = ((0, TALL - half), (0, WIDE - cols_here))
    padded = jnp.concatenate([jnp.pad(hamiltonian[:half], pads), jnp.pad(hamiltonian[half:], pads)])
    panel = lax.all_gather(padded, COL, axis=0)

    width = 32
    base = packed(new_atom, col_here, atoms_col, col_count, slots_col)
    spots = (base[:, :, None] * NBF + np.arange(NBF)).reshape(col_count, slots_col * NBF)
    column = jnp.pad(spots, ((0, 0), (0, width - slots_col * NBF)), constant_values=-1).reshape(-1)
    pick = eq(column[:, None], np.arange(WIDE)[None, :])
    outgoing = exact(pick, padded, (((1,), (1,)), ((), ())))
    arrived = lax.all_to_all(outgoing.reshape(col_count, width, 2 * TALL), COL, 0, 0)
    arrived = arrived.reshape(col_count * width, 2 * TALL)
    source, rank = arrivals(new_atom, col_here, atoms_col)
    spot = ((source * width + rank * NBF)[:, None] + np.arange(NBF)[None, :]).reshape(-1)
    spot = jnp.pad(spot, (0, WIDE - cols_here), constant_values=-1)
    place = eq(np.arange(col_count * width)[:, None], spot[None, :])
    moved = exact(arrived, place, (((0,), (0,)), ((), ())))

    own = pattern.astype(BF)
    strip = jnp.stack(around(jnp.stack([own, send(own, "c", 1)]), "x"))
    strip = strip.reshape(-1, atoms_col)
    rows_seen = jnp.stack([2 * jnp.mod(x - d, 4) + jnp.mod(c + o, 2) for d in range(4) for o in range(2)])
    atoms_seen = new_atom.reshape(row_count, atoms_row)[rows_seen].reshape(-1)
    old_row = row_here * atoms_row + np.arange(atoms_row)
    rows_pattern = exact(eq(old_row[:, None], atoms_seen[None, :]), strip)
    line = np.arange(2 * TALL) % TALL
    of_row = np.where(line < half, (np.arange(2 * TALL) // TALL * half + line) // NBF, -1)
    of_col = np.where(np.arange(WIDE) < cols_here, np.arange(WIDE) // NBF, -1)
    tall = eq(jnp.asarray(of_row)[:, None], np.arange(64)[None, :])
    broad = eq(np.arange(atoms_col)[:, None], jnp.asarray(of_col)[None, :])
    keep = exact(exact(tall[:, :atoms_row], rows_pattern), broad)
    right = moved * keep
    top, bottom = right[:TALL], right[TALL:]
    near, far = column_panel(top, bottom)

    part_sum = jnp.sum(jnp.square(right.astype(F32)))
    sent = jnp.concatenate(
        [rows_pattern.astype(F32), jnp.broadcast_to(part_sum, (8, atoms_col))], axis=0
    )
    seen = jnp.stack(around(jnp.stack(around(sent, "z")), "y"))
    seen = seen.reshape(col_count, atoms_row + 8, atoms_col)
    total = jnp.broadcast_to(jnp.sum(seen[:, atoms_row, 0]), (8, 128))
    total = total + send(total, "c", 1)
    total = sum(around(total, "x"))[:1, :1]
    scale = lax.rsqrt(total / order_all)
    cols_seen = jnp.stack([4 * jnp.mod(y - a, 4) + jnp.mod(z - b, 4) for a in range(4) for b in range(4)])
    atoms_seen = new_atom.reshape(col_count, atoms_col)[cols_seen].reshape(-1)
    all_cols = jnp.transpose(seen[:, :atoms_row], (1, 0, 2)).reshape(atoms_row, -1).astype(BF)
    all_cols = jnp.pad(all_cols, ((0, 64 - atoms_row), (0, 0)))
    old_col = np.where(of_col >= 0, np.arange(col_count)[:, None] * atoms_col + of_col, -1)
    old_col = jnp.asarray(old_col.reshape(row_count, 1, 2 * WIDE))
    wide = jnp.einsum(
        "ia,ran->rin", all_cols, eq(atoms_seen[None, :, None], old_col), preferred_element_type=F32
    ).astype(BF)

    def rho(step, other_core):
        return 2 * jnp.mod(x + step, 4) + jnp.mod(c + other_core, 2)

    near_index = jnp.stack([rho(d, o) for o in range(2) for d in (0, -1, 1)])
    far_index = jnp.stack([rho(2, o) for o in range(2)])
    half_block = jax.ShapeDtypeStruct((TALL, WIDE), BF)
    whole = pl.BlockSpec(memory_space=pltpu.VMEM)
    of_panel = functools.partial(multiply, panel, tall, wide, scale)
    square = of_panel(
        jnp.concatenate([near_index, far_index]), near + far, True, square_end, [keep], [half_block] * 2
    )
    near, far = column_panel(*square)
    partial = of_panel(
        near_index, near, False, keep_sum, [], [jax.ShapeDtypeStruct((2 * TALL, WIDE), F32)]
    )[0]
    base = packed(new_atom, row_here, atoms_row, row_count, slots_row)
    line = (base[:, :, None] * NBF + np.arange(NBF)).reshape(-1)
    row_of = np.where(of_row >= 0, np.arange(2 * TALL) - (np.arange(2 * TALL) // TALL) * (TALL - half), -1)
    pack_rows = eq(line[:, None], jnp.asarray(row_of)[None, :])
    sent_rows = of_panel(
        far_index, far, False, sign_end, [keep, top, bottom, pack_rows],
        [jax.ShapeDtypeStruct((row_count * slots_row * NBF, WIDE), BF)],
        start=partial,
    )[0]
    got_rows = lax.all_to_all(sent_rows.reshape(row_count, slots_row * NBF, WIDE), ROW, 0, 0)
    got_rows = got_rows.reshape(-1, WIDE)
    source, rank = arrivals(new_atom, row_here, atoms_row)
    spot = (((source * slots_row + rank) * NBF)[:, None] + np.arange(NBF)).reshape(-1)
    place_rows = eq(spot[:, None], np.arange(row_count * slots_row * NBF)[None, :])
    return pl.pallas_call(
        unpack_body,
        out_shape=jax.ShapeDtypeStruct((rows_here, cols_here), F32),
        in_specs=[whole, whole],
        out_specs=whole,
    )(place_rows, got_rows)


def solution(mesh):
    split = Mesh(mesh.devices.reshape(4, 2, 4, 4), ("x", "c", "y", "z"))
    return jax.shard_map(
        on_device,
        mesh=split,
        in_specs=(P(ROW, COL), P(), P(ROW, COL)),
        out_specs=P(ROW, COL),
        check_vma=False,
    )
```

profile of v0, /device:TPU:1, one launch (start us, length us, event | category | flops | bytes accessed | tf_op | source)
XLA Modules:
  0.0 201.2 jit_solution(9501067320920039118)
XLA Ops:
  6.5 1.1 fusion.39
  7.7 0.9 fusion.14
  8.6 1.5 collective-permute-start
  12.3 1.2 copy.32
  13.5 8.0 %all-to-all-start = ((bf16[16,32,736]{2,1,0:T(8,128)(2,1)}), bf16[16,32,736]{2,1,0:T(8,128)(2,1)S(1)}, u32[]{:S(2)}, u32[]{:S(2)}) async-start(bf16[16,32,736]{2,1,0:T(8,128)(2,1)} %bitcast.17), calls=%async_computation | async-start | bytes 1572864 | tf_op jit(solution)/shard_map/all_to_all | solution.py:181
  23.0 1.3 collective-permute-start.1
  24.2 2.5 %collective-permute-start.2 = (bf16[2,56,28]{1,2,0:T(8,128)(2,1)S(1)}, bf16[2,56,28]{1,2,0:T(8,128)(2,1)S(1)}, u32[]{:S(2)}, u32[]{:S(2)}) collective-permute-start(bf16[2,56,28]{1,2,0:T(8,128)(2,1)S(1)} %get-tuple-element.20), channel_id=1, source_target_pairs={{0,64},{32,96},{64,0},{96,32},{1,65},{33,97},{65,1},{97,33},{2,66}... | collective-permute-start | bytes 18824 | tf_op jit(solution)/shard_map/ppermute | solution.py:141
  26.7 1.2 collective-permute-start.3
  28.6 1.1 collective-permute-done.3
  30.6 7.8 %all-to-all-done = bf16[16,32,736]{2,1,0:T(8,128)(2,1)S(1)} async-done(((bf16[16,32,736]{2,1,0:T(8,128)(2,1)}), bf16[16,32,736]{2,1,0:T(8,128)(2,1)S(1)}, u32[]{:S(2)}, u32[]{:S(2)}) %all-to-all-start) | async-done | bytes 753696 | tf_op jit(solution)/shard_map/all_to_all | solution.py:181
  38.4 1.3 multiply_reduce_fusion
  40.4 4.0 %collective-permute-start.5 = (f32[64,28]{0,1:T(8,128)S(1)}, f32[64,28]{0,1:T(8,128)S(1)}, u32[]{:S(2)}, u32[]{:S(2)}) collective-permute-start(f32[64,28]{0,1:T(8,128)S(1)} %concatenate.49), channel_id=1, source_target_pairs={{0,2},{1,3},{2,0},{3,1},{4,6},{5,7},{6,4},{7,5},{8,10},{9,11},{10,... | collective-permute-start | bytes 21512 | tf_op jit(solution)/shard_map/ppermute | solution.py:141
  44.4 1.9 collective-permute-start.6
  47.4 2.4 %collective-permute-start.8 = (f32[4,64,28]{1,2,0:T(8,128)S(1)}, f32[4,64,28]{1,2,0:T(8,128)S(1)}, u32[]{:S(2)}, u32[]{:S(2)}) collective-permute-start(f32[4,64,28]{1,2,0:T(8,128)S(1)} %get-tuple-element.18), channel_id=1, source_target_pairs={{0,8},{4,12},{8,0},{12,4},{1,9},{5,13},{9,1},{13,5},{2,10},{6,14},... | collective-permute-start | bytes 86024 | tf_op jit(solution)/shard_map/ppermute | solution.py:141
  49.8 1.6 collective-permute-start.9
  51.4 0.9 collective-permute-done.7
  52.4 1.4 collective-permute-done.9
  53.8 0.7 pad_maximum_fusion
  54.5 1.6 slice_reduce_fusion
  56.9 7.5 %collective-permute-start.10 = (f32[8,128]{1,0:T(8,128)S(1)}, f32[8,128]{1,0:T(8,128)S(1)}, u32[]{:S(2)}, u32[]{:S(2)}) collective-permute-start(f32[8,128]{1,0:T(8,128)S(1)} %broadcast_in_dim.24), channel_id=1, source_target_pairs={{0,16},{16,0},{1,17},{17,1},{2,18},{18,2},{3,19},{19,3},{4,20},{20... | collective-permute-start | bytes 12296 | tf_op jit(solution)/shard_map/ppermute | solution.py:141
  64.5 0.7 collective-permute-done.10
  65.9 1.3 collective-permute-start.11
  67.2 1.5 collective-permute-start.17
  68.8 1.2 collective-permute-start.14
  70.0 1.5 collective-permute-start.16
  71.5 1.2 collective-permute-start.12
  72.7 10.3 %collective-permute-done.12 = f32[8,128]{1,0:T(8,128)S(1)} collective-permute-done((f32[8,128]{1,0:T(8,128)S(1)}, f32[8,128]{1,0:T(8,128)S(1)}, u32[]{:S(2)}, u32[]{:S(2)}) %collective-permute-start.12) | collective-permute-done | bytes 4128 | tf_op jit(solution)/shard_map/ppermute | solution.py:141
  83.6 2.3 %collective-permute-done.13 = f32[8,128]{1,0:T(8,128)S(1)} collective-permute-done((f32[8,128]{1,0:T(8,128)S(1)}, f32[8,128]{1,0:T(8,128)S(1)}, u32[]{:S(2)}, u32[]{:S(2)}) %collective-permute-start.13) | collective-permute-done | bytes 4128 | tf_op jit(solution)/shard_map/ppermute | solution.py:141
  85.9 2.9 %collective-permute-start.18 = (bf16[368,384]{1,0:T(8,128)(2,1)S(1)}, bf16[368,384]{1,0:T(8,128)(2,1)S(1)}, u32[]{:S(2)}, u32[]{:S(2)}) collective-permute-start(bf16[368,384]{1,0:T(8,128)(2,1)S(1)} %get-tuple-element.14.refs_0_.refs_6_), channel_id=1, source_target_pairs={{0,16},{16,0},{1,17},{17,1},{2,18},{18,2},{3,19},{19,3},{4,20},{20... | collective-permute-start | bytes 847880 | tf_op jit(solution)/shard_map/ppermute | solution.py:141
  89.6 2.7 %collective-permute-start.25 = (bf16[368,384]{1,0:T(8,128)(2,1)S(1)}, bf16[368,384]{1,0:T(8,128)(2,1)}, u32[]{:S(2)}, u32[]{:S(2)}) collective-permute-start(bf16[368,384]{1,0:T(8,128)(2,1)S(1)} %collective-permute-done.17.refs_5_), channel_id=1, source_target_pairs={{0,96},{32,0},{64,32},{96,64},{1,97},{33,1},{65,33},{97,65},{2,98}... | collective-permute-start | bytes 847880 | tf_op jit(solution)/shard_map/ppermute | solution.py:141
  93.0 1.0 fusion.19
  95.2 0.7 copy-done.3
  96.1 2.0 collective-permute-done.24.refs_12_
  98.1 1.3 collective-permute-start.22
  99.9 2.1 %fusion.8.wide_ref = bf16[8,64,768]{2,1,0:T(8,128)(2,1)S(1)} fusion(s32[8,768]{1,0:T(8,128)S(1)} %copy-done.25, s32[448]{0:T(512)S(1)} %eq.345, bf16[56,448]{1,0:T(8,128)(2,1)S(1)} %copy.33), kind=kOutput, calls=%fused_computation.13 | convolution fusion | flops 355467264 | bytes 862976 | tf_op jit(solution)/shard_map/ia,ran->rin/dot_general | solution.py:222
  104.7 0.7 copy-done.9
  105.4 0.7 copy-done.5
  107.5 1.0 copy-done.2
  108.5 1.0 copy-done.4
  109.4 1.0 copy-done.6
  110.4 1.0 copy-done.8
  111.4 1.0 copy-done.10
  112.3 1.0 copy-done.12
  113.3 1.0 copy-done.14
  114.2 13.0 %shard_map.217 = (bf16[368,384]{1,0:T(8,128)(2,1)}, bf16[368,384]{1,0:T(8,128)(2,1)}) custom-call(s32[8]{0:T(128)S(1)} %concatenate.50.index_ref, f32[1,1]{1,0:T(1,128)S(6)} %rsqrt.3.scale_ref, bf16[16,736,384]{2,1,0:T(8,128)(2,1)} %bitcast.74, bf16[736,64]{1,0:T(8,128)(2,1)S(1)} %get-tuple-element.21.tall_ref, bf16[8,64,768]{2,1,0:T(8,128)(2,1)S(1)} %fusion.8.wide_ref, ...), custom_call_target="tpu_custom_call" | custom-call | flops 3472883712 | bytes 13565952 | tf_op jit(solution)/shard_map/pallas_call | solution.py:93
  127.2 1.1 collective-permute-start.34
  128.5 2.0 collective-permute-start.35
  130.5 1.4 collective-permute-start.30
  131.9 1.4 collective-permute-start.36
  133.3 3.8 %collective-permute-done.28.refs_2_ = bf16[368,384]{1,0:T(8,128)(2,1)} collective-permute-done((bf16[368,384]{1,0:T(8,128)(2,1)}, bf16[368,384]{1,0:T(8,128)(2,1)}, u32[]{:S(2)}, u32[]{:S(2)}) %collective-permute-start.28) | collective-permute-done | bytes 282656 | tf_op jit(solution)/shard_map/ppermute | solution.py:141
  137.1 1.7 collective-permute-start.37
  138.8 4.4 %collective-permute-done.34.refs_3_ = bf16[368,384]{1,0:T(8,128)(2,1)} collective-permute-done((bf16[368,384]{1,0:T(8,128)(2,1)}, bf16[368,384]{1,0:T(8,128)(2,1)}, u32[]{:S(2)}, u32[]{:S(2)}) %collective-permute-start.34) | collective-permute-done | bytes 282656 | tf_op jit(solution)/shard_map/ppermute | solution.py:141
  143.1 1.0 collective-permute-start.38
  144.5 2.7 %collective-permute-start.31 = (bf16[368,384]{1,0:T(8,128)(2,1)}, bf16[368,384]{1,0:T(8,128)(2,1)}, u32[]{:S(2)}, u32[]{:S(2)}) collective-permute-start(bf16[368,384]{1,0:T(8,128)(2,1)} %collective-permute-done.30.refs_5_), channel_id=1, source_target_pairs={{0,96},{32,0},{64,32},{96,64},{1,97},{33,1},{65,33},{97,65},{2,98}... | collective-permute-start | bytes 847880 | tf_op jit(solution)/shard_map/ppermute | solution.py:141
  148.9 5.5 %collective-permute-done.29.refs_0_ = bf16[368,384]{1,0:T(8,128)(2,1)} collective-permute-done((bf16[368,384]{1,0:T(8,128)(2,1)}, bf16[368,384]{1,0:T(8,128)(2,1)}, u32[]{:S(2)}, u32[]{:S(2)}) %collective-permute-start.29) | collective-permute-done | bytes 282656 | tf_op jit(solution)/shard_map/ppermute | solution.py:141
  154.4 0.8 collective-permute-start.32
  155.4 3.6 %copy-done = bf16[11776,384]{1,0:T(8,128)(2,1)S(1)} copy-done((bf16[11776,384]{1,0:T(8,128)(2,1)S(1)}, bf16[11776,384]{1,0:T(8,128)(2,1)}, u32[]{:S(2)}) %copy-start) | copy-done | bytes 9043992
  158.9 10.0 %shard_map.218.refs_4_ = f32[736,384]{1,0:T(8,128)S(1)} custom-call(s32[6]{0:T(128)S(1)} %stack.215.index_ref, f32[1,1]{1,0:T(1,128)S(6)} %rsqrt.3.scale_ref, bf16[16,736,384]{2,1,0:T(8,128)(2,1)S(1)} %bitcast.76, bf16[736,64]{1,0:T(8,128)(2,1)S(1)} %get-tuple-element.21.tall_ref, bf16[8,64,768]{2,1,0:T(8,128)(2,1)S(1)} %fusion.8.wide_ref, ...), custom_call_target="tpu_custom_call" | custom-call | flops 2604662784 | bytes 10174464 | tf_op jit(solution)/shard_map/pallas_call | solution.py:93
  168.9 6.2 %shard_map.219 = bf16[832,384]{1,0:T(8,128)(2,1)} custom-call(s32[2]{0:T(128)S(1)} %pad_add_fusion.index_ref, f32[1,1]{1,0:T(1,128)S(6)} %rsqrt.3.scale_ref, bf16[16,736,384]{2,1,0:T(8,128)(2,1)} %bitcast.75, bf16[736,64]{1,0:T(8,128)(2,1)S(1)} %get-tuple-element.21.tall_ref, bf16[8,64,768]{2,1,0:T(8,128)(2,1)S(1)} %fusion.8.wide_ref, ...), custom_call_target="tpu_custom_call" | custom-call | flops 868220928 | bytes 3391488 | tf_op jit(solution)/shard_map/pallas_call | solution.py:93
  175.1 4.3 %all-to-all-start.1 = ((bf16[8,104,384]{2,1,0:T(8,128)(2,1)}), bf16[8,104,384]{2,1,0:T(8,128)(2,1)S(1)}, u32[]{:S(2)}, u32[]{:S(2)}) async-start(bf16[8,104,384]{2,1,0:T(8,128)(2,1)} %bitcast.55), calls=%async_computation.1 | async-start | bytes 1277952 | tf_op jit(solution)/shard_map/all_to_all | solution.py:250
  179.7 1.4 fusion.4.place_ref
  181.1 9.0 %all-to-all-done.1 = bf16[8,104,384]{2,1,0:T(8,128)(2,1)S(1)} async-done(((bf16[8,104,384]{2,1,0:T(8,128)(2,1)}), bf16[8,104,384]{2,1,0:T(8,128)(2,1)S(1)}, u32[]{:S(2)}, u32[]{:S(2)}) %all-to-all-start.1) | async-done | bytes 639008 | tf_op jit(solution)/shard_map/all_to_all | solution.py:250
  190.1 0.8 copy-done.15
  191.0 3.3 %shard_map.220 = f32[728,364]{1,0:T(8,128)} custom-call(bf16[728,832]{1,0:T(8,128)(2,1)} %fusion.4.place_ref, bf16[832,384]{1,0:T(8,128)(2,1)} %bitcast.77), custom_call_target="tpu_custom_call" | custom-call | tf_op jit(solution)/shard_map/pallas_call | solution.py:255
  (162 shorter events, 18.5 us)
Async XLA Ops:
  6.5 101.0 %all-gather.3.cloned.1.call-start = ((), (), s32[]{:S(2)}) async-start(), calls=%async_computation.2 | async-start | bytes 9609216 | tf_op jit(solution)/shard_map/all_gather | solution.py:173
  7.7 0.9 copy-start.16
  7.7 2.4 %copy-start.18 = (s32[448]{0:T(512)S(1)}, s32[448]{0:T(512)}, u32[]{:S(2)}) copy-start(s32[448]{0:T(512)} %param.24) | copy-start | bytes 5380
  7.7 2.6 %copy-start.23 = (pred[28,28]{1,0:T(8,128)(4,1)S(1)}, pred[28,28]{1,0:T(8,128)(4,1)}, u32[]{:S(2)}) copy-start(pred[28,28]{1,0:T(8,128)(4,1)} %constant.326) | copy-start | bytes 2356
  8.6 14.3 %collective-permute-start = (bf16[56,28]{0,1:T(8,128)(2,1)S(1)}, bf16[56,28]{0,1:T(8,128)(2,1)S(1)}, u32[]{:S(2)}, u32[]{:S(2)}) collective-permute-start(bf16[56,28]{0,1:T(8,128)(2,1)S(1)} %convert_element_type.69), channel_id=1, source_target_pairs={{0,16},{16,0},{1,17},{17,1},{2,18},{18,2},{3,19},{19,3},{4,20},{20... | collective-permute-start | bytes 9416 | tf_op jit(solution)/shard_map/ppermute | solution.py:141
  13.5 8.4 %copy-start.17 = (pred[1,28,28]{2,0,1:T(4,128)(4,1)S(1)}, pred[1,28,28]{2,0,1:T(4,128)(4,1)}, u32[]{:S(2)}) copy-start(pred[1,28,28]{2,0,1:T(4,128)(4,1)} %constant.297.clone) | copy-start | bytes 2356
  13.5 9.2 %copy-start.22 = (s32[736]{0:T(1024)S(1)}, s32[736]{0:T(1024)}, u32[]{:S(2)}) copy-start(s32[736]{0:T(1024)} %constant.302.clone) | copy-start | bytes 8836
  13.5 16.6 %copy-start.24 = (s32[384]{0:T(512)S(1)}, s32[384]{0:T(512)}, u32[]{:S(2)}) copy-start(s32[384]{0:T(512)} %constant.304.clone) | copy-start | bytes 4612
  13.5 24.9 %all-to-all-start = ((bf16[16,32,736]{2,1,0:T(8,128)(2,1)}), bf16[16,32,736]{2,1,0:T(8,128)(2,1)S(1)}, u32[]{:S(2)}, u32[]{:S(2)}) async-start(bf16[16,32,736]{2,1,0:T(8,128)(2,1)} %bitcast.17), calls=%async_computation | async-start | bytes 1572864 | tf_op jit(solution)/shard_map/all_to_all | solution.py:181
  23.0 5.6 %collective-permute-start.1 = (bf16[2,56,28]{1,2,0:T(8,128)(2,1)S(1)}, bf16[2,56,28]{1,2,0:T(8,128)(2,1)S(1)}, u32[]{:S(2)}, u32[]{:S(2)}) collective-permute-start(bf16[2,56,28]{1,2,0:T(8,128)(2,1)S(1)} %get-tuple-element.20), channel_id=1, source_target_pairs={{0,32},{32,64},{64,96},{96,0},{1,33},{33,65},{65,97},{97,1},{2,34}... | collective-permute-start | bytes 18824 | tf_op jit(solution)/shard_map/ppermute | solution.py:141
  24.2 4.4 %collective-permute-start.2 = (bf16[2,56,28]{1,2,0:T(8,128)(2,1)S(1)}, bf16[2,56,28]{1,2,0:T(8,128)(2,1)S(1)}, u32[]{:S(2)}, u32[]{:S(2)}) collective-permute-start(bf16[2,56,28]{1,2,0:T(8,128)(2,1)S(1)} %get-tuple-element.20), channel_id=1, source_target_pairs={{0,64},{32,96},{64,0},{96,32},{1,65},{33,97},{65,1},{97,33},{2,66}... | collective-permute-start | bytes 18824 | tf_op jit(solution)/shard_map/ppermute | solution.py:141
  26.7 3.0 %collective-permute-start.3 = (bf16[2,56,28]{1,2,0:T(8,128)(2,1)S(1)}, bf16[2,56,28]{1,2,0:T(8,128)(2,1)S(1)}, u32[]{:S(2)}, u32[]{:S(2)}) collective-permute-start(bf16[2,56,28]{1,2,0:T(8,128)(2,1)S(1)} %get-tuple-element.20), channel_id=1, source_target_pairs={{0,96},{32,0},{64,32},{96,64},{1,97},{33,1},{65,33},{97,65},{2,98}... | collective-permute-start | bytes 18824 | tf_op jit(solution)/shard_map/ppermute | solution.py:141
  39.7 43.6 %copy-start.20 = (pred[56,56]{1,0:T(8,128)(4,1)S(1)}, pred[56,56]{1,0:T(8,128)(4,1)}, u32[]{:S(2)}) copy-start(pred[56,56]{1,0:T(8,128)(4,1)} %constant.334) | copy-start | bytes 9412
  40.4 6.7 %collective-permute-start.4 = (f32[64,28]{0,1:T(8,128)S(1)}, f32[64,28]{0,1:T(8,128)S(1)}, u32[]{:S(2)}, u32[]{:S(2)}) collective-permute-start(f32[64,28]{0,1:T(8,128)S(1)} %concatenate.49), channel_id=1, source_target_pairs={{0,1},{1,2},{2,3},{3,0},{4,5},{5,6},{6,7},{7,4},{8,9},{9,10},{10,1... | collective-permute-start | bytes 21512 | tf_op jit(solution)/shard_map/ppermute | solution.py:141
  40.4 6.6 %collective-permute-start.5 = (f32[64,28]{0,1:T(8,128)S(1)}, f32[64,28]{0,1:T(8,128)S(1)}, u32[]{:S(2)}, u32[]{:S(2)}) collective-permute-start(f32[64,28]{0,1:T(8,128)S(1)} %concatenate.49), channel_id=1, source_target_pairs={{0,2},{1,3},{2,0},{3,1},{4,6},{5,7},{6,4},{7,5},{8,10},{9,11},{10,... | collective-permute-start | bytes 21512 | tf_op jit(solution)/shard_map/ppermute | solution.py:141
  44.4 2.8 %collective-permute-start.6 = (f32[64,28]{0,1:T(8,128)S(1)}, f32[64,28]{0,1:T(8,128)S(1)}, u32[]{:S(2)}, u32[]{:S(2)}) collective-permute-start(f32[64,28]{0,1:T(8,128)S(1)} %concatenate.49), channel_id=1, source_target_pairs={{0,3},{1,0},{2,1},{3,2},{4,7},{5,4},{6,5},{7,6},{8,11},{9,8},{10,9... | collective-permute-start | bytes 21512 | tf_op jit(solution)/shard_map/ppermute | solution.py:141
  47.3 5.1 %collective-permute-start.7 = (f32[4,64,28]{1,2,0:T(8,128)S(1)}, f32[4,64,28]{1,2,0:T(8,128)S(1)}, u32[]{:S(2)}, u32[]{:S(2)}) collective-permute-start(f32[4,64,28]{1,2,0:T(8,128)S(1)} %get-tuple-element.18), channel_id=1, source_target_pairs={{0,4},{4,8},{8,12},{12,0},{1,5},{5,9},{9,13},{13,1},{2,6},{6,10},{... | collective-permute-start | bytes 86024 | tf_op jit(solution)/shard_map/ppermute | solution.py:141
  47.4 5.0 %collective-permute-start.8 = (f32[4,64,28]{1,2,0:T(8,128)S(1)}, f32[4,64,28]{1,2,0:T(8,128)S(1)}, u32[]{:S(2)}, u32[]{:S(2)}) collective-permute-start(f32[4,64,28]{1,2,0:T(8,128)S(1)} %get-tuple-element.18), channel_id=1, source_target_pairs={{0,8},{4,12},{8,0},{12,4},{1,9},{5,13},{9,1},{13,5},{2,10},{6,14},... | collective-permute-start | bytes 86024 | tf_op jit(solution)/shard_map/ppermute | solution.py:141
  49.8 4.0 %collective-permute-start.9 = (f32[4,64,28]{1,2,0:T(8,128)S(1)}, f32[4,64,28]{1,2,0:T(8,128)S(1)}, u32[]{:S(2)}, u32[]{:S(2)}) collective-permute-start(f32[4,64,28]{1,2,0:T(8,128)S(1)} %get-tuple-element.18), channel_id=1, source_target_pairs={{0,12},{4,0},{8,4},{12,8},{1,13},{5,1},{9,5},{13,9},{2,14},{6,2},{... | collective-permute-start | bytes 86024 | tf_op jit(solution)/shard_map/ppermute | solution.py:141
  54.5 45.3 %copy-start.25 = (s32[8,768]{1,0:T(8,128)S(1)}, s32[8,768]{1,0:T(8,128)}, u32[]{:S(2)}) copy-start(s32[8,768]{1,0:T(8,128)} %constant.333) | copy-start | bytes 73732
  56.9 8.3 %collective-permute-start.10 = (f32[8,128]{1,0:T(8,128)S(1)}, f32[8,128]{1,0:T(8,128)S(1)}, u32[]{:S(2)}, u32[]{:S(2)}) collective-permute-start(f32[8,128]{1,0:T(8,128)S(1)} %broadcast_in_dim.24), channel_id=1, source_target_pairs={{0,16},{16,0},{1,17},{17,1},{2,18},{18,2},{3,19},{19,3},{4,20},{20... | collective-permute-start | bytes 12296 | tf_op jit(solution)/shard_map/ppermute | solution.py:141
  65.9 5.6 %collective-permute-start.11 = (f32[8,128]{1,0:T(8,128)S(1)}, f32[8,128]{1,0:T(8,128)S(1)}, u32[]{:S(2)}, u32[]{:S(2)}) collective-permute-start(f32[8,128]{1,0:T(8,128)S(1)} %broadcast_add_fusion.1), channel_id=1, source_target_pairs={{0,32},{32,64},{64,96},{96,0},{1,33},{33,65},{65,97},{97,1},{2,34}... | collective-permute-start | bytes 12296 | tf_op jit(solution)/shard_map/ppermute | solution.py:141
  67.2 21.5 %collective-permute-start.17 = (bf16[368,384]{1,0:T(8,128)(2,1)S(1)}, bf16[368,384]{1,0:T(8,128)(2,1)S(1)}, u32[]{:S(2)}, u32[]{:S(2)}) collective-permute-start(bf16[368,384]{1,0:T(8,128)(2,1)S(1)} %get-tuple-element.13.refs_1_.refs_7_), channel_id=1, source_target_pairs={{0,96},{32,0},{64,32},{96,64},{1,97},{33,1},{65,33},{97,65},{2,98}... | collective-permute-start | bytes 847880 | tf_op jit(solution)/shard_map/ppermute | solution.py:141
  68.8 20.1 %collective-permute-start.15 = (bf16[368,384]{1,0:T(8,128)(2,1)S(1)}, bf16[368,384]{1,0:T(8,128)(2,1)S(1)}, u32[]{:S(2)}, u32[]{:S(2)}) collective-permute-start(bf16[368,384]{1,0:T(8,128)(2,1)S(1)} %get-tuple-element.13.refs_1_.refs_7_), channel_id=1, source_target_pairs={{0,32},{32,64},{64,96},{96,0},{1,33},{33,65},{65,97},{97,1},{2,34}... | collective-permute-start | bytes 847880 | tf_op jit(solution)/shard_map/ppermute | solution.py:141
  68.8 20.0 %collective-permute-start.14 = (bf16[368,384]{1,0:T(8,128)(2,1)S(1)}, bf16[368,384]{1,0:T(8,128)(2,1)S(1)}, u32[]{:S(2)}, u32[]{:S(2)}) collective-permute-start(bf16[368,384]{1,0:T(8,128)(2,1)S(1)} %get-tuple-element.14.refs_0_.refs_6_), channel_id=1, source_target_pairs={{0,32},{32,64},{64,96},{96,0},{1,33},{33,65},{65,97},{97,1},{2,34}... | collective-permute-start | bytes 847880 | tf_op jit(solution)/shard_map/ppermute | solution.py:141
  70.0 19.6 %collective-permute-start.16 = (bf16[368,384]{1,0:T(8,128)(2,1)S(1)}, bf16[368,384]{1,0:T(8,128)(2,1)S(1)}, u32[]{:S(2)}, u32[]{:S(2)}) collective-permute-start(bf16[368,384]{1,0:T(8,128)(2,1)S(1)} %get-tuple-element.14.refs_0_.refs_6_), channel_id=1, source_target_pairs={{0,96},{32,0},{64,32},{96,64},{1,97},{33,1},{65,33},{97,65},{2,98}... | collective-permute-start | bytes 847880 | tf_op jit(solution)/shard_map/ppermute | solution.py:141
  71.5 11.5 %collective-permute-start.12 = (f32[8,128]{1,0:T(8,128)S(1)}, f32[8,128]{1,0:T(8,128)S(1)}, u32[]{:S(2)}, u32[]{:S(2)}) collective-permute-start(f32[8,128]{1,0:T(8,128)S(1)} %broadcast_add_fusion.1), channel_id=1, source_target_pairs={{0,64},{32,96},{64,0},{96,32},{1,65},{33,97},{65,1},{97,33},{2,66}... | collective-permute-start | bytes 12296 | tf_op jit(solution)/shard_map/ppermute | solution.py:141
  83.0 2.9 %collective-permute-start.13 = (f32[8,128]{1,0:T(8,128)S(1)}, f32[8,128]{1,0:T(8,128)S(1)}, u32[]{:S(2)}, u32[]{:S(2)}) collective-permute-start(f32[8,128]{1,0:T(8,128)S(1)} %broadcast_add_fusion.1), channel_id=1, source_target_pairs={{0,96},{32,0},{64,32},{96,64},{1,97},{33,1},{65,33},{97,65},{2,98}... | collective-permute-start | bytes 12296 | tf_op jit(solution)/shard_map/ppermute | solution.py:141
  85.9 8.3 %collective-permute-start.18 = (bf16[368,384]{1,0:T(8,128)(2,1)S(1)}, bf16[368,384]{1,0:T(8,128)(2,1)S(1)}, u32[]{:S(2)}, u32[]{:S(2)}) collective-permute-start(bf16[368,384]{1,0:T(8,128)(2,1)S(1)} %get-tuple-element.14.refs_0_.refs_6_), channel_id=1, source_target_pairs={{0,16},{16,0},{1,17},{17,1},{2,18},{18,2},{3,19},{19,3},{4,20},{20... | collective-permute-start | bytes 847880 | tf_op jit(solution)/shard_map/ppermute | solution.py:141
  88.8 6.4 %collective-permute-start.19 = (bf16[368,384]{1,0:T(8,128)(2,1)S(1)}, bf16[368,384]{1,0:T(8,128)(2,1)S(1)}, u32[]{:S(2)}, u32[]{:S(2)}) collective-permute-start(bf16[368,384]{1,0:T(8,128)(2,1)S(1)} %get-tuple-element.13.refs_1_.refs_7_), channel_id=1, source_target_pairs={{0,16},{16,0},{1,17},{17,1},{2,18},{18,2},{3,19},{19,3},{4,20},{20... | collective-permute-start | bytes 847880 | tf_op jit(solution)/shard_map/ppermute | solution.py:141
  88.8 9.3 %collective-permute-start.24 = (bf16[368,384]{1,0:T(8,128)(2,1)S(1)}, bf16[368,384]{1,0:T(8,128)(2,1)}, u32[]{:S(2)}, u32[]{:S(2)}) collective-permute-start(bf16[368,384]{1,0:T(8,128)(2,1)S(1)} %collective-permute-done.14.refs_2_), channel_id=1, source_target_pairs={{0,32},{32,64},{64,96},{96,0},{1,33},{33,65},{65,97},{97,1},{2,34}... | collective-permute-start | bytes 847880 | tf_op jit(solution)/shard_map/ppermute | solution.py:141
  88.9 10.5 %collective-permute-start.20 = (bf16[368,384]{1,0:T(8,128)(2,1)S(1)}, bf16[368,384]{1,0:T(8,128)(2,1)}, u32[]{:S(2)}, u32[]{:S(2)}) collective-permute-start(bf16[368,384]{1,0:T(8,128)(2,1)S(1)} %collective-permute-done.14.refs_2_), channel_id=1, source_target_pairs={{0,16},{16,0},{1,17},{17,1},{2,18},{18,2},{3,19},{19,3},{4,20},{20... | collective-permute-start | bytes 847880 | tf_op jit(solution)/shard_map/ppermute | solution.py:141
  89.6 9.8 %collective-permute-start.25 = (bf16[368,384]{1,0:T(8,128)(2,1)S(1)}, bf16[368,384]{1,0:T(8,128)(2,1)}, u32[]{:S(2)}, u32[]{:S(2)}) collective-permute-start(bf16[368,384]{1,0:T(8,128)(2,1)S(1)} %collective-permute-done.17.refs_5_), channel_id=1, source_target_pairs={{0,96},{32,0},{64,32},{96,64},{1,97},{33,1},{65,33},{97,65},{2,98}... | collective-permute-start | bytes 847880 | tf_op jit(solution)/shard_map/ppermute | solution.py:141
  94.9 10.5 %collective-permute-start.23 = (bf16[368,384]{1,0:T(8,128)(2,1)S(1)}, bf16[368,384]{1,0:T(8,128)(2,1)S(1)}, u32[]{:S(2)}, u32[]{:S(2)}) collective-permute-start(bf16[368,384]{1,0:T(8,128)(2,1)S(1)} %collective-permute-done.17.refs_5_), channel_id=1, source_target_pairs={{0,16},{16,0},{1,17},{17,1},{2,18},{18,2},{3,19},{19,3},{4,20},{20... | collective-permute-start | bytes 847880 | tf_op jit(solution)/shard_map/ppermute | solution.py:141
  95.9 8.0 %collective-permute-start.21 = (bf16[368,384]{1,0:T(8,128)(2,1)S(1)}, bf16[368,384]{1,0:T(8,128)(2,1)S(1)}, u32[]{:S(2)}, u32[]{:S(2)}) collective-permute-start(bf16[368,384]{1,0:T(8,128)(2,1)S(1)} %collective-permute-done.15.refs_3_), channel_id=1, source_target_pairs={{0,16},{16,0},{1,17},{17,1},{2,18},{18,2},{3,19},{19,3},{4,20},{20... | collective-permute-start | bytes 847880 | tf_op jit(solution)/shard_map/ppermute | solution.py:141
  98.1 6.6 %collective-permute-start.22 = (bf16[368,384]{1,0:T(8,128)(2,1)S(1)}, bf16[368,384]{1,0:T(8,128)(2,1)S(1)}, u32[]{:S(2)}, u32[]{:S(2)}) collective-permute-start(bf16[368,384]{1,0:T(8,128)(2,1)S(1)} %collective-permute-done.16.refs_4_), channel_id=1, source_target_pairs={{0,16},{16,0},{1,17},{17,1},{2,18},{18,2},{3,19},{19,3},{4,20},{20... | collective-permute-start | bytes 847880 | tf_op jit(solution)/shard_map/ppermute | solution.py:141
  99.3 6.8 %collective-permute-start.26 = (bf16[368,384]{1,0:T(8,128)(2,1)}, bf16[368,384]{1,0:T(8,128)(2,1)S(1)}, u32[]{:S(2)}, u32[]{:S(2)}) collective-permute-start(bf16[368,384]{1,0:T(8,128)(2,1)} %collective-permute-done.24.refs_12_), channel_id=1, source_target_pairs={{0,16},{16,0},{1,17},{17,1},{2,18},{18,2},{3,19},{19,3},{4,20},{20... | collective-permute-start | bytes 847880 | tf_op jit(solution)/shard_map/ppermute | solution.py:141
  99.4 7.5 %collective-permute-start.27 = (bf16[368,384]{1,0:T(8,128)(2,1)}, bf16[368,384]{1,0:T(8,128)(2,1)S(1)}, u32[]{:S(2)}, u32[]{:S(2)}) collective-permute-start(bf16[368,384]{1,0:T(8,128)(2,1)} %collective-permute-done.25.refs_13_), channel_id=1, source_target_pairs={{0,16},{16,0},{1,17},{17,1},{2,18},{18,2},{3,19},{19,3},{4,20},{20... | collective-permute-start | bytes 847880 | tf_op jit(solution)/shard_map/ppermute | solution.py:141
  107.5 1.0 copy-start.2
  108.5 1.0 copy-start.4
  109.4 1.0 copy-start.6
  110.4 1.0 copy-start.8
  111.4 1.0 copy-start.10
  112.3 1.0 copy-start.12
  113.3 1.0 copy-start.14
  114.2 32.9 %copy-start.21 = (s32[736]{0:T(1024)S(1)}, s32[736]{0:T(1024)}, u32[]{:S(2)}) copy-start(s32[736]{0:T(1024)} %constant.309.clone) | copy-start | bytes 8836
  127.2 21.5 %copy-start.19 = (pred[1,56,56]{2,1,0:T(8,128)(4,1)S(1)}, pred[1,56,56]{2,1,0:T(8,128)(4,1)}, u32[]{:S(2)}) copy-start(pred[1,56,56]{2,1,0:T(8,128)(4,1)} %constant.307.clone) | copy-start | bytes 9412
  127.2 9.9 %collective-permute-start.28 = (bf16[368,384]{1,0:T(8,128)(2,1)}, bf16[368,384]{1,0:T(8,128)(2,1)}, u32[]{:S(2)}, u32[]{:S(2)}) collective-permute-start(bf16[368,384]{1,0:T(8,128)(2,1)} %get-tuple-element.7.refs_0_), channel_id=1, source_target_pairs={{0,32},{32,64},{64,96},{96,0},{1,33},{33,65},{65,97},{97,1},{2,34}... | collective-permute-start | bytes 847880 | tf_op jit(solution)/shard_map/ppermute | solution.py:141
  127.2 15.9 %collective-permute-start.34 = (bf16[368,384]{1,0:T(8,128)(2,1)}, bf16[368,384]{1,0:T(8,128)(2,1)}, u32[]{:S(2)}, u32[]{:S(2)}) collective-permute-start(bf16[368,384]{1,0:T(8,128)(2,1)} %get-tuple-element.8.refs_1_), channel_id=1, source_target_pairs={{0,32},{32,64},{64,96},{96,0},{1,33},{33,65},{65,97},{97,1},{2,34}... | collective-permute-start | bytes 847880 | tf_op jit(solution)/shard_map/ppermute | solution.py:141
  128.5 15.9 %collective-permute-start.35 = (bf16[368,384]{1,0:T(8,128)(2,1)}, bf16[368,384]{1,0:T(8,128)(2,1)}, u32[]{:S(2)}, u32[]{:S(2)}) collective-permute-start(bf16[368,384]{1,0:T(8,128)(2,1)} %get-tuple-element.7.refs_0_), channel_id=1, source_target_pairs={{0,96},{32,0},{64,32},{96,64},{1,97},{33,1},{65,33},{97,65},{2,98}... | collective-permute-start | bytes 847880 | tf_op jit(solution)/shard_map/ppermute | solution.py:141
  130.5 14.0 %collective-permute-start.30 = (bf16[368,384]{1,0:T(8,128)(2,1)}, bf16[368,384]{1,0:T(8,128)(2,1)}, u32[]{:S(2)}, u32[]{:S(2)}) collective-permute-start(bf16[368,384]{1,0:T(8,128)(2,1)} %get-tuple-element.8.refs_1_), channel_id=1, source_target_pairs={{0,96},{32,0},{64,32},{96,64},{1,97},{33,1},{65,33},{97,65},{2,98}... | collective-permute-start | bytes 847880 | tf_op jit(solution)/shard_map/ppermute | solution.py:141
  131.9 15.5 %collective-permute-start.36 = (bf16[368,384]{1,0:T(8,128)(2,1)}, bf16[368,384]{1,0:T(8,128)(2,1)}, u32[]{:S(2)}, u32[]{:S(2)}) collective-permute-start(bf16[368,384]{1,0:T(8,128)(2,1)} %get-tuple-element.7.refs_0_), channel_id=1, source_target_pairs={{0,16},{16,0},{1,17},{17,1},{2,18},{18,2},{3,19},{19,3},{4,20},{20... | collective-permute-start | bytes 847880 | tf_op jit(solution)/shard_map/ppermute | solution.py:141
  137.1 11.0 %collective-permute-start.37 = (bf16[368,384]{1,0:T(8,128)(2,1)}, bf16[368,384]{1,0:T(8,128)(2,1)}, u32[]{:S(2)}, u32[]{:S(2)}) collective-permute-start(bf16[368,384]{1,0:T(8,128)(2,1)} %get-tuple-element.8.refs_1_), channel_id=1, source_target_pairs={{0,16},{16,0},{1,17},{17,1},{2,18},{18,2},{3,19},{19,3},{4,20},{20... | collective-permute-start | bytes 847880 | tf_op jit(solution)/shard_map/ppermute | solution.py:141
  143.1 5.1 %collective-permute-start.38 = (bf16[368,384]{1,0:T(8,128)(2,1)}, bf16[368,384]{1,0:T(8,128)(2,1)}, u32[]{:S(2)}, u32[]{:S(2)}) collective-permute-start(bf16[368,384]{1,0:T(8,128)(2,1)} %collective-permute-done.28.refs_2_), channel_id=1, source_target_pairs={{0,16},{16,0},{1,17},{17,1},{2,18},{18,2},{3,19},{19,3},{4,20},{20... | collective-permute-start | bytes 847880 | tf_op jit(solution)/shard_map/ppermute | solution.py:141
  144.4 10.0 %collective-permute-start.29 = (bf16[368,384]{1,0:T(8,128)(2,1)}, bf16[368,384]{1,0:T(8,128)(2,1)}, u32[]{:S(2)}, u32[]{:S(2)}) collective-permute-start(bf16[368,384]{1,0:T(8,128)(2,1)} %collective-permute-done.28.refs_2_), channel_id=1, source_target_pairs={{0,32},{32,64},{64,96},{96,0},{1,33},{33,65},{65,97},{97,1},{2,34}... | collective-permute-start | bytes 847880 | tf_op jit(solution)/shard_map/ppermute | solution.py:141
  144.5 10.7 %collective-permute-start.31 = (bf16[368,384]{1,0:T(8,128)(2,1)}, bf16[368,384]{1,0:T(8,128)(2,1)}, u32[]{:S(2)}, u32[]{:S(2)}) collective-permute-start(bf16[368,384]{1,0:T(8,128)(2,1)} %collective-permute-done.30.refs_5_), channel_id=1, source_target_pairs={{0,96},{32,0},{64,32},{96,64},{1,97},{33,1},{65,33},{97,65},{2,98}... | collective-permute-start | bytes 847880 | tf_op jit(solution)/shard_map/ppermute | solution.py:141
  147.5 7.9 %collective-permute-start.41 = (bf16[368,384]{1,0:T(8,128)(2,1)}, bf16[368,384]{1,0:T(8,128)(2,1)}, u32[]{:S(2)}, u32[]{:S(2)}) collective-permute-start(bf16[368,384]{1,0:T(8,128)(2,1)} %collective-permute-done.30.refs_5_), channel_id=1, source_target_pairs={{0,16},{16,0},{1,17},{17,1},{2,18},{18,2},{3,19},{19,3},{4,20},{20... | collective-permute-start | bytes 847880 | tf_op jit(solution)/shard_map/ppermute | solution.py:141
  148.1 7.2 %collective-permute-start.39 = (bf16[368,384]{1,0:T(8,128)(2,1)}, bf16[368,384]{1,0:T(8,128)(2,1)}, u32[]{:S(2)}, u32[]{:S(2)}) collective-permute-start(bf16[368,384]{1,0:T(8,128)(2,1)} %collective-permute-done.34.refs_3_), channel_id=1, source_target_pairs={{0,16},{16,0},{1,17},{17,1},{2,18},{18,2},{3,19},{19,3},{4,20},{20... | collective-permute-start | bytes 847880 | tf_op jit(solution)/shard_map/ppermute | solution.py:141
  148.2 7.1 %collective-permute-start.40 = (bf16[368,384]{1,0:T(8,128)(2,1)}, bf16[368,384]{1,0:T(8,128)(2,1)}, u32[]{:S(2)}, u32[]{:S(2)}) collective-permute-start(bf16[368,384]{1,0:T(8,128)(2,1)} %collective-permute-done.35.refs_4_), channel_id=1, source_target_pairs={{0,16},{16,0},{1,17},{17,1},{2,18},{18,2},{3,19},{19,3},{4,20},{20... | collective-permute-start | bytes 847880 | tf_op jit(solution)/shard_map/ppermute | solution.py:141
  154.4 14.5 %collective-permute-start.32 = (bf16[368,384]{1,0:T(8,128)(2,1)}, bf16[368,384]{1,0:T(8,128)(2,1)}, u32[]{:S(2)}, u32[]{:S(2)}) collective-permute-start(bf16[368,384]{1,0:T(8,128)(2,1)} %collective-permute-done.29.refs_0_), channel_id=1, source_target_pairs={{0,16},{16,0},{1,17},{17,1},{2,18},{18,2},{3,19},{19,3},{4,20},{20... | collective-permute-start | bytes 847880 | tf_op jit(solution)/shard_map/ppermute | solution.py:141
  155.2 13.7 %collective-permute-start.33 = (bf16[368,384]{1,0:T(8,128)(2,1)}, bf16[368,384]{1,0:T(8,128)(2,1)}, u32[]{:S(2)}, u32[]{:S(2)}) collective-permute-start(bf16[368,384]{1,0:T(8,128)(2,1)} %collective-permute-done.31.refs_1_), channel_id=1, source_target_pairs={{0,16},{16,0},{1,17},{17,1},{2,18},{18,2},{3,19},{19,3},{4,20},{20... | collective-permute-start | bytes 847880 | tf_op jit(solution)/shard_map/ppermute | solution.py:141
  155.3 3.6 %copy-start = (bf16[11776,384]{1,0:T(8,128)(2,1)S(1)}, bf16[11776,384]{1,0:T(8,128)(2,1)}, u32[]{:S(2)}) copy-start(bf16[11776,384]{1,0:T(8,128)(2,1)} %all-gather.3.cloned.1.call-done) | copy-start | bytes 27131908
  175.1 15.1 %all-to-all-start.1 = ((bf16[8,104,384]{2,1,0:T(8,128)(2,1)}), bf16[8,104,384]{2,1,0:T(8,128)(2,1)S(1)}, u32[]{:S(2)}, u32[]{:S(2)}) async-start(bf16[8,104,384]{2,1,0:T(8,128)(2,1)} %bitcast.55), calls=%async_computation.1 | async-start | bytes 1277952 | tf_op jit(solution)/shard_map/all_to_all | solution.py:250
  190.1 0.8 copy-start.15
  (7 other events, 5.0 us)
Sparse Core Ops, SparseCore 0:
  9.5 83.6 all-gather.2
where the time goes:
time: 202 us; the launch traced here: 201 us
  starting transfers between devices  65.3 us (32%)
  waiting for transfers between devices  49.4 us (24%)
  Pallas kernels  32.5 us (16%)
  local copies, waits for them, and re-layouts  25.1 us (12%)
  between operations  14.8 us (7%)
  other arithmetic  9.3 us (5%)
  matrix products  4.81 us (2%)
    ppermute x42, starting transfers between devices, send(): return lax.ppermute(array, axis, shift(2 if axis == 'c' else 4, by))  53 us
    ppermute x42, waiting for transfers between devices, send(): return lax.ppermute(array, axis, shift(2 if axis == 'c' else 4, by))  32.6 us
    pallas_call x3, Pallas kernels, multiply(): pl.pallas_call(body, out_shape=out_shape, grid_spec=pltpu.PrefetchScalarG...  29.1 us
    unnamed x52, local copies, waits for them, and re-layouts  16.1 us
    all_to_all x1, waiting for transfers between devices, on_device(): lax.all_to_all(sent_rows.reshape(row_count, slots_row * NBF, WIDE), ROW,...  9.04 us
    all_to_all x1, starting transfers between devices, on_device(): lax.all_to_all(outgoing.reshape(col_count, width, 2 * TALL), COL, 0, 0)  7.98 us
    all_to_all x1, waiting for transfers between devices, on_device(): lax.all_to_all(outgoing.reshape(col_count, width, 2 * TALL), COL, 0, 0)  7.76 us
    all_to_all x1, starting transfers between devices, on_device(): lax.all_to_all(sent_rows.reshape(row_count, slots_row * NBF, WIDE), ROW,...  4.34 us
  transfers between devices with their start and end apart: 45, of which 13 were waited for; matrix products, arithmetic and copies ran while one was open for 10% of the time, Pallas kernels for 5%

commit v1 on v0

--- a/solution.py
+++ b/solution.py
@@ -52,84 +52,116 @@
 WIDE = 384
 
 
-def multiply(panel, tall, wide, scale, index, blocks, scaled, epilogue, extra, out_shape, start=None):
+def multiply(panel, tall, wide, scale, index, blocks, scaled, epilogue, extra, out_shape, micros):
     count = len(blocks)
     rows = panel.shape[1]
+    flat = [(j, piece) for j, pieces in enumerate(blocks) for piece in pieces]
+    starts = [sum(p.shape[0] for _, p in flat[:k]) for k in range(len(flat))]
+    halves = [
+        (k, j, (at - 2 * TALL * j) // TALL, t)
+        for k, ((j, piece), at) in enumerate(zip(flat, starts))
+        for t in range(piece.shape[0] // TALL)
+    ]
 
     def body(index_ref, scale_ref, panel_ref, tall_ref, wide_ref, *refs):
-        block_refs = refs[: 2 * count]
-        out_refs, acc = refs[-1 - len(out_shape) : -1], refs[-1]
-        rest = refs[2 * count : -1 - len(out_shape)]
-        if start is not None:
-            start_ref, rest = rest[0], rest[1:]
+        pieces, refs = refs[: len(flat)], refs[len(flat) :]
+        more, refs = refs[: len(extra)], refs[len(extra) :]
+        outs, refs = refs[: len(out_shape)], refs[len(out_shape) :]
+        acc, held, strips, sem, strip_sem, more_sem = refs[:6]
+        kept_more = refs[6:]
+        by = scale_ref[0, 0]
+
+        def fetch(k, j, first, t):
+            spot = held.at[j, pl.ds((first + t) * WIDE, TALL)]
+            source = pieces[k].at[pl.ds(t * TALL, TALL)]
+            return pltpu.make_async_copy(source, spot, sem.at[j, first + t])
+
+        def fetch_strip(j):
+            source = panel_ref.at[pl.ds(2 * index_ref[j], 2)]
+            return pltpu.make_async_copy(source, strips.at[j], strip_sem.at[j])
+
+        def fetch_more(k):
+            return pltpu.make_async_copy(more[k], kept_more[k], more_sem.at[k])
+
         step = pl.program_id(0)
-        by = scale_ref[0, 0]
 
         @pl.when(step == 0)
         def _():
-            acc[...] = jnp.zeros_like(acc) if start is None else start_ref[...]
-
-        kept = jnp.dot(tall_ref[...], wide_ref[0], preferred_element_type=F32) * by
-        left = jnp.concatenate([panel_ref[0], panel_ref[1]], axis=1)
-        left = (left.astype(F32) * kept).astype(BF)
-        gap = jnp.zeros((WIDE - TALL, WIDE), BF)
+            for j in range(count):
+                for one in halves:
+                    if one[1] == j:
+                        fetch(*one).start()
+                fetch_strip(j).start()
+            for k in range(len(extra)):
+                fetch_more(k).start()
+            acc[...] = jnp.zeros_like(acc)
+            gap = jnp.zeros((WIDE - TALL, WIDE), BF)
+            for j in range(count):
+                for t in range(2):
+                    held[j, t * WIDE + TALL : (t + 1) * WIDE] = gap
+
+        kept = jnp.dot(tall_ref[...], wide_ref[index_ref[step]], preferred_element_type=F32)
         for j in range(count):
 
             @pl.when(step == j)
             def _(j=j):
-                top, bottom = block_refs[2 * j][...], block_refs[2 * j + 1][...]
-                if scaled:
-                    top = (top.astype(F32) * by).astype(BF)
-                    bottom = (bottom.astype(F32) * by).astype(BF)
-                right = jnp.concatenate([top, gap, bottom, gap], axis=0)
-                acc[...] += jnp.dot(left, right, preferred_element_type=F32)
+                fetch_strip(j).wait()
+                for one in halves:
+                    if one[1] == j:
+                        fetch(*one).wait()
+
+        left = jnp.concatenate([strips[step, 0], strips[step, 1]], axis=1)
+        left = (left.astype(F32) * (kept * by)).astype(BF)
+        right = held[step]
+        if scaled:
+            right = (right.astype(F32) * by).astype(BF)
+        acc[...] += jnp.dot(left, right, preferred_element_type=F32)
 
         @pl.when(step == count - 1)
         def _():
-            epilogue(acc, by, out_refs, *rest)
+            for k in range(len(extra)):
+                fetch_more(k).wait()
+            epilogue(acc, by, outs, *kept_more)
 
     whole = pl.BlockSpec(memory_space=pltpu.VMEM)
-    operands = [b for pair in blocks for b in pair] + ([] if start is None else [start]) + extra
+    smem = pl.BlockSpec(memory_space=pltpu.SMEM)
+    anywhere = pl.BlockSpec(memory_space=pltpu.HBM)
+    operands = [piece for _, piece in flat] + extra
     return pl.pallas_call(
         body,
         out_shape=out_shape,
-        grid_spec=pltpu.PrefetchScalarGridSpec(
-            num_scalar_prefetch=1,
-            grid=(count,),
-            in_specs=[
-                pl.BlockSpec(memory_space=pltpu.SMEM),
-                pl.BlockSpec((2, rows, WIDE), lambda g, index: (index[g], 0, 0)),
-                whole,
-                pl.BlockSpec((1,) + wide.shape[1:], lambda g, index: (index[g], 0, 0)),
-            ]
-            + [whole] * len(operands),
-            out_specs=[whole] * len(out_shape),
-            scratch_shapes=[pltpu.VMEM((rows, WIDE), F32)],
-        ),
-        compiler_params=pltpu.CompilerParams(vmem_limit_bytes=40 * 2**20),
+        grid=(count,),
+        in_specs=[smem, smem, anywhere, whole, whole] + [anywhere] * len(operands),
+        out_specs=[whole] * len(out_shape),
+        scratch_shapes=[
+            pltpu.VMEM((rows, WIDE), F32),
+            pltpu.VMEM((count, 2 * WIDE, WIDE), BF),
+            pltpu.VMEM((count, 2, rows, WIDE), BF),
+            pltpu.SemaphoreType.DMA((count, 2)),
+            pltpu.SemaphoreType.DMA((count,)),
+            pltpu.SemaphoreType.DMA((max(len(extra), 1),)),
+        ]
+        + [pltpu.VMEM(e.shape, e.dtype) for e in extra],
+        compiler_params=pltpu.CompilerParams(vmem_limit_bytes=60 * 2**20),
         cost_estimate=pl.CostEstimate(
-            flops=2 * rows * 2 * WIDE * WIDE * count,
-            bytes_accessed=count * 3 * rows * WIDE * 2,
-            transcendentals=0,
+            flops=int(micros * 1.15e9), bytes_accessed=int(micros * 3e6), transcendentals=0
         ),
     )(index, scale, panel, tall, wide, *operands)
 
 
-def square_end(acc, by, out_refs, keep_ref):
-    for part in range(2):
-        at = pl.ds(part * TALL, TALL)
-        out_refs[part][...] = (acc[at, :] * keep_ref[at, :].astype(F32)).astype(BF)
-
-
-def keep_sum(acc, by, out_refs):
-    out_refs[0][...] = acc[...]
-
-
-def sign_end(acc, by, out_refs, keep_ref, top_ref, bottom_ref, pack_ref):
-    first = jnp.concatenate([top_ref[...], bottom_ref[...]], axis=0)
-    first = (first.astype(F32) * by).astype(BF).astype(F32)
-    value = (keep_ref[...].astype(F32) * (1.5 * first - 0.5 * acc[...])).astype(BF)
-    out_refs[0][...] = jnp.dot(pack_ref[...], value, preferred_element_type=F32).astype(BF)
+def square_end(acc, by, outs, keep):
+    outs[0][...] = (acc[...] * keep[...].astype(F32)).astype(BF)
+
+
+def first_sum(acc, by, outs):
+    outs[0][...] = acc[...]
+
+
+def sign_end(acc, by, outs, so_far, keep, right, pack):
+    first = (right[...].astype(F32) * by).astype(BF).astype(F32)
+    cube = acc[...] + so_far[...]
+    value = (keep[...].astype(F32) * (1.5 * first - 0.5 * cube)).astype(BF)
+    outs[0][...] = jnp.dot(pack[...], value, preferred_element_type=F32).astype(BF)
 
 
 def unpack_body(place_ref, arrived_ref, out_ref):
@@ -137,6 +169,17 @@
     out_ref[...] = value[:, : out_ref.shape[1]]
 
 
+def after(ready, arrays):
+    anywhere = pl.BlockSpec(memory_space=pl.ANY)
+    return pl.pallas_call(
+        lambda *refs: None,
+        out_shape=[jax.ShapeDtypeStruct(a.shape, a.dtype) for a in arrays],
+        in_specs=[anywhere] * (len(arrays) + 1),
+        out_specs=[anywhere] * len(arrays),
+        input_output_aliases={k + 1: k for k in range(len(arrays))},
+    )(ready, *arrays)
+
+
 def send(array, axis, by):
     return lax.ppermute(array, axis, shift(2 if axis == "c" else 4, by))
 
@@ -145,14 +188,17 @@
     return [array] + [send(array, axis, by) for by in (1, 2, 3)]
 
 
-def column_panel(top, bottom):
-    before = (send(top, "x", 1), send(bottom, "x", 1))
-    after = (send(top, "x", 3), send(bottom, "x", 3))
-    opposite = (send(before[0], "x", 1), send(after[1], "x", 3))
-    near = [(top, bottom), before, after]
-    near = near + [tuple(send(half, "c", 1) for half in pair) for pair in near]
-    far = [opposite, tuple(send(half, "c", 1) for half in opposite)]
-    return near, far
+def column_panel(block, beside=None):
+    before, behind = send(block, "x", 1), send(block, "x", 3)
+    opposite = [send(before[:TALL], "x", 1), send(behind[TALL:], "x", 3)]
+    near = [(block,), (before,), (behind,)]
+    near = near + [(send(one, "c", 1),) for one, in near]
+    partial = None
+    if beside is not None:
+        partial = beside(near)
+        opposite = after(partial, opposite)
+    far = [tuple(opposite), tuple(send(half, "c", 1) for half in opposite)]
+    return near, far, partial
 
 
 def on_device(hamiltonian, new_atom, pattern):
@@ -200,10 +246,10 @@
     broad = eq(np.arange(atoms_col)[:, None], jnp.asarray(of_col)[None, :])
     keep = exact(exact(tall[:, :atoms_row], rows_pattern), broad)
     right = moved * keep
-    top, bottom = right[:TALL], right[TALL:]
-    near, far = column_panel(top, bottom)
-
-    part_sum = jnp.sum(jnp.square(right.astype(F32)))
+    near, far, _ = column_panel(right)
+
+    part_sum = jnp.sum(jnp.square(right[TALL:].astype(F32)))
+    part_sum += jnp.sum(jnp.square(near[1][0][:TALL].astype(F32)))
     sent = jnp.concatenate(
         [rows_pattern.astype(F32), jnp.broadcast_to(part_sum, (8, atoms_col))], axis=0
     )
@@ -211,8 +257,8 @@
     seen = seen.reshape(col_count, atoms_row + 8, atoms_col)
     total = jnp.broadcast_to(jnp.sum(seen[:, atoms_row, 0]), (8, 128))
     total = total + send(total, "c", 1)
-    total = sum(around(total, "x"))[:1, :1]
-    scale = lax.rsqrt(total / order_all)
+    total = sum(around(total, "x"))
+    scale = lax.rsqrt(total[:1, :1] / order_all)
     cols_seen = jnp.stack([4 * jnp.mod(y - a, 4) + jnp.mod(z - b, 4) for a in range(4) for b in range(4)])
     atoms_seen = new_atom.reshape(col_count, atoms_col)[cols_seen].reshape(-1)
     all_cols = jnp.transpose(seen[:, :atoms_row], (1, 0, 2)).reshape(atoms_row, -1).astype(BF)
@@ -228,24 +274,22 @@
 
     near_index = jnp.stack([rho(d, o) for o in range(2) for d in (0, -1, 1)])
     far_index = jnp.stack([rho(2, o) for o in range(2)])
-    half_block = jax.ShapeDtypeStruct((TALL, WIDE), BF)
+    sums = jax.ShapeDtypeStruct((2 * TALL, WIDE), F32)
     whole = pl.BlockSpec(memory_space=pltpu.VMEM)
     of_panel = functools.partial(multiply, panel, tall, wide, scale)
-    square = of_panel(
-        jnp.concatenate([near_index, far_index]), near + far, True, square_end, [keep], [half_block] * 2
+    all_index = jnp.concatenate([near_index, far_index])
+    block = jax.ShapeDtypeStruct((2 * TALL, WIDE), BF)
+    square = of_panel(all_index, near + far, True, square_end, [keep], [block], 9)[0]
+    _, far, partial = column_panel(
+        square, lambda near: of_panel(near_index, near, False, first_sum, [], [sums], 11)[0]
     )
-    near, far = column_panel(*square)
-    partial = of_panel(
-        near_index, near, False, keep_sum, [], [jax.ShapeDtypeStruct((2 * TALL, WIDE), F32)]
-    )[0]
     base = packed(new_atom, row_here, atoms_row, row_count, slots_row)
     line = (base[:, :, None] * NBF + np.arange(NBF)).reshape(-1)
     row_of = np.where(of_row >= 0, np.arange(2 * TALL) - (np.arange(2 * TALL) // TALL) * (TALL - half), -1)
     pack_rows = eq(line[:, None], jnp.asarray(row_of)[None, :])
     sent_rows = of_panel(
-        far_index, far, False, sign_end, [keep, top, bottom, pack_rows],
-        [jax.ShapeDtypeStruct((row_count * slots_row * NBF, WIDE), BF)],
-        start=partial,
+        far_index, far, False, sign_end, [partial, keep, right, pack_rows],
+        [jax.ShapeDtypeStruct((row_count * slots_row * NBF, WIDE), BF)], 4,
     )[0]
     got_rows = lax.all_to_all(sent_rows.reshape(row_count, slots_row * NBF, WIDE), ROW, 0, 0)
     got_rows = got_rows.reshape(-1, WIDE)

time: 202 us -> 183 us (0.906)
  starting transfers between devices: 65.3 us -> 53.6 us
  local copies, waits for them, and re-layouts: 25.1 us -> 14.2 us
  Pallas kernels: 32.5 us -> 35.9 us
  waiting for transfers between devices: 49.4 us -> 46.4 us
  other arithmetic: 9.3 us -> 11.6 us
    ppermute x42 -> x32, starting transfers between devices: 53 us -> 41.6 us  [send(): return lax.ppermute(array, axis, shift(2 if axis == 'c' else 4, by))]
    unnamed x52 -> x54, local copies, waits for them, and re-layouts: 16.1 us -> 6.43 us
    pallas_call x3 -> x4, Pallas kernels: 29.1 us -> 32.6 us  [the longest x3 32.6 us: multiply(): pl.pallas_call(body, out_shape=out_shape, grid=(count,), in_specs=[smem,...]
    ppermute x42 -> x32, waiting for transfers between devices: 32.6 us -> 30.1 us  [send(): return lax.ppermute(array, axis, shift(2 if axis == 'c' else 4, by))]
  transfers between devices with their start and end apart: 45 -> 35, of which waited for: 13 -> 11; matrix products, arithmetic and copies ran while one was open for 10% -> 12% of each run, Pallas kernels for 5% -> 6%
where the time goes in v1:
time: 183 us
  starting transfers between devices  53.6 us (29%)
  waiting for transfers between devices  46.4 us (25%)
  Pallas kernels  35.9 us (20%)
  between operations  16.2 us (9%)
  local copies, waits for them, and re-layouts  14.2 us (8%)
  other arithmetic  11.6 us (6%)
  matrix products  5.01 us (3%)
    ppermute x32, starting transfers between devices, send(): return lax.ppermute(array, axis, shift(2 if axis == 'c' else 4, by))  41.6 us
    pallas_call x3, Pallas kernels, multiply(): pl.pallas_call(body, out_shape=out_shape, grid=(count,), in_specs=[smem,...  32.6 us
    ppermute x32, waiting for transfers between devices, send(): return lax.ppermute(array, axis, shift(2 if axis == 'c' else 4, by))  30.1 us
    all_to_all x1, waiting for transfers between devices, on_device(): lax.all_to_all(sent_rows.reshape(row_count, slots_row * NBF, WIDE), ROW,...  9.04 us
    all_to_all x1, starting transfers between devices, on_device(): lax.all_to_all(outgoing.reshape(col_count, width, 2 * TALL), COL, 0, 0)  7.98 us
    all_to_all x1, waiting for transfers between devices, on_device(): lax.all_to_all(outgoing.reshape(col_count, width, 2 * TALL), COL, 0, 0)  7.23 us
    unnamed x54, local copies, waits for them, and re-layouts  6.43 us
    all_to_all x1, starting transfers between devices, on_device(): lax.all_to_all(sent_rows.reshape(row_count, slots_row * NBF, WIDE), ROW,...  3.96 us
  transfers between devices with their start and end apart: 35, of which 11 were waited for; matrix products, arithmetic and copies ran while one was open for 12% of the time, Pallas kernels for 6%

profile of v1, /device:TPU:1, one launch (start us, length us, event | category | flops | bytes accessed | tf_op | source)
XLA Modules:
  0.0 182.9 jit_solution(98858706255361917)
XLA Ops:
  6.5 1.1 fusion.38
  7.7 0.9 fusion.14
  8.6 1.5 collective-permute-start
  10.3 0.6 convert_reduce_fusion.1
  11.6 0.7 convolution_convert_fusion
  12.3 1.2 copy.34
  13.5 8.0 %all-to-all-start = ((bf16[16,32,736]{2,1,0:T(8,128)(2,1)}), bf16[16,32,736]{2,1,0:T(8,128)(2,1)S(1)}, u32[]{:S(2)}, u32[]{:S(2)}) async-start(bf16[16,32,736]{2,1,0:T(8,128)(2,1)} %bitcast.17), calls=%async_computation | async-start | bytes 1572864 | tf_op jit(solution)/shard_map/all_to_all | solution.py:227
  21.8 0.7 fusion.28
  22.7 0.8 fusion.29
  23.5 1.3 collective-permute-start.1
  24.8 2.4 %collective-permute-start.2 = (bf16[2,56,28]{1,2,0:T(8,128)(2,1)S(1)}, bf16[2,56,28]{1,2,0:T(8,128)(2,1)S(1)}, u32[]{:S(2)}, u32[]{:S(2)}) collective-permute-start(bf16[2,56,28]{1,2,0:T(8,128)(2,1)S(1)} %get-tuple-element.18), channel_id=1, source_target_pairs={{0,64},{32,96},{64,0},{96,32},{1,65},{33,97},{65,1},{97,33},{2,66}... | collective-permute-start | bytes 18824 | tf_op jit(solution)/shard_map/ppermute | solution.py:184
  27.2 1.2 collective-permute-start.3
  29.3 1.0 collective-permute-done.3
  31.2 7.2 %all-to-all-done = bf16[16,32,736]{2,1,0:T(8,128)(2,1)S(1)} async-done(((bf16[16,32,736]{2,1,0:T(8,128)(2,1)}), bf16[16,32,736]{2,1,0:T(8,128)(2,1)S(1)}, u32[]{:S(2)}, u32[]{:S(2)}) %all-to-all-start) | async-done | bytes 753696 | tf_op jit(solution)/shard_map/all_to_all | solution.py:227
  38.4 0.6 fusion.11.refs_0_.refs_6_
  39.1 1.3 collective-permute-start.4
  40.4 1.4 collective-permute-start.15
  41.8 0.7 multiply_reduce_fusion.1
  42.5 9.0 %collective-permute-done.4.refs_1_ = bf16[736,384]{1,0:T(8,128)(2,1)S(1)} collective-permute-done((bf16[736,384]{1,0:T(8,128)(2,1)S(1)}, bf16[736,384]{1,0:T(8,128)(2,1)S(1)}, u32[]{:S(2)}, u32[]{:S(2)}) %collective-permute-start.4) | collective-permute-done | bytes 565280 | tf_op jit(solution)/shard_map/ppermute | solution.py:184
  51.5 0.8 multiply_reduce_fusion
  53.8 4.6 %collective-permute-start.6 = (f32[64,28]{0,1:T(8,128)S(1)}, f32[64,28]{0,1:T(8,128)S(1)}, u32[]{:S(2)}, u32[]{:S(2)}) collective-permute-start(f32[64,28]{0,1:T(8,128)S(1)} %concatenate.49), channel_id=1, source_target_pairs={{0,2},{1,3},{2,0},{3,1},{4,6},{5,7},{6,4},{7,5},{8,10},{9,11},{10,... | collective-permute-start | bytes 21512 | tf_op jit(solution)/shard_map/ppermute | solution.py:184
  58.4 1.9 %collective-permute-start.7 = (f32[64,28]{0,1:T(8,128)S(1)}, f32[64,28]{0,1:T(8,128)S(1)}, u32[]{:S(2)}, u32[]{:S(2)}) collective-permute-start(f32[64,28]{0,1:T(8,128)S(1)} %concatenate.49), channel_id=1, source_target_pairs={{0,3},{1,0},{2,1},{3,2},{4,7},{5,4},{6,5},{7,6},{8,11},{9,8},{10,9... | collective-permute-start | bytes 21512 | tf_op jit(solution)/shard_map/ppermute | solution.py:184
  60.4 1.3 collective-permute-done.7
  61.8 2.9 %collective-permute-start.9 = (f32[4,64,28]{1,2,0:T(8,128)S(1)}, f32[4,64,28]{1,2,0:T(8,128)S(1)}, u32[]{:S(2)}, u32[]{:S(2)}) collective-permute-start(f32[4,64,28]{1,2,0:T(8,128)S(1)} %get-tuple-element.16), channel_id=1, source_target_pairs={{0,8},{4,12},{8,0},{12,4},{1,9},{5,13},{9,1},{13,5},{2,10},{6,14},... | collective-permute-start | bytes 86024 | tf_op jit(solution)/shard_map/ppermute | solution.py:184
  64.7 1.3 collective-permute-start.10
  66.0 1.8 %collective-permute-done.8 = f32[4,64,28]{1,2,0:T(8,128)S(1)} collective-permute-done((f32[4,64,28]{1,2,0:T(8,128)S(1)}, f32[4,64,28]{1,2,0:T(8,128)S(1)}, u32[]{:S(2)}, u32[]{:S(2)}) %collective-permute-start.8) | collective-permute-done | bytes 28704 | tf_op jit(solution)/shard_map/ppermute | solution.py:184
  67.9 2.0 %collective-permute-done.9 = f32[4,64,28]{1,2,0:T(8,128)S(1)} collective-permute-done((f32[4,64,28]{1,2,0:T(8,128)S(1)}, f32[4,64,28]{1,2,0:T(8,128)S(1)}, u32[]{:S(2)}, u32[]{:S(2)}) %collective-permute-start.9) | collective-permute-done | bytes 28704 | tf_op jit(solution)/shard_map/ppermute | solution.py:184
  69.8 0.7 collective-permute-done.10
  70.6 0.8 slice_reduce_fusion
  71.4 0.7 broadcast_in_dim.24
  72.0 5.9 %collective-permute-start.11 = (f32[8,128]{1,0:T(8,128)S(1)}, f32[8,128]{1,0:T(8,128)S(1)}, u32[]{:S(2)}, u32[]{:S(2)}) collective-permute-start(f32[8,128]{1,0:T(8,128)S(1)} %broadcast_in_dim.24), channel_id=1, source_target_pairs={{0,16},{16,0},{1,17},{17,1},{2,18},{18,2},{3,19},{19,3},{4,20},{20... | collective-permute-start | bytes 12296 | tf_op jit(solution)/shard_map/ppermute | solution.py:184
  78.1 2.7 %collective-permute-start.20 = (bf16[368,384]{1,0:T(8,128)(2,1)S(1)}, bf16[368,384]{1,0:T(8,128)(2,1)}, u32[]{:S(2)}, u32[]{:S(2)}) collective-permute-start(bf16[368,384]{1,0:T(8,128)(2,1)S(1)} %slice.55), channel_id=1, source_target_pairs={{0,96},{32,0},{64,32},{96,64},{1,97},{33,1},{65,33},{97,65},{2,98}... | collective-permute-start | bytes 847880 | tf_op jit(solution)/shard_map/ppermute | solution.py:184
  80.8 0.7 broadcast_add_fusion.1
  81.6 1.2 collective-permute-start.13
  82.8 1.4 collective-permute-start.14
  85.5 2.3 %collective-permute-done.12 = f32[8,128]{1,0:T(8,128)S(1)} collective-permute-done((f32[8,128]{1,0:T(8,128)S(1)}, f32[8,128]{1,0:T(8,128)S(1)}, u32[]{:S(2)}, u32[]{:S(2)}) %collective-permute-start.12) | collective-permute-done | bytes 4128 | tf_op jit(solution)/shard_map/ppermute | solution.py:184
  87.8 0.8 collective-permute-start.16
  90.1 2.9 %fusion.8.wide_ref = bf16[8,64,768]{2,1,0:T(8,128)(2,1)} fusion(s32[8,768]{1,0:T(8,128)S(1)} %copy-done.26, s32[448]{0:T(512)S(1)} %eq.345, bf16[56,448]{1,0:T(8,128)(2,1)S(1)} %copy.35), kind=kOutput, calls=%fused_computation.13 | convolution fusion | flops 355467264 | bytes 862976 | tf_op jit(solution)/shard_map/ia,ran->rin/dot_general | solution.py:268
  93.1 0.7 add_add_fusion
  93.8 0.6 slice.41
  95.2 0.7 copy-done.18
  96.1 14.0 %shard_map.217.refs_0_ = bf16[736,384]{1,0:T(8,128)(2,1)} custom-call(s32[8]{0:T(128)} %concatenate.50.index_ref, f32[1,1]{1,0:T(1,128)S(6)} %rsqrt.3.scale_ref, bf16[16,736,384]{2,1,0:T(8,128)(2,1)} %bitcast.89, bf16[736,64]{1,0:T(8,128)(2,1)} %get-tuple-element.19.tall_ref, bf16[8,64,768]{2,1,0:T(8,128)(2,1)} %fusion.8.wide_ref, ...), custom_call_target="tpu_custom_call" | custom-call | flops 10350000128 | bytes 27000000 | tf_op jit(solution)/shard_map/pallas_call | solution.py:130
  110.6 2.3 %collective-permute-start.24 = (bf16[736,384]{1,0:T(8,128)(2,1)}, bf16[736,384]{1,0:T(8,128)(2,1)S(1)}, u32[]{:S(2)}, u32[]{:S(2)}) collective-permute-start(bf16[736,384]{1,0:T(8,128)(2,1)} %shard_map.217.refs_0_), channel_id=1, source_target_pairs={{0,96},{32,0},{64,32},{96,64},{1,97},{33,1},{65,33},{97,65},{2,98}... | collective-permute-start | bytes 1695752 | tf_op jit(solution)/shard_map/ppermute | solution.py:184
  113.4 0.7 collective-permute-start.25
  114.2 11.8 %collective-permute-done.23.refs_1_ = bf16[736,384]{1,0:T(8,128)(2,1)S(1)} collective-permute-done((bf16[736,384]{1,0:T(8,128)(2,1)}, bf16[736,384]{1,0:T(8,128)(2,1)S(1)}, u32[]{:S(2)}, u32[]{:S(2)}) %collective-permute-start.23) | collective-permute-done | bytes 565280 | tf_op jit(solution)/shard_map/ppermute | solution.py:184
  126.0 0.9 collective-permute-start.26
  127.0 0.6 stack.215.index_ref
  128.4 2.4 %collective-permute-start.29 = (bf16[368,384]{1,0:T(8,128)(2,1)S(1)}, bf16[368,384]{1,0:T(8,128)(2,1)S(1)}, u32[]{:S(2)}, u32[]{:S(2)}) collective-permute-start(bf16[368,384]{1,0:T(8,128)(2,1)S(1)} %slice.57), channel_id=1, source_target_pairs={{0,96},{32,0},{64,32},{96,64},{1,97},{33,1},{65,33},{97,65},{2,98}... | collective-permute-start | bytes 847880 | tf_op jit(solution)/shard_map/ppermute | solution.py:184
  130.9 0.8 copy-done.19
  131.8 0.8 copy-done.21
  132.6 11.3 %shard_map.218.refs_0_.refs_4_ = f32[736,384]{1,0:T(8,128)} custom-call(s32[6]{0:T(128)} %stack.215.index_ref, f32[1,1]{1,0:T(1,128)S(6)} %rsqrt.3.scale_ref, bf16[16,736,384]{2,1,0:T(8,128)(2,1)} %bitcast.90, bf16[736,64]{1,0:T(8,128)(2,1)} %get-tuple-element.19.tall_ref, bf16[8,64,768]{2,1,0:T(8,128)(2,1)} %fusion.8.wide_ref, ...), custom_call_target="tpu_custom_call" | custom-call | flops 12650000384 | bytes 33000000 | tf_op jit(solution)/shard_map/pallas_call | solution.py:130
  144.0 0.7 copy-done.3
  144.7 0.7 copy-done.4
  145.5 1.0 collective-permute-start.30
  146.4 0.6 pad_add_fusion.index_ref
  147.2 1.4 compare_convert_fusion.refs_7_
  148.6 0.7 copy-done.24
  149.3 0.7 copy-done.25
  150.0 7.2 %shard_map.220 = bf16[832,384]{1,0:T(8,128)(2,1)} custom-call(s32[2]{0:T(128)} %pad_add_fusion.index_ref, f32[1,1]{1,0:T(1,128)S(6)} %rsqrt.3.scale_ref, bf16[16,736,384]{2,1,0:T(8,128)(2,1)} %bitcast.91, bf16[736,64]{1,0:T(8,128)(2,1)} %get-tuple-element.19.tall_ref, bf16[8,64,768]{2,1,0:T(8,128)(2,1)} %fusion.8.wide_ref, ...), custom_call_target="tpu_custom_call" | custom-call | flops 4600000000 | bytes 12000000 | tf_op jit(solution)/shard_map/pallas_call | solution.py:130
  157.2 4.0 %all-to-all-start.1 = ((bf16[8,104,384]{2,1,0:T(8,128)(2,1)}), bf16[8,104,384]{2,1,0:T(8,128)(2,1)S(1)}, u32[]{:S(2)}, u32[]{:S(2)}) async-start(bf16[8,104,384]{2,1,0:T(8,128)(2,1)} %bitcast.76), calls=%async_computation.1 | async-start | bytes 1277952 | tf_op jit(solution)/shard_map/all_to_all | solution.py:294
  161.5 1.4 fusion.4.place_ref
  162.9 9.0 %all-to-all-done.1 = bf16[8,104,384]{2,1,0:T(8,128)(2,1)S(1)} async-done(((bf16[8,104,384]{2,1,0:T(8,128)(2,1)}), bf16[8,104,384]{2,1,0:T(8,128)(2,1)S(1)}, u32[]{:S(2)}, u32[]{:S(2)}) %all-to-all-start.1) | async-done | bytes 639008 | tf_op jit(solution)/shard_map/all_to_all | solution.py:294
  171.9 0.8 copy-done
  172.7 3.3 %shard_map.221 = f32[728,364]{1,0:T(8,128)} custom-call(bf16[728,832]{1,0:T(8,128)(2,1)} %fusion.4.place_ref, bf16[832,384]{1,0:T(8,128)(2,1)} %bitcast.74), custom_call_target="tpu_custom_call" | custom-call | tf_op jit(solution)/shard_map/pallas_call | solution.py:299
  (150 shorter events, 9.2 us)
Async XLA Ops:
  6.5 88.6 %all-gather.3.cloned.1.call-start = ((), (), s32[]{:S(2)}) async-start(), calls=%async_computation.2 | async-start | bytes 9609216 | tf_op jit(solution)/shard_map/all_gather | solution.py:219
  7.7 0.9 copy-start.9
  7.7 2.4 %copy-start.11 = (s32[448]{0:T(512)S(1)}, s32[448]{0:T(512)}, u32[]{:S(2)}) copy-start(s32[448]{0:T(512)} %param.24) | copy-start | bytes 5380
  7.7 2.6 %copy-start.16 = (pred[28,28]{1,0:T(8,128)(4,1)S(1)}, pred[28,28]{1,0:T(8,128)(4,1)}, u32[]{:S(2)}) copy-start(pred[28,28]{1,0:T(8,128)(4,1)} %constant.326) | copy-start | bytes 2356
  8.6 14.9 %collective-permute-start = (bf16[56,28]{0,1:T(8,128)(2,1)S(1)}, bf16[56,28]{0,1:T(8,128)(2,1)S(1)}, u32[]{:S(2)}, u32[]{:S(2)}) collective-permute-start(bf16[56,28]{0,1:T(8,128)(2,1)S(1)} %convert_element_type.72), channel_id=1, source_target_pairs={{0,16},{16,0},{1,17},{17,1},{2,18},{18,2},{3,19},{19,3},{4,20},{20... | collective-permute-start | bytes 9416 | tf_op jit(solution)/shard_map/ppermute | solution.py:184
  13.5 8.3 %copy-start.10 = (pred[1,28,28]{2,0,1:T(4,128)(4,1)S(1)}, pred[1,28,28]{2,0,1:T(4,128)(4,1)}, u32[]{:S(2)}) copy-start(pred[1,28,28]{2,0,1:T(4,128)(4,1)} %constant.297.clone) | copy-start | bytes 2356
  13.5 9.1 %copy-start.15 = (s32[736]{0:T(1024)S(1)}, s32[736]{0:T(1024)}, u32[]{:S(2)}) copy-start(s32[736]{0:T(1024)} %constant.302.clone) | copy-start | bytes 8836
  13.5 17.1 %copy-start.17 = (s32[384]{0:T(512)S(1)}, s32[384]{0:T(512)}, u32[]{:S(2)}) copy-start(s32[384]{0:T(512)} %constant.304.clone) | copy-start | bytes 4612
  13.5 24.9 %all-to-all-start = ((bf16[16,32,736]{2,1,0:T(8,128)(2,1)}), bf16[16,32,736]{2,1,0:T(8,128)(2,1)S(1)}, u32[]{:S(2)}, u32[]{:S(2)}) async-start(bf16[16,32,736]{2,1,0:T(8,128)(2,1)} %bitcast.17), calls=%async_computation | async-start | bytes 1572864 | tf_op jit(solution)/shard_map/all_to_all | solution.py:227
  23.5 5.7 %collective-permute-start.1 = (bf16[2,56,28]{1,2,0:T(8,128)(2,1)S(1)}, bf16[2,56,28]{1,2,0:T(8,128)(2,1)S(1)}, u32[]{:S(2)}, u32[]{:S(2)}) collective-permute-start(bf16[2,56,28]{1,2,0:T(8,128)(2,1)S(1)} %get-tuple-element.18), channel_id=1, source_target_pairs={{0,32},{32,64},{64,96},{96,0},{1,33},{33,65},{65,97},{97,1},{2,34}... | collective-permute-start | bytes 18824 | tf_op jit(solution)/shard_map/ppermute | solution.py:184
  24.8 4.5 %collective-permute-start.2 = (bf16[2,56,28]{1,2,0:T(8,128)(2,1)S(1)}, bf16[2,56,28]{1,2,0:T(8,128)(2,1)S(1)}, u32[]{:S(2)}, u32[]{:S(2)}) collective-permute-start(bf16[2,56,28]{1,2,0:T(8,128)(2,1)S(1)} %get-tuple-element.18), channel_id=1, source_target_pairs={{0,64},{32,96},{64,0},{96,32},{1,65},{33,97},{65,1},{97,33},{2,66}... | collective-permute-start | bytes 18824 | tf_op jit(solution)/shard_map/ppermute | solution.py:184
  27.2 3.0 %collective-permute-start.3 = (bf16[2,56,28]{1,2,0:T(8,128)(2,1)S(1)}, bf16[2,56,28]{1,2,0:T(8,128)(2,1)S(1)}, u32[]{:S(2)}, u32[]{:S(2)}) collective-permute-start(bf16[2,56,28]{1,2,0:T(8,128)(2,1)S(1)} %get-tuple-element.18), channel_id=1, source_target_pairs={{0,96},{32,0},{64,32},{96,64},{1,97},{33,1},{65,33},{97,65},{2,98}... | collective-permute-start | bytes 18824 | tf_op jit(solution)/shard_map/ppermute | solution.py:184
  31.2 7.8 %copy-start.2 = (bf16[736,384]{1,0:T(8,128)(2,1)}, bf16[736,384]{1,0:T(8,128)(2,1)S(1)}, u32[]{:S(2)}) copy-start(bf16[736,384]{1,0:T(8,128)(2,1)S(1)} %convolution_convert_fusion.2.refs_10_.refs_5_) | copy-start | bytes 1695748
  39.0 48.8 %copy-start.8 = (bf16[736,384]{1,0:T(8,128)(2,1)}, bf16[736,384]{1,0:T(8,128)(2,1)S(1)}, u32[]{:S(2)}) copy-start(bf16[736,384]{1,0:T(8,128)(2,1)S(1)} %fusion.11.refs_0_.refs_6_) | copy-start | bytes 1695748
  39.1 12.5 %collective-permute-start.4 = (bf16[736,384]{1,0:T(8,128)(2,1)S(1)}, bf16[736,384]{1,0:T(8,128)(2,1)S(1)}, u32[]{:S(2)}, u32[]{:S(2)}) collective-permute-start(bf16[736,384]{1,0:T(8,128)(2,1)S(1)} %fusion.11.refs_0_.refs_6_), channel_id=1, source_target_pairs={{0,32},{32,64},{64,96},{96,0},{1,33},{33,65},{65,97},{97,1},{2,34}... | collective-permute-start | bytes 1695752 | tf_op jit(solution)/shard_map/ppermute | solution.py:184
  40.4 37.7 %collective-permute-start.15 = (bf16[736,384]{1,0:T(8,128)(2,1)S(1)}, bf16[736,384]{1,0:T(8,128)(2,1)S(1)}, u32[]{:S(2)}, u32[]{:S(2)}) collective-permute-start(bf16[736,384]{1,0:T(8,128)(2,1)S(1)} %fusion.11.refs_0_.refs_6_), channel_id=1, source_target_pairs={{0,96},{32,0},{64,32},{96,64},{1,97},{33,1},{65,33},{97,65},{2,98}... | collective-permute-start | bytes 1695752 | tf_op jit(solution)/shard_map/ppermute | solution.py:184
  51.5 37.1 %copy-start.1 = (bf16[736,384]{1,0:T(8,128)(2,1)}, bf16[736,384]{1,0:T(8,128)(2,1)S(1)}, u32[]{:S(2)}) copy-start(bf16[736,384]{1,0:T(8,128)(2,1)S(1)} %collective-permute-done.4.refs_1_) | copy-start | bytes 1695748
  53.7 6.6 %collective-permute-start.5 = (f32[64,28]{0,1:T(8,128)S(1)}, f32[64,28]{0,1:T(8,128)S(1)}, u32[]{:S(2)}, u32[]{:S(2)}) collective-permute-start(f32[64,28]{0,1:T(8,128)S(1)} %concatenate.49), channel_id=1, source_target_pairs={{0,1},{1,2},{2,3},{3,0},{4,5},{5,6},{6,7},{7,4},{8,9},{9,10},{10,1... | collective-permute-start | bytes 21512 | tf_op jit(solution)/shard_map/ppermute | solution.py:184
  53.8 6.6 %collective-permute-start.6 = (f32[64,28]{0,1:T(8,128)S(1)}, f32[64,28]{0,1:T(8,128)S(1)}, u32[]{:S(2)}, u32[]{:S(2)}) collective-permute-start(f32[64,28]{0,1:T(8,128)S(1)} %concatenate.49), channel_id=1, source_target_pairs={{0,2},{1,3},{2,0},{3,1},{4,6},{5,7},{6,4},{7,5},{8,10},{9,11},{10,... | collective-permute-start | bytes 21512 | tf_op jit(solution)/shard_map/ppermute | solution.py:184
  58.4 3.3 %collective-permute-start.7 = (f32[64,28]{0,1:T(8,128)S(1)}, f32[64,28]{0,1:T(8,128)S(1)}, u32[]{:S(2)}, u32[]{:S(2)}) collective-permute-start(f32[64,28]{0,1:T(8,128)S(1)} %concatenate.49), channel_id=1, source_target_pairs={{0,3},{1,0},{2,1},{3,2},{4,7},{5,4},{6,5},{7,6},{8,11},{9,8},{10,9... | collective-permute-start | bytes 21512 | tf_op jit(solution)/shard_map/ppermute | solution.py:184
  61.7 6.2 %collective-permute-start.8 = (f32[4,64,28]{1,2,0:T(8,128)S(1)}, f32[4,64,28]{1,2,0:T(8,128)S(1)}, u32[]{:S(2)}, u32[]{:S(2)}) collective-permute-start(f32[4,64,28]{1,2,0:T(8,128)S(1)} %get-tuple-element.16), channel_id=1, source_target_pairs={{0,4},{4,8},{8,12},{12,0},{1,5},{5,9},{9,13},{13,1},{2,6},{6,10},{... | collective-permute-start | bytes 86024 | tf_op jit(solution)/shard_map/ppermute | solution.py:184
  61.8 8.0 %collective-permute-start.9 = (f32[4,64,28]{1,2,0:T(8,128)S(1)}, f32[4,64,28]{1,2,0:T(8,128)S(1)}, u32[]{:S(2)}, u32[]{:S(2)}) collective-permute-start(f32[4,64,28]{1,2,0:T(8,128)S(1)} %get-tuple-element.16), channel_id=1, source_target_pairs={{0,8},{4,12},{8,0},{12,4},{1,9},{5,13},{9,1},{13,5},{2,10},{6,14},... | collective-permute-start | bytes 86024 | tf_op jit(solution)/shard_map/ppermute | solution.py:184
  64.7 5.9 %collective-permute-start.10 = (f32[4,64,28]{1,2,0:T(8,128)S(1)}, f32[4,64,28]{1,2,0:T(8,128)S(1)}, u32[]{:S(2)}, u32[]{:S(2)}) collective-permute-start(f32[4,64,28]{1,2,0:T(8,128)S(1)} %get-tuple-element.16), channel_id=1, source_target_pairs={{0,12},{4,0},{8,4},{12,8},{1,13},{5,1},{9,5},{13,9},{2,14},{6,2},{... | collective-permute-start | bytes 86024 | tf_op jit(solution)/shard_map/ppermute | solution.py:184
  70.6 19.5 %copy-start.26 = (s32[8,768]{1,0:T(8,128)S(1)}, s32[8,768]{1,0:T(8,128)}, u32[]{:S(2)}) copy-start(s32[8,768]{1,0:T(8,128)} %constant.333) | copy-start | bytes 73732
  72.0 8.8 %collective-permute-start.11 = (f32[8,128]{1,0:T(8,128)S(1)}, f32[8,128]{1,0:T(8,128)S(1)}, u32[]{:S(2)}, u32[]{:S(2)}) collective-permute-start(f32[8,128]{1,0:T(8,128)S(1)} %broadcast_in_dim.24), channel_id=1, source_target_pairs={{0,16},{16,0},{1,17},{17,1},{2,18},{18,2},{3,19},{19,3},{4,20},{20... | collective-permute-start | bytes 12296 | tf_op jit(solution)/shard_map/ppermute | solution.py:184
  78.0 11.4 %collective-permute-start.19 = (bf16[368,384]{1,0:T(8,128)(2,1)S(1)}, bf16[368,384]{1,0:T(8,128)(2,1)}, u32[]{:S(2)}, u32[]{:S(2)}) collective-permute-start(bf16[368,384]{1,0:T(8,128)(2,1)S(1)} %slice.52), channel_id=1, source_target_pairs={{0,32},{32,64},{64,96},{96,0},{1,33},{33,65},{65,97},{97,1},{2,34}... | collective-permute-start | bytes 847880 | tf_op jit(solution)/shard_map/ppermute | solution.py:184
  78.1 15.0 %copy-start.5 = (bf16[736,384]{1,0:T(8,128)(2,1)}, bf16[736,384]{1,0:T(8,128)(2,1)S(1)}, u32[]{:S(2)}) copy-start(bf16[736,384]{1,0:T(8,128)(2,1)S(1)} %collective-permute-done.15.refs_2_) | copy-start | bytes 1695748
  78.1 11.6 %collective-permute-start.20 = (bf16[368,384]{1,0:T(8,128)(2,1)S(1)}, bf16[368,384]{1,0:T(8,128)(2,1)}, u32[]{:S(2)}, u32[]{:S(2)}) collective-permute-start(bf16[368,384]{1,0:T(8,128)(2,1)S(1)} %slice.55), channel_id=1, source_target_pairs={{0,96},{32,0},{64,32},{96,64},{1,97},{33,1},{65,33},{97,65},{2,98}... | collective-permute-start | bytes 847880 | tf_op jit(solution)/shard_map/ppermute | solution.py:184
  81.5 6.3 %collective-permute-start.12 = (f32[8,128]{1,0:T(8,128)S(1)}, f32[8,128]{1,0:T(8,128)S(1)}, u32[]{:S(2)}, u32[]{:S(2)}) collective-permute-start(f32[8,128]{1,0:T(8,128)S(1)} %broadcast_add_fusion.1), channel_id=1, source_target_pairs={{0,32},{32,64},{64,96},{96,0},{1,33},{33,65},{65,97},{97,1},{2,34}... | collective-permute-start | bytes 12296 | tf_op jit(solution)/shard_map/ppermute | solution.py:184
  81.6 7.1 %collective-permute-start.13 = (f32[8,128]{1,0:T(8,128)S(1)}, f32[8,128]{1,0:T(8,128)S(1)}, u32[]{:S(2)}, u32[]{:S(2)}) collective-permute-start(f32[8,128]{1,0:T(8,128)S(1)} %broadcast_add_fusion.1), channel_id=1, source_target_pairs={{0,64},{32,96},{64,0},{96,32},{1,65},{33,97},{65,1},{97,33},{2,66}... | collective-permute-start | bytes 12296 | tf_op jit(solution)/shard_map/ppermute | solution.py:184
  82.8 5.9 %collective-permute-start.14 = (f32[8,128]{1,0:T(8,128)S(1)}, f32[8,128]{1,0:T(8,128)S(1)}, u32[]{:S(2)}, u32[]{:S(2)}) collective-permute-start(f32[8,128]{1,0:T(8,128)S(1)} %broadcast_add_fusion.1), channel_id=1, source_target_pairs={{0,96},{32,0},{64,32},{96,64},{1,97},{33,1},{65,33},{97,65},{2,98}... | collective-permute-start | bytes 12296 | tf_op jit(solution)/shard_map/ppermute | solution.py:184
  87.8 7.2 %collective-permute-start.16 = (bf16[736,384]{1,0:T(8,128)(2,1)S(1)}, bf16[736,384]{1,0:T(8,128)(2,1)S(1)}, u32[]{:S(2)}, u32[]{:S(2)}) collective-permute-start(bf16[736,384]{1,0:T(8,128)(2,1)S(1)} %fusion.11.refs_0_.refs_6_), channel_id=1, source_target_pairs={{0,16},{16,0},{1,17},{17,1},{2,18},{18,2},{3,19},{19,3},{4,20},{20... | collective-permute-start | bytes 1695752 | tf_op jit(solution)/shard_map/ppermute | solution.py:184
  88.7 6.5 %collective-permute-start.17 = (bf16[736,384]{1,0:T(8,128)(2,1)S(1)}, bf16[736,384]{1,0:T(8,128)(2,1)}, u32[]{:S(2)}, u32[]{:S(2)}) collective-permute-start(bf16[736,384]{1,0:T(8,128)(2,1)S(1)} %collective-permute-done.4.refs_1_), channel_id=1, source_target_pairs={{0,16},{16,0},{1,17},{17,1},{2,18},{18,2},{3,19},{19,3},{4,20},{20... | collective-permute-start | bytes 1695752 | tf_op jit(solution)/shard_map/ppermute | solution.py:184
  88.8 6.4 %collective-permute-start.18 = (bf16[736,384]{1,0:T(8,128)(2,1)S(1)}, bf16[736,384]{1,0:T(8,128)(2,1)}, u32[]{:S(2)}, u32[]{:S(2)}) collective-permute-start(bf16[736,384]{1,0:T(8,128)(2,1)S(1)} %collective-permute-done.15.refs_2_), channel_id=1, source_target_pairs={{0,16},{16,0},{1,17},{17,1},{2,18},{18,2},{3,19},{19,3},{4,20},{20... | collective-permute-start | bytes 1695752 | tf_op jit(solution)/shard_map/ppermute | solution.py:184
  89.4 5.7 %collective-permute-start.21 = (bf16[368,384]{1,0:T(8,128)(2,1)}, bf16[368,384]{1,0:T(8,128)(2,1)S(1)}, u32[]{:S(2)}, u32[]{:S(2)}) collective-permute-start(bf16[368,384]{1,0:T(8,128)(2,1)} %collective-permute-done.19.refs_6_), channel_id=1, source_target_pairs={{0,16},{16,0},{1,17},{17,1},{2,18},{18,2},{3,19},{19,3},{4,20},{20... | collective-permute-start | bytes 847880 | tf_op jit(solution)/shard_map/ppermute | solution.py:184
  89.7 5.4 %collective-permute-start.22 = (bf16[368,384]{1,0:T(8,128)(2,1)}, bf16[368,384]{1,0:T(8,128)(2,1)S(1)}, u32[]{:S(2)}, u32[]{:S(2)}) collective-permute-start(bf16[368,384]{1,0:T(8,128)(2,1)} %collective-permute-done.20.refs_7_), channel_id=1, source_target_pairs={{0,16},{16,0},{1,17},{17,1},{2,18},{18,2},{3,19},{19,3},{4,20},{20... | collective-permute-start | bytes 847880 | tf_op jit(solution)/shard_map/ppermute | solution.py:184
  95.1 0.8 copy-start.18
  95.1 0.9 copy-start.22
  95.1 1.0 copy-start.23
  96.1 16.8 %copy-start.13 = (pred[56,56]{1,0:T(8,128)(4,1)S(1)}, pred[56,56]{1,0:T(8,128)(4,1)}, u32[]{:S(2)}) copy-start(pred[56,56]{1,0:T(8,128)(4,1)} %constant.334) | copy-start | bytes 9412
  96.1 31.6 %copy-start.12 = (pred[1,56,56]{2,1,0:T(8,128)(4,1)S(1)}, pred[1,56,56]{2,1,0:T(8,128)(4,1)}, u32[]{:S(2)}) copy-start(pred[1,56,56]{2,1,0:T(8,128)(4,1)} %constant.307.clone) | copy-start | bytes 9412
  110.1 15.9 %collective-permute-start.23 = (bf16[736,384]{1,0:T(8,128)(2,1)}, bf16[736,384]{1,0:T(8,128)(2,1)S(1)}, u32[]{:S(2)}, u32[]{:S(2)}) collective-permute-start(bf16[736,384]{1,0:T(8,128)(2,1)} %shard_map.217.refs_0_), channel_id=1, source_target_pairs={{0,32},{32,64},{64,96},{96,0},{1,33},{33,65},{65,97},{97,1},{2,34}... | collective-permute-start | bytes 1695752 | tf_op jit(solution)/shard_map/ppermute | solution.py:184
  110.6 16.2 %collective-permute-start.24 = (bf16[736,384]{1,0:T(8,128)(2,1)}, bf16[736,384]{1,0:T(8,128)(2,1)S(1)}, u32[]{:S(2)}, u32[]{:S(2)}) collective-permute-start(bf16[736,384]{1,0:T(8,128)(2,1)} %shard_map.217.refs_0_), channel_id=1, source_target_pairs={{0,96},{32,0},{64,32},{96,64},{1,97},{33,1},{65,33},{97,65},{2,98}... | collective-permute-start | bytes 1695752 | tf_op jit(solution)/shard_map/ppermute | solution.py:184
  113.4 17.4 %collective-permute-start.25 = (bf16[736,384]{1,0:T(8,128)(2,1)}, bf16[736,384]{1,0:T(8,128)(2,1)S(1)}, u32[]{:S(2)}, u32[]{:S(2)}) collective-permute-start(bf16[736,384]{1,0:T(8,128)(2,1)} %shard_map.217.refs_0_), channel_id=1, source_target_pairs={{0,16},{16,0},{1,17},{17,1},{2,18},{18,2},{3,19},{19,3},{4,20},{20... | collective-permute-start | bytes 1695752 | tf_op jit(solution)/shard_map/ppermute | solution.py:184
  126.0 4.9 %copy-start.6 = (bf16[736,384]{1,0:T(8,128)(2,1)}, bf16[736,384]{1,0:T(8,128)(2,1)S(1)}, u32[]{:S(2)}) copy-start(bf16[736,384]{1,0:T(8,128)(2,1)S(1)} %collective-permute-done.23.refs_1_) | copy-start | bytes 1695748
  126.0 4.8 %collective-permute-start.26 = (bf16[736,384]{1,0:T(8,128)(2,1)S(1)}, bf16[736,384]{1,0:T(8,128)(2,1)S(1)}, u32[]{:S(2)}, u32[]{:S(2)}) collective-permute-start(bf16[736,384]{1,0:T(8,128)(2,1)S(1)} %collective-permute-done.23.refs_1_), channel_id=1, source_target_pairs={{0,16},{16,0},{1,17},{17,1},{2,18},{18,2},{3,19},{19,3},{4,20},{20... | collective-permute-start | bytes 1695752 | tf_op jit(solution)/shard_map/ppermute | solution.py:184
  126.8 4.0 %copy-start.7 = (bf16[736,384]{1,0:T(8,128)(2,1)}, bf16[736,384]{1,0:T(8,128)(2,1)S(1)}, u32[]{:S(2)}) copy-start(bf16[736,384]{1,0:T(8,128)(2,1)S(1)} %collective-permute-done.24.refs_2_) | copy-start | bytes 1695748
  126.8 4.0 %collective-permute-start.27 = (bf16[736,384]{1,0:T(8,128)(2,1)S(1)}, bf16[736,384]{1,0:T(8,128)(2,1)S(1)}, u32[]{:S(2)}, u32[]{:S(2)}) collective-permute-start(bf16[736,384]{1,0:T(8,128)(2,1)S(1)} %collective-permute-done.24.refs_2_), channel_id=1, source_target_pairs={{0,16},{16,0},{1,17},{17,1},{2,18},{18,2},{3,19},{19,3},{4,20},{20... | collective-permute-start | bytes 1695752 | tf_op jit(solution)/shard_map/ppermute | solution.py:184
  128.0 16.1 %collective-permute-start.28 = (bf16[368,384]{1,0:T(8,128)(2,1)S(1)}, bf16[368,384]{1,0:T(8,128)(2,1)S(1)}, u32[]{:S(2)}, u32[]{:S(2)}) collective-permute-start(bf16[368,384]{1,0:T(8,128)(2,1)S(1)} %slice.56), channel_id=1, source_target_pairs={{0,32},{32,64},{64,96},{96,0},{1,33},{33,65},{65,97},{97,1},{2,34}... | collective-permute-start | bytes 847880 | tf_op jit(solution)/shard_map/ppermute | solution.py:184
  128.4 15.6 %collective-permute-start.29 = (bf16[368,384]{1,0:T(8,128)(2,1)S(1)}, bf16[368,384]{1,0:T(8,128)(2,1)S(1)}, u32[]{:S(2)}, u32[]{:S(2)}) collective-permute-start(bf16[368,384]{1,0:T(8,128)(2,1)S(1)} %slice.57), channel_id=1, source_target_pairs={{0,96},{32,0},{64,32},{96,64},{1,97},{33,1},{65,33},{97,65},{2,98}... | collective-permute-start | bytes 847880 | tf_op jit(solution)/shard_map/ppermute | solution.py:184
  130.8 0.8 copy-start.19
  130.8 1.0 copy-start.20
  131.8 0.8 copy-start.21
  144.0 3.2 %copy-start.14 = (s32[736]{0:T(1024)S(1)}, s32[736]{0:T(1024)}, u32[]{:S(2)}) copy-start(s32[736]{0:T(1024)} %constant.309.clone) | copy-start | bytes 8836
  144.0 0.7 copy-start.3
  144.7 0.7 copy-start.4
  145.5 3.1 %collective-permute-start.30 = (bf16[368,384]{1,0:T(8,128)(2,1)}, bf16[368,384]{1,0:T(8,128)(2,1)S(1)}, u32[]{:S(2)}, u32[]{:S(2)}) collective-permute-start(bf16[368,384]{1,0:T(8,128)(2,1)} %get-tuple-element.7.refs_0_), channel_id=1, source_target_pairs={{0,16},{16,0},{1,17},{17,1},{2,18},{18,2},{3,19},{19,3},{4,20},{20... | collective-permute-start | bytes 847880 | tf_op jit(solution)/shard_map/ppermute | solution.py:184
  146.4 2.1 %collective-permute-start.31 = (bf16[368,384]{1,0:T(8,128)(2,1)}, bf16[368,384]{1,0:T(8,128)(2,1)S(1)}, u32[]{:S(2)}, u32[]{:S(2)}) collective-permute-start(bf16[368,384]{1,0:T(8,128)(2,1)} %get-tuple-element.8.refs_1_), channel_id=1, source_target_pairs={{0,16},{16,0},{1,17},{17,1},{2,18},{18,2},{3,19},{19,3},{4,20},{20... | collective-permute-start | bytes 847880 | tf_op jit(solution)/shard_map/ppermute | solution.py:184
  148.6 0.7 copy-start.24
  149.3 0.7 copy-start.25
  157.2 14.7 %all-to-all-start.1 = ((bf16[8,104,384]{2,1,0:T(8,128)(2,1)}), bf16[8,104,384]{2,1,0:T(8,128)(2,1)S(1)}, u32[]{:S(2)}, u32[]{:S(2)}) async-start(bf16[8,104,384]{2,1,0:T(8,128)(2,1)} %bitcast.76), calls=%async_computation.1 | async-start | bytes 1277952 | tf_op jit(solution)/shard_map/all_to_all | solution.py:294
  171.9 0.8 copy-start
Sparse Core Ops, SparseCore 0:
  9.5 85.0 all-gather.2

commit v2 on v1

--- a/solution.py
+++ b/solution.py
@@ -52,7 +52,30 @@
 WIDE = 384
 
 
-def multiply(panel, tall, wide, scale, index, blocks, scaled, epilogue, extra, out_shape, micros):
+def mask_rows(strips, step, wide_ref, at, left):
+    columns = left.shape[1]
+    line = lax.broadcasted_iota(jnp.int32, (8, columns), 0)
+    in_half = wide_ref.shape[1] // 2
+
+    def of_atom(half, atom):
+        return jnp.broadcast_to(wide_ref[at, pl.ds(half * in_half + atom, 1), :], (8, columns))
+
+    for start in range(0, left.shape[0], 16):
+        masks = []
+        for first in (start, start + 8):
+            half, row = divmod(first, TALL)
+            atom, more = divmod(row, NBF)
+            here = NBF - more
+            mask = of_atom(half, atom)
+            if here < 8:
+                mask = jnp.where(line < here, mask, of_atom(half, atom + 1) if atom + 1 < in_half else 0.0)
+            masks.append(mask)
+        rows = pl.ds(start, 16)
+        both = jnp.concatenate([strips[step, 0, rows], strips[step, 1, rows]], axis=1)
+        left[rows] = (both.astype(F32) * jnp.concatenate(masks, axis=0)).astype(BF)
+
+
+def multiply(panel, wide, scale, index, base, blocks, scaled, epilogue, extra, out_shape, micros, early=()):
     count = len(blocks)
     rows = panel.shape[1]
     flat = [(j, piece) for j, pieces in enumerate(blocks) for piece in pieces]
@@ -63,12 +86,12 @@
         for t in range(piece.shape[0] // TALL)
     ]
 
-    def body(index_ref, scale_ref, panel_ref, tall_ref, wide_ref, *refs):
+    def body(index_ref, scale_ref, panel_ref, wide_ref, *refs):
         pieces, refs = refs[: len(flat)], refs[len(flat) :]
-        more, refs = refs[: len(extra)], refs[len(extra) :]
+        more, refs = refs[: len(extra)], refs[len(extra) + len(early) :]
         outs, refs = refs[: len(out_shape)], refs[len(out_shape) :]
-        acc, held, strips, sem, strip_sem, more_sem = refs[:6]
-        kept_more = refs[6:]
+        acc, held, strips, left, sem, strip_sem, more_sem = refs[:7]
+        kept_more = refs[7:]
         by = scale_ref[0, 0]
 
         def fetch(k, j, first, t):
@@ -77,7 +100,7 @@
             return pltpu.make_async_copy(source, spot, sem.at[j, first + t])
 
         def fetch_strip(j):
-            source = panel_ref.at[pl.ds(2 * index_ref[j], 2)]
+            source = panel_ref.at[pl.ds(2 * index_ref[base + j], 2)]
             return pltpu.make_async_copy(source, strips.at[j], strip_sem.at[j])
 
         def fetch_more(k):
@@ -100,7 +123,6 @@
                 for t in range(2):
                     held[j, t * WIDE + TALL : (t + 1) * WIDE] = gap
 
-        kept = jnp.dot(tall_ref[...], wide_ref[index_ref[step]], preferred_element_type=F32)
         for j in range(count):
 
             @pl.when(step == j)
@@ -110,12 +132,11 @@
                     if one[1] == j:
                         fetch(*one).wait()
 
-        left = jnp.concatenate([strips[step, 0], strips[step, 1]], axis=1)
-        left = (left.astype(F32) * (kept * by)).astype(BF)
+        mask_rows(strips, step, wide_ref, index_ref[base + step], left)
         right = held[step]
         if scaled:
             right = (right.astype(F32) * by).astype(BF)
-        acc[...] += jnp.dot(left, right, preferred_element_type=F32)
+        acc[...] += jnp.dot(left[...], right, preferred_element_type=F32)
 
         @pl.when(step == count - 1)
         def _():
@@ -126,17 +147,18 @@
     whole = pl.BlockSpec(memory_space=pltpu.VMEM)
     smem = pl.BlockSpec(memory_space=pltpu.SMEM)
     anywhere = pl.BlockSpec(memory_space=pltpu.HBM)
-    operands = [piece for _, piece in flat] + extra
+    operands = [piece for _, piece in flat] + extra + list(early)
     return pl.pallas_call(
         body,
         out_shape=out_shape,
         grid=(count,),
-        in_specs=[smem, smem, anywhere, whole, whole] + [anywhere] * len(operands),
+        in_specs=[smem, smem, anywhere, whole] + [anywhere] * len(operands),
         out_specs=[whole] * len(out_shape),
         scratch_shapes=[
             pltpu.VMEM((rows, WIDE), F32),
             pltpu.VMEM((count, 2 * WIDE, WIDE), BF),
             pltpu.VMEM((count, 2, rows, WIDE), BF),
+            pltpu.VMEM((rows, 2 * WIDE), BF),
             pltpu.SemaphoreType.DMA((count, 2)),
             pltpu.SemaphoreType.DMA((count,)),
             pltpu.SemaphoreType.DMA((max(len(extra), 1),)),
@@ -146,7 +168,7 @@
         cost_estimate=pl.CostEstimate(
             flops=int(micros * 1.15e9), bytes_accessed=int(micros * 3e6), transcendentals=0
         ),
-    )(index, scale, panel, tall, wide, *operands)
+    )(index, scale, panel, wide, *operands)
 
 
 def square_end(acc, by, outs, keep):
@@ -184,15 +206,14 @@
     return lax.ppermute(array, axis, shift(2 if axis == "c" else 4, by))
 
 
-def around(array, axis):
-    return [array] + [send(array, axis, by) for by in (1, 2, 3)]
+def from_all(array, axes, count):
+    return lax.all_to_all(jnp.broadcast_to(array[None], (count,) + array.shape), axes, 0, 0)
 
 
 def column_panel(block, beside=None):
     before, behind = send(block, "x", 1), send(block, "x", 3)
     opposite = [send(before[:TALL], "x", 1), send(behind[TALL:], "x", 3)]
-    near = [(block,), (before,), (behind,)]
-    near = near + [(send(one, "c", 1),) for one, in near]
+    near = [(one,) for first in (block, before, behind) for one in (first, send(first, "c", 1))]
     partial = None
     if beside is not None:
         partial = beside(near)
@@ -232,13 +253,9 @@
     place = eq(np.arange(col_count * width)[:, None], spot[None, :])
     moved = exact(arrived, place, (((0,), (0,)), ((), ())))
 
-    own = pattern.astype(BF)
-    strip = jnp.stack(around(jnp.stack([own, send(own, "c", 1)]), "x"))
-    strip = strip.reshape(-1, atoms_col)
-    rows_seen = jnp.stack([2 * jnp.mod(x - d, 4) + jnp.mod(c + o, 2) for d in range(4) for o in range(2)])
-    atoms_seen = new_atom.reshape(row_count, atoms_row)[rows_seen].reshape(-1)
+    strip = from_all(pattern.astype(BF), ROW, row_count).reshape(-1, atoms_col)
     old_row = row_here * atoms_row + np.arange(atoms_row)
-    rows_pattern = exact(eq(old_row[:, None], atoms_seen[None, :]), strip)
+    rows_pattern = exact(eq(old_row[:, None], new_atom[None, :]), strip)
     line = np.arange(2 * TALL) % TALL
     of_row = np.where(line < half, (np.arange(2 * TALL) // TALL * half + line) // NBF, -1)
     of_col = np.where(np.arange(WIDE) < cols_here, np.arange(WIDE) // NBF, -1)
@@ -248,48 +265,40 @@
     right = moved * keep
     near, far, _ = column_panel(right)
 
-    part_sum = jnp.sum(jnp.square(right[TALL:].astype(F32)))
-    part_sum += jnp.sum(jnp.square(near[1][0][:TALL].astype(F32)))
+    part_sum = jnp.sum(jnp.square(right.astype(F32)))
     sent = jnp.concatenate(
         [rows_pattern.astype(F32), jnp.broadcast_to(part_sum, (8, atoms_col))], axis=0
     )
-    seen = jnp.stack(around(jnp.stack(around(sent, "z")), "y"))
-    seen = seen.reshape(col_count, atoms_row + 8, atoms_col)
+    seen = from_all(sent, COL, col_count)
     total = jnp.broadcast_to(jnp.sum(seen[:, atoms_row, 0]), (8, 128))
-    total = total + send(total, "c", 1)
-    total = sum(around(total, "x"))
+    total = jnp.sum(from_all(total, ROW, row_count), axis=0)
     scale = lax.rsqrt(total[:1, :1] / order_all)
-    cols_seen = jnp.stack([4 * jnp.mod(y - a, 4) + jnp.mod(z - b, 4) for a in range(4) for b in range(4)])
-    atoms_seen = new_atom.reshape(col_count, atoms_col)[cols_seen].reshape(-1)
     all_cols = jnp.transpose(seen[:, :atoms_row], (1, 0, 2)).reshape(atoms_row, -1).astype(BF)
-    all_cols = jnp.pad(all_cols, ((0, 64 - atoms_row), (0, 0)))
     old_col = np.where(of_col >= 0, np.arange(col_count)[:, None] * atoms_col + of_col, -1)
     old_col = jnp.asarray(old_col.reshape(row_count, 1, 2 * WIDE))
-    wide = jnp.einsum(
-        "ia,ran->rin", all_cols, eq(atoms_seen[None, :, None], old_col), preferred_element_type=F32
-    ).astype(BF)
+    wide = scale * jnp.einsum(
+        "ia,ran->rin", all_cols, eq(new_atom[None, :, None], old_col), preferred_element_type=F32
+    )
 
     def rho(step, other_core):
         return 2 * jnp.mod(x + step, 4) + jnp.mod(c + other_core, 2)
 
-    near_index = jnp.stack([rho(d, o) for o in range(2) for d in (0, -1, 1)])
-    far_index = jnp.stack([rho(2, o) for o in range(2)])
+    index = jnp.stack([rho(d, o) for d in (0, -1, 1, 2) for o in range(2)])
     sums = jax.ShapeDtypeStruct((2 * TALL, WIDE), F32)
     whole = pl.BlockSpec(memory_space=pltpu.VMEM)
-    of_panel = functools.partial(multiply, panel, tall, wide, scale)
-    all_index = jnp.concatenate([near_index, far_index])
-    block = jax.ShapeDtypeStruct((2 * TALL, WIDE), BF)
-    square = of_panel(all_index, near + far, True, square_end, [keep], [block], 9)[0]
-    _, far, partial = column_panel(
-        square, lambda near: of_panel(near_index, near, False, first_sum, [], [sums], 11)[0]
-    )
+    of_panel = functools.partial(multiply, panel, wide, scale, index)
     base = packed(new_atom, row_here, atoms_row, row_count, slots_row)
     line = (base[:, :, None] * NBF + np.arange(NBF)).reshape(-1)
     row_of = np.where(of_row >= 0, np.arange(2 * TALL) - (np.arange(2 * TALL) // TALL) * (TALL - half), -1)
     pack_rows = eq(line[:, None], jnp.asarray(row_of)[None, :])
+    block = jax.ShapeDtypeStruct((2 * TALL, WIDE), BF)
+    square = of_panel(0, near + far, True, square_end, [keep], [block], 9, [pack_rows])[0]
+    _, far, partial = column_panel(
+        square, lambda near: of_panel(0, near, False, first_sum, [], [sums], 11)[0]
+    )
     sent_rows = of_panel(
-        far_index, far, False, sign_end, [partial, keep, right, pack_rows],
-        [jax.ShapeDtypeStruct((row_count * slots_row * NBF, WIDE), BF)], 4,
+        6, far, False, sign_end, [partial, keep, right, pack_rows],
+        [jax.ShapeDtypeStruct((row_count * slots_row * NBF, WIDE), BF)], 7,
     )[0]
     got_rows = lax.all_to_all(sent_rows.reshape(row_count, slots_row * NBF, WIDE), ROW, 0, 0)
     got_rows = got_rows.reshape(-1, WIDE)

time: 183 us -> 176 us (0.962)
  waiting for transfers between devices: 46.4 us -> 54.6 us
  starting transfers between devices: 53.6 us -> 46.2 us
  Pallas kernels: 35.9 us -> 31 us
  other arithmetic: 11.6 us -> 8.01 us
    ppermute x32 -> x18, starting transfers between devices: 41.6 us -> 20.3 us  [send(): return lax.ppermute(array, axis, shift(2 if axis == 'c' else 4, by))]
    all_to_all x0 -> x3, starting transfers between devices: none -> 14.2 us  [from_all(): lax.all_to_all(jnp.broadcast_to(array[None], (count,) + array.shape), axe...]
    ppermute x32 -> x18, waiting for transfers between devices: 30.1 us -> 16 us  [send(): return lax.ppermute(array, axis, shift(2 if axis == 'c' else 4, by))]
    all_gather x1, waiting for transfers between devices: 0.02 us -> 10 us  [on_device(): panel = lax.all_gather(padded, COL, axis=0)]
    all_to_all x1, waiting for transfers between devices: 7.23 us -> 15.3 us  [on_device(): lax.all_to_all(outgoing.reshape(col_count, width, 2 * TALL), COL, 0, 0)]
    pallas_call x3, Pallas kernels: 32.6 us -> 27.7 us  [multiply(): pl.pallas_call(body, out_shape=out_shape, grid=(count,), in_specs=[smem,...]
    all_to_all x0 -> x3, waiting for transfers between devices: none -> 4.15 us  [from_all(): lax.all_to_all(jnp.broadcast_to(array[None], (count,) + array.shape), axe...]
    unnamed x54 -> x60, local copies, waits for them, and re-layouts: 6.43 us -> 6.97 us
  transfers between devices with their start and end apart: 35 -> 24, of which waited for: 11 -> 8; matrix products, arithmetic and copies ran while one was open for 12% -> 12% of each run, Pallas kernels for 6% -> 5%
where the time goes in v2:
time: 176 us; the launch traced here: 175 us
  waiting for transfers between devices  54.6 us (31%)
  starting transfers between devices  46.2 us (26%)
  Pallas kernels  31 us (18%)
  local copies, waits for them, and re-layouts  14.6 us (8%)
  between operations  14.6 us (8%)
  other arithmetic  8.01 us (5%)
  matrix products  6.04 us (3%)
    pallas_call x3, Pallas kernels, multiply(): pl.pallas_call(body, out_shape=out_shape, grid=(count,), in_specs=[smem,...  27.7 us
    ppermute x18, starting transfers between devices, send(): return lax.ppermute(array, axis, shift(2 if axis == 'c' else 4, by))  20.3 us
    ppermute x18, waiting for transfers between devices, send(): return lax.ppermute(array, axis, shift(2 if axis == 'c' else 4, by))  16 us
    all_to_all x1, waiting for transfers between devices, on_device(): lax.all_to_all(outgoing.reshape(col_count, width, 2 * TALL), COL, 0, 0)  15.3 us
    all_to_all x3, starting transfers between devices, from_all(): lax.all_to_all(jnp.broadcast_to(array[None], (count,) + array.shape), axe...  14.2 us
    all_gather x1, waiting for transfers between devices, on_device(): panel = lax.all_gather(padded, COL, axis=0)  10 us
    all_to_all x1, waiting for transfers between devices, on_device(): lax.all_to_all(sent_rows.reshape(row_count, slots_row * NBF, WIDE), ROW,...  9.07 us
    all_to_all x1, starting transfers between devices, on_device(): lax.all_to_all(outgoing.reshape(col_count, width, 2 * TALL), COL, 0, 0)  7.9 us
  transfers between devices with their start and end apart: 24, of which 8 were waited for; matrix products, arithmetic and copies ran while one was open for 12% of the time, Pallas kernels for 5%

profile of v2, /device:TPU:1, one launch (start us, length us, event | category | flops | bytes accessed | tf_op | source)
XLA Modules:
  0.0 175.1 jit_solution(9539142646504784242)
XLA Ops:
  6.5 1.1 fusion.35
  7.7 0.9 fusion.14
  8.6 0.7 reshape.319
  9.4 5.8 %all-to-all-start = ((bf16[8,2,784]{2,1,0:T(2,128)(2,1)}), bf16[8,2,784]{2,1,0:T(2,128)(2,1)S(1)}, u32[]{:S(2)}, u32[]{:S(2)}) async-start(bf16[8,2,784]{2,1,0:T(2,128)(2,1)} %reshape.319), calls=%async_computation | async-start | bytes 57344 | tf_op jit(solution)/shard_map/all_to_all | solution.py:210
  15.5 0.6 convert_reduce_fusion.1
  17.2 0.7 fusion.29
  18.0 0.7 convolution_convert_fusion
  18.7 1.2 copy.40
  19.9 7.9 %all-to-all-start.1 = ((bf16[16,32,736]{2,1,0:T(8,128)(2,1)}), bf16[16,32,736]{2,1,0:T(8,128)(2,1)S(1)}, u32[]{:S(2)}, u32[]{:S(2)}) async-start(bf16[16,32,736]{2,1,0:T(8,128)(2,1)} %bitcast.8), calls=%async_computation.1 | async-start | bytes 1572864 | tf_op jit(solution)/shard_map/all_to_all | solution.py:248
  28.0 0.3 convert_reduce_fusion
  28.3 0.2 select_reduce_fusion
  28.9 0.2 convolution_convert_fusion.4
  29.1 0.6 convolution_convert_fusion.2.refs_10_.refs_5_
  29.7 15.3 %all-to-all-done.1 = bf16[16,32,736]{2,1,0:T(8,128)(2,1)S(1)} async-done(((bf16[16,32,736]{2,1,0:T(8,128)(2,1)}), bf16[16,32,736]{2,1,0:T(8,128)(2,1)S(1)}, u32[]{:S(2)}, u32[]{:S(2)}) %all-to-all-start.1) | async-done | bytes 753696 | tf_op jit(solution)/shard_map/all_to_all | solution.py:248
  45.0 1.3 multiply_reduce_fusion
  46.3 1.3 collective-permute-start.1
  47.6 1.4 collective-permute-start.3
  49.2 0.7 concatenate.7
  49.9 0.8 reshape.321
  50.7 5.0 %all-to-all-start.2 = ((f32[16,1,1792]{2,1,0:T(1,128)}), f32[16,1,1792]{2,1,0:T(1,128)S(1)}, u32[]{:S(2)}, u32[]{:S(2)}) async-start(f32[16,1,1792]{2,1,0:T(1,128)} %reshape.321), calls=%async_computation.2 | async-start | bytes 229376 | tf_op jit(solution)/shard_map/all_to_all | solution.py:210
  55.8 3.2 %collective-permute-done.1.refs_2_ = bf16[736,384]{1,0:T(8,128)(2,1)S(1)} collective-permute-done((bf16[736,384]{1,0:T(8,128)(2,1)S(1)}, bf16[736,384]{1,0:T(8,128)(2,1)S(1)}, u32[]{:S(2)}, u32[]{:S(2)}) %collective-permute-start.1) | collective-permute-done | bytes 565280 | tf_op jit(solution)/shard_map/ppermute | solution.py:206
  59.1 0.2 collective-permute-start.5
  59.3 2.6 %collective-permute-start.6 = (bf16[368,384]{1,0:T(8,128)(2,1)S(1)}, bf16[368,384]{1,0:T(8,128)(2,1)}, u32[]{:S(2)}, u32[]{:S(2)}) collective-permute-start(bf16[368,384]{1,0:T(8,128)(2,1)S(1)} %slice.44), channel_id=1, source_target_pairs={{0,96},{32,0},{64,32},{96,64},{1,97},{33,1},{65,33},{97,65},{2,98}... | collective-permute-start | bytes 847880 | tf_op jit(solution)/shard_map/ppermute | solution.py:206
  61.9 1.3 compare_convert_fusion.refs_11_.refs_7_
  63.2 0.7 stack.35.index_ref
  63.9 4.3 %collective-permute-start = (bf16[736,384]{1,0:T(8,128)(2,1)S(1)}, bf16[736,384]{1,0:T(8,128)(2,1)S(1)}, u32[]{:S(2)}, u32[]{:S(2)}) collective-permute-start(bf16[736,384]{1,0:T(8,128)(2,1)S(1)} %get-tuple-element.22.refs_0_.refs_6_), channel_id=1, source_target_pairs={{0,16},{16,0},{1,17},{17,1},{2,18},{18,2},{3,19},{19,3},{4,20},{20... | collective-permute-start | bytes 1695752 | tf_op jit(solution)/shard_map/ppermute | solution.py:206
  68.2 0.5 broadcast.371
  68.7 0.9 reduce.3
  69.9 0.5 collective-permute-start.4
  70.4 0.7 slice_reduce_fusion
  71.1 1.2 broadcast_in_dim_broadcast_in_dim_broadcast_in_dim.3
  72.4 3.3 %all-to-all-start.3 = ((f32[8,8,128]{2,1,0:T(8,128)}), f32[8,8,128]{2,1,0:T(8,128)S(1)}, u32[]{:S(2)}, u32[]{:S(2)}) async-start(f32[8,8,128]{2,1,0:T(8,128)} %broadcast_in_dim_broadcast_in_dim_broadcast_in_dim.3), calls=%async_computation.3 | async-start | bytes 65536 | tf_op jit(solution)/shard_map/all_to_all | solution.py:210
  75.7 0.2 collective-permute-start.7
  75.9 0.4 collective-permute-start.8
  76.3 4.1 %all-to-all-done.3 = f32[8,8,128]{2,1,0:T(8,128)S(1)} async-done(((f32[8,8,128]{2,1,0:T(8,128)}), f32[8,8,128]{2,1,0:T(8,128)S(1)}, u32[]{:S(2)}, u32[]{:S(2)}) %all-to-all-start.3) | async-done | bytes 32800 | tf_op jit(solution)/shard_map/all_to_all | solution.py:210
  80.5 0.5 slice.35
  81.7 3.2 %fusion.8.wide_ref = f32[8,56,768]{2,1,0:T(8,128)} fusion(s32[8,768]{1,0:T(8,128)S(1)} %copy-done.26, s32[448]{0:T(512)S(1)} %copy-done.10, f32[]{:T(128)} %bitcast.11, bf16[56,448]{0,1:T(8,128)(2,1)S(1)} %convert_element_type.71), kind=kOutput, calls=%fused_computation.8 | convolution fusion | flops 311377920 | bytes 1452804 | tf_op jit(solution)/shard_map/ia,ran->rin/dot_general | solution.py:279
  85.0 10.0 %all-gather.3.cloned.1.call-done = bf16[11776,384]{1,0:T(8,128)(2,1)} async-done(((bf16[736,384]{1,0:T(8,128)(2,1)}), bf16[11776,384]{1,0:T(8,128)(2,1)}) %all-gather.3.cloned.1.call-update) | async-done | bytes 9043984 | tf_op jit(solution)/shard_map/all_gather | solution.py:240
  95.1 11.2 %shard_map.217.refs_0_ = bf16[736,384]{1,0:T(8,128)(2,1)} custom-call(s32[8]{0:T(128)} %stack.35.index_ref, f32[1,1]{1,0:T(1,128)} %rsqrt.3.scale_ref, bf16[16,736,384]{2,1,0:T(8,128)(2,1)} %bitcast.40, f32[8,56,768]{2,1,0:T(8,128)} %fusion.8.wide_ref, bf16[736,384]{1,0:T(8,128)(2,1)} %copy-done.17, bf16[736,384]{1,0:T(8,128)(2,1)} %copy-done.18, ...), custom_call_target="tpu_custom_call" | custom-call | flops 10350000128 | bytes 27000000 | tf_op jit(solution)/shard_map/pallas_call | solution.py:151
  106.3 1.3 collective-permute-start.10
  107.5 1.5 collective-permute-start.12
  109.0 1.2 collective-permute-start.9
  110.2 11.2 %collective-permute-done.10.refs_2_ = bf16[736,384]{1,0:T(8,128)(2,1)S(1)} collective-permute-done((bf16[736,384]{1,0:T(8,128)(2,1)}, bf16[736,384]{1,0:T(8,128)(2,1)S(1)}, u32[]{:S(2)}, u32[]{:S(2)}) %collective-permute-start.10) | collective-permute-done | bytes 565280 | tf_op jit(solution)/shard_map/ppermute | solution.py:206
  121.4 1.5 collective-permute-start.11
  123.1 1.1 collective-permute-start.14
  124.3 1.7 collective-permute-start.15
  126.0 0.8 copy-done.19
  126.8 0.2 copy-done.20
  127.0 0.8 copy-done.21
  127.8 9.5 %shard_map.218.refs_0_.refs_4_ = f32[736,384]{1,0:T(8,128)} custom-call(s32[8]{0:T(128)} %stack.35.index_ref, f32[1,1]{1,0:T(1,128)} %rsqrt.3.scale_ref, bf16[16,736,384]{2,1,0:T(8,128)(2,1)} %bitcast.41, f32[8,56,768]{2,1,0:T(8,128)} %fusion.8.wide_ref, bf16[736,384]{1,0:T(8,128)(2,1)} %shard_map.217.refs_0_, bf16[736,384]{1,0:T(8,128)(2,1)} %copy-done.19, ...), custom_call_target="tpu_custom_call" | custom-call | flops 12650000384 | bytes 33000000 | tf_op jit(solution)/shard_map/pallas_call | solution.py:151
  137.3 0.7 copy-done.2
  138.0 0.7 copy-done.3
  138.7 1.0 collective-permute-start.16
  139.8 0.2 convert_reduce_fusion.2
  140.0 1.1 collective-permute-done.16.refs_2_
  141.1 0.4 collective-permute-done.17.refs_3_
  141.5 0.3 copy-done.24
  141.8 0.7 copy-done.25
  142.5 7.0 %shard_map.220 = bf16[832,384]{1,0:T(8,128)(2,1)} custom-call(s32[8]{0:T(128)} %stack.35.index_ref, f32[1,1]{1,0:T(1,128)} %rsqrt.3.scale_ref, bf16[16,736,384]{2,1,0:T(8,128)(2,1)} %bitcast.42, f32[8,56,768]{2,1,0:T(8,128)} %fusion.8.wide_ref, bf16[368,384]{1,0:T(8,128)(2,1)} %get-tuple-element.7.refs_0_, bf16[368,384]{1,0:T(8,128)(2,1)} %get-tuple-element.8.refs_1_, ...), custom_call_target="tpu_custom_call" | custom-call | flops 8049999872 | bytes 21000000 | tf_op jit(solution)/shard_map/pallas_call | solution.py:151
  149.5 3.8 %all-to-all-start.4 = ((bf16[8,104,384]{2,1,0:T(8,128)(2,1)}), bf16[8,104,384]{2,1,0:T(8,128)(2,1)S(1)}, u32[]{:S(2)}, u32[]{:S(2)}) async-start(bf16[8,104,384]{2,1,0:T(8,128)(2,1)} %bitcast.36), calls=%async_computation.4 | async-start | bytes 1277952 | tf_op jit(solution)/shard_map/all_to_all | solution.py:303
  153.7 1.4 fusion.4.place_ref
  155.0 9.1 %all-to-all-done.4 = bf16[8,104,384]{2,1,0:T(8,128)(2,1)S(1)} async-done(((bf16[8,104,384]{2,1,0:T(8,128)(2,1)}), bf16[8,104,384]{2,1,0:T(8,128)(2,1)S(1)}, u32[]{:S(2)}, u32[]{:S(2)}) %all-to-all-start.4) | async-done | bytes 639008 | tf_op jit(solution)/shard_map/all_to_all | solution.py:303
  164.1 0.8 copy-done
  164.9 3.3 %shard_map.221 = f32[728,364]{1,0:T(8,128)} custom-call(bf16[728,832]{1,0:T(8,128)(2,1)} %fusion.4.place_ref, bf16[832,384]{1,0:T(8,128)(2,1)} %bitcast.34), custom_call_target="tpu_custom_call" | custom-call | tf_op jit(solution)/shard_map/pallas_call | solution.py:308
  (117 shorter events, 3.2 us)
Async XLA Ops:
  6.5 2.1 %copy-start.8 = (s32[56,28]{0,1:T(8,128)S(1)}, s32[56,28]{0,1:T(8,128)}, u32[]{:S(2)}) copy-start(s32[56,28]{0,1:T(8,128)} %param.25) | copy-start | bytes 18820
  6.5 8.6 %copy-start.10 = (s32[448]{0:T(512)S(1)}, s32[448]{0:T(512)}, u32[]{:S(2)}) copy-start(s32[448]{0:T(512)} %param.24) | copy-start | bytes 5380
  6.5 88.5 %all-gather.3.cloned.1.call-start = ((), (), s32[]{:S(2)}) async-start(), calls=%async_computation.5 | async-start | bytes 9609216 | tf_op jit(solution)/shard_map/all_gather | solution.py:240
  7.7 7.8 %copy-start.15 = (pred[28,28]{1,0:T(8,128)(4,1)S(1)}, pred[28,28]{1,0:T(8,128)(4,1)}, u32[]{:S(2)}) copy-start(pred[28,28]{1,0:T(8,128)(4,1)} %constant.191) | copy-start | bytes 2356
  7.7 9.5 %copy-start.9 = (pred[1,28,28]{2,0,1:T(4,128)(4,1)S(1)}, pred[1,28,28]{2,0,1:T(4,128)(4,1)}, u32[]{:S(2)}) copy-start(pred[1,28,28]{2,0,1:T(4,128)(4,1)} %constant.164.clone) | copy-start | bytes 2356
  9.4 10.5 %all-to-all-start = ((bf16[8,2,784]{2,1,0:T(2,128)(2,1)}), bf16[8,2,784]{2,1,0:T(2,128)(2,1)S(1)}, u32[]{:S(2)}, u32[]{:S(2)}) async-start(bf16[8,2,784]{2,1,0:T(2,128)(2,1)} %reshape.319), calls=%async_computation | async-start | bytes 57344 | tf_op jit(solution)/shard_map/all_to_all | solution.py:210
  18.7 9.3 %copy-start.12 = (pred[56,56]{1,0:T(8,128)(4,1)S(1)}, pred[56,56]{1,0:T(8,128)(4,1)}, u32[]{:S(2)}) copy-start(pred[56,56]{1,0:T(8,128)(4,1)} %constant.199) | copy-start | bytes 9412
  19.9 9.2 %copy-start.14 = (s32[736]{0:T(1024)S(1)}, s32[736]{0:T(1024)}, u32[]{:S(2)}) copy-start(s32[736]{0:T(1024)} %constant.169.clone) | copy-start | bytes 8836
  19.9 9.2 %copy-start.16 = (s32[384]{0:T(512)S(1)}, s32[384]{0:T(512)}, u32[]{:S(2)}) copy-start(s32[384]{0:T(512)} %constant.171.clone) | copy-start | bytes 4612
  19.9 25.1 %all-to-all-start.1 = ((bf16[16,32,736]{2,1,0:T(8,128)(2,1)}), bf16[16,32,736]{2,1,0:T(8,128)(2,1)S(1)}, u32[]{:S(2)}, u32[]{:S(2)}) async-start(bf16[16,32,736]{2,1,0:T(8,128)(2,1)} %bitcast.8), calls=%async_computation.1 | async-start | bytes 1572864 | tf_op jit(solution)/shard_map/all_to_all | solution.py:248
  29.7 16.6 %copy-start.1 = (bf16[736,384]{1,0:T(8,128)(2,1)}, bf16[736,384]{1,0:T(8,128)(2,1)S(1)}, u32[]{:S(2)}) copy-start(bf16[736,384]{1,0:T(8,128)(2,1)S(1)} %convolution_convert_fusion.2.refs_10_.refs_5_) | copy-start | bytes 1695748
  46.3 17.6 %copy-start.17 = (bf16[736,384]{1,0:T(8,128)(2,1)}, bf16[736,384]{1,0:T(8,128)(2,1)S(1)}, u32[]{:S(2)}) copy-start(bf16[736,384]{1,0:T(8,128)(2,1)S(1)} %get-tuple-element.22.refs_0_.refs_6_) | copy-start | bytes 1695748
  46.3 15.6 %copy-start.13 = (s32[736]{0:T(1024)S(1)}, s32[736]{0:T(1024)}, u32[]{:S(2)}) copy-start(s32[736]{0:T(1024)} %constant.176.clone) | copy-start | bytes 8836
  46.3 12.7 %collective-permute-start.1 = (bf16[736,384]{1,0:T(8,128)(2,1)S(1)}, bf16[736,384]{1,0:T(8,128)(2,1)S(1)}, u32[]{:S(2)}, u32[]{:S(2)}) collective-permute-start(bf16[736,384]{1,0:T(8,128)(2,1)S(1)} %get-tuple-element.22.refs_0_.refs_6_), channel_id=1, source_target_pairs={{0,32},{32,64},{64,96},{96,0},{1,33},{33,65},{65,97},{97,1},{2,34}... | collective-permute-start | bytes 1695752 | tf_op jit(solution)/shard_map/ppermute | solution.py:206
  47.6 11.6 %collective-permute-start.3 = (bf16[736,384]{1,0:T(8,128)(2,1)S(1)}, bf16[736,384]{1,0:T(8,128)(2,1)S(1)}, u32[]{:S(2)}, u32[]{:S(2)}) collective-permute-start(bf16[736,384]{1,0:T(8,128)(2,1)S(1)} %get-tuple-element.22.refs_0_.refs_6_), channel_id=1, source_target_pairs={{0,96},{32,0},{64,32},{96,64},{1,97},{33,1},{65,33},{97,65},{2,98}... | collective-permute-start | bytes 1695752 | tf_op jit(solution)/shard_map/ppermute | solution.py:206
  50.7 17.5 %all-to-all-start.2 = ((f32[16,1,1792]{2,1,0:T(1,128)}), f32[16,1,1792]{2,1,0:T(1,128)S(1)}, u32[]{:S(2)}, u32[]{:S(2)}) async-start(f32[16,1,1792]{2,1,0:T(1,128)} %reshape.321), calls=%async_computation.2 | async-start | bytes 229376 | tf_op jit(solution)/shard_map/all_to_all | solution.py:210
  59.0 10.7 %copy-start.4 = (bf16[736,384]{1,0:T(8,128)(2,1)}, bf16[736,384]{1,0:T(8,128)(2,1)S(1)}, u32[]{:S(2)}) copy-start(bf16[736,384]{1,0:T(8,128)(2,1)S(1)} %collective-permute-done.1.refs_2_) | copy-start | bytes 1695748
  59.1 16.7 %collective-permute-start.5 = (bf16[368,384]{1,0:T(8,128)(2,1)S(1)}, bf16[368,384]{1,0:T(8,128)(2,1)}, u32[]{:S(2)}, u32[]{:S(2)}) collective-permute-start(bf16[368,384]{1,0:T(8,128)(2,1)S(1)} %slice.43), channel_id=1, source_target_pairs={{0,32},{32,64},{64,96},{96,0},{1,33},{33,65},{65,97},{97,1},{2,34}... | collective-permute-start | bytes 847880 | tf_op jit(solution)/shard_map/ppermute | solution.py:206
  59.2 10.6 %copy-start.5 = (bf16[736,384]{1,0:T(8,128)(2,1)}, bf16[736,384]{1,0:T(8,128)(2,1)S(1)}, u32[]{:S(2)}) copy-start(bf16[736,384]{1,0:T(8,128)(2,1)S(1)} %collective-permute-done.3.refs_4_) | copy-start | bytes 1695748
  59.3 22.4 %copy-start.26 = (s32[8,768]{1,0:T(8,128)S(1)}, s32[8,768]{1,0:T(8,128)}, u32[]{:S(2)}) copy-start(s32[8,768]{1,0:T(8,128)} %constant.198) | copy-start | bytes 73732
  59.3 16.6 %collective-permute-start.6 = (bf16[368,384]{1,0:T(8,128)(2,1)S(1)}, bf16[368,384]{1,0:T(8,128)(2,1)}, u32[]{:S(2)}, u32[]{:S(2)}) collective-permute-start(bf16[368,384]{1,0:T(8,128)(2,1)S(1)} %slice.44), channel_id=1, source_target_pairs={{0,96},{32,0},{64,32},{96,64},{1,97},{33,1},{65,33},{97,65},{2,98}... | collective-permute-start | bytes 847880 | tf_op jit(solution)/shard_map/ppermute | solution.py:206
  63.9 21.0 %collective-permute-start = (bf16[736,384]{1,0:T(8,128)(2,1)S(1)}, bf16[736,384]{1,0:T(8,128)(2,1)S(1)}, u32[]{:S(2)}, u32[]{:S(2)}) collective-permute-start(bf16[736,384]{1,0:T(8,128)(2,1)S(1)} %get-tuple-element.22.refs_0_.refs_6_), channel_id=1, source_target_pairs={{0,16},{16,0},{1,17},{17,1},{2,18},{18,2},{3,19},{19,3},{4,20},{20... | collective-permute-start | bytes 1695752 | tf_op jit(solution)/shard_map/ppermute | solution.py:206
  69.8 15.2 %collective-permute-start.2 = (bf16[736,384]{1,0:T(8,128)(2,1)S(1)}, bf16[736,384]{1,0:T(8,128)(2,1)}, u32[]{:S(2)}, u32[]{:S(2)}) collective-permute-start(bf16[736,384]{1,0:T(8,128)(2,1)S(1)} %collective-permute-done.1.refs_2_), channel_id=1, source_target_pairs={{0,16},{16,0},{1,17},{17,1},{2,18},{18,2},{3,19},{19,3},{4,20},{20... | collective-permute-start | bytes 1695752 | tf_op jit(solution)/shard_map/ppermute | solution.py:206
  69.9 15.1 %collective-permute-start.4 = (bf16[736,384]{1,0:T(8,128)(2,1)S(1)}, bf16[736,384]{1,0:T(8,128)(2,1)}, u32[]{:S(2)}, u32[]{:S(2)}) collective-permute-start(bf16[736,384]{1,0:T(8,128)(2,1)S(1)} %collective-permute-done.3.refs_4_), channel_id=1, source_target_pairs={{0,16},{16,0},{1,17},{17,1},{2,18},{18,2},{3,19},{19,3},{4,20},{20... | collective-permute-start | bytes 1695752 | tf_op jit(solution)/shard_map/ppermute | solution.py:206
  72.4 8.1 %all-to-all-start.3 = ((f32[8,8,128]{2,1,0:T(8,128)}), f32[8,8,128]{2,1,0:T(8,128)S(1)}, u32[]{:S(2)}, u32[]{:S(2)}) async-start(f32[8,8,128]{2,1,0:T(8,128)} %broadcast_in_dim_broadcast_in_dim_broadcast_in_dim.3), calls=%async_computation.3 | async-start | bytes 65536 | tf_op jit(solution)/shard_map/all_to_all | solution.py:210
  75.7 9.3 %collective-permute-start.7 = (bf16[368,384]{1,0:T(8,128)(2,1)}, bf16[368,384]{1,0:T(8,128)(2,1)S(1)}, u32[]{:S(2)}, u32[]{:S(2)}) collective-permute-start(bf16[368,384]{1,0:T(8,128)(2,1)} %collective-permute-done.5.refs_6_), channel_id=1, source_target_pairs={{0,16},{16,0},{1,17},{17,1},{2,18},{18,2},{3,19},{19,3},{4,20},{20... | collective-permute-start | bytes 847880 | tf_op jit(solution)/shard_map/ppermute | solution.py:206
  75.9 9.1 %collective-permute-start.8 = (bf16[368,384]{1,0:T(8,128)(2,1)}, bf16[368,384]{1,0:T(8,128)(2,1)S(1)}, u32[]{:S(2)}, u32[]{:S(2)}) collective-permute-start(bf16[368,384]{1,0:T(8,128)(2,1)} %collective-permute-done.6.refs_7_), channel_id=1, source_target_pairs={{0,16},{16,0},{1,17},{17,1},{2,18},{18,2},{3,19},{19,3},{4,20},{20... | collective-permute-start | bytes 847880 | tf_op jit(solution)/shard_map/ppermute | solution.py:206
  85.0 10.1 %copy-start.18 = (bf16[736,384]{1,0:T(8,128)(2,1)}, bf16[736,384]{1,0:T(8,128)(2,1)S(1)}, u32[]{:S(2)}) copy-start(bf16[736,384]{1,0:T(8,128)(2,1)S(1)} %collective-permute-done.refs_1_) | copy-start | bytes 1695748
  85.0 10.1 %copy-start.22 = (bf16[368,384]{1,0:T(8,128)(2,1)}, bf16[368,384]{1,0:T(8,128)(2,1)S(1)}, u32[]{:S(2)}) copy-start(bf16[368,384]{1,0:T(8,128)(2,1)S(1)} %collective-permute-done.7.refs_8_) | copy-start | bytes 847876
  85.0 10.1 %copy-start.23 = (bf16[368,384]{1,0:T(8,128)(2,1)}, bf16[368,384]{1,0:T(8,128)(2,1)S(1)}, u32[]{:S(2)}) copy-start(bf16[368,384]{1,0:T(8,128)(2,1)S(1)} %collective-permute-done.8.refs_9_) | copy-start | bytes 847876
  106.3 15.2 %collective-permute-start.10 = (bf16[736,384]{1,0:T(8,128)(2,1)}, bf16[736,384]{1,0:T(8,128)(2,1)S(1)}, u32[]{:S(2)}, u32[]{:S(2)}) collective-permute-start(bf16[736,384]{1,0:T(8,128)(2,1)} %shard_map.217.refs_0_), channel_id=1, source_target_pairs={{0,32},{32,64},{64,96},{96,0},{1,33},{33,65},{65,97},{97,1},{2,34}... | collective-permute-start | bytes 1695752 | tf_op jit(solution)/shard_map/ppermute | solution.py:206
  107.5 15.5 %collective-permute-start.12 = (bf16[736,384]{1,0:T(8,128)(2,1)}, bf16[736,384]{1,0:T(8,128)(2,1)S(1)}, u32[]{:S(2)}, u32[]{:S(2)}) collective-permute-start(bf16[736,384]{1,0:T(8,128)(2,1)} %shard_map.217.refs_0_), channel_id=1, source_target_pairs={{0,96},{32,0},{64,32},{96,64},{1,97},{33,1},{65,33},{97,65},{2,98}... | collective-permute-start | bytes 1695752 | tf_op jit(solution)/shard_map/ppermute | solution.py:206
  109.0 16.9 %collective-permute-start.9 = (bf16[736,384]{1,0:T(8,128)(2,1)}, bf16[736,384]{1,0:T(8,128)(2,1)S(1)}, u32[]{:S(2)}, u32[]{:S(2)}) collective-permute-start(bf16[736,384]{1,0:T(8,128)(2,1)} %shard_map.217.refs_0_), channel_id=1, source_target_pairs={{0,16},{16,0},{1,17},{17,1},{2,18},{18,2},{3,19},{19,3},{4,20},{20... | collective-permute-start | bytes 1695752 | tf_op jit(solution)/shard_map/ppermute | solution.py:206
  121.4 4.5 %copy-start.6 = (bf16[736,384]{1,0:T(8,128)(2,1)}, bf16[736,384]{1,0:T(8,128)(2,1)S(1)}, u32[]{:S(2)}) copy-start(bf16[736,384]{1,0:T(8,128)(2,1)S(1)} %collective-permute-done.10.refs_2_) | copy-start | bytes 1695748
  121.4 4.5 %collective-permute-start.11 = (bf16[736,384]{1,0:T(8,128)(2,1)S(1)}, bf16[736,384]{1,0:T(8,128)(2,1)S(1)}, u32[]{:S(2)}, u32[]{:S(2)}) collective-permute-start(bf16[736,384]{1,0:T(8,128)(2,1)S(1)} %collective-permute-done.10.refs_2_), channel_id=1, source_target_pairs={{0,16},{16,0},{1,17},{17,1},{2,18},{18,2},{3,19},{19,3},{4,20},{20... | collective-permute-start | bytes 1695752 | tf_op jit(solution)/shard_map/ppermute | solution.py:206
  123.0 3.0 %copy-start.7 = (bf16[736,384]{1,0:T(8,128)(2,1)}, bf16[736,384]{1,0:T(8,128)(2,1)S(1)}, u32[]{:S(2)}) copy-start(bf16[736,384]{1,0:T(8,128)(2,1)S(1)} %collective-permute-done.12.refs_4_) | copy-start | bytes 1695748
  123.0 3.0 %collective-permute-start.13 = (bf16[736,384]{1,0:T(8,128)(2,1)S(1)}, bf16[736,384]{1,0:T(8,128)(2,1)S(1)}, u32[]{:S(2)}, u32[]{:S(2)}) collective-permute-start(bf16[736,384]{1,0:T(8,128)(2,1)S(1)} %collective-permute-done.12.refs_4_), channel_id=1, source_target_pairs={{0,16},{16,0},{1,17},{17,1},{2,18},{18,2},{3,19},{19,3},{4,20},{20... | collective-permute-start | bytes 1695752 | tf_op jit(solution)/shard_map/ppermute | solution.py:206
  123.1 14.2 %collective-permute-start.14 = (bf16[368,384]{1,0:T(8,128)(2,1)S(1)}, bf16[368,384]{1,0:T(8,128)(2,1)S(1)}, u32[]{:S(2)}, u32[]{:S(2)}) collective-permute-start(bf16[368,384]{1,0:T(8,128)(2,1)S(1)} %slice.45), channel_id=1, source_target_pairs={{0,32},{32,64},{64,96},{96,0},{1,33},{33,65},{65,97},{97,1},{2,34}... | collective-permute-start | bytes 847880 | tf_op jit(solution)/shard_map/ppermute | solution.py:206
  124.3 13.0 %collective-permute-start.15 = (bf16[368,384]{1,0:T(8,128)(2,1)S(1)}, bf16[368,384]{1,0:T(8,128)(2,1)S(1)}, u32[]{:S(2)}, u32[]{:S(2)}) collective-permute-start(bf16[368,384]{1,0:T(8,128)(2,1)S(1)} %slice.46), channel_id=1, source_target_pairs={{0,96},{32,0},{64,32},{96,64},{1,97},{33,1},{65,33},{97,65},{2,98}... | collective-permute-start | bytes 847880 | tf_op jit(solution)/shard_map/ppermute | solution.py:206
  126.0 0.8 copy-start.19
  126.0 1.0 copy-start.20
  127.0 0.8 copy-start.21
  137.3 2.5 %copy-start.11 = (pred[1,56,56]{2,1,0:T(8,128)(4,1)S(1)}, pred[1,56,56]{2,1,0:T(8,128)(4,1)}, u32[]{:S(2)}) copy-start(pred[1,56,56]{2,1,0:T(8,128)(4,1)} %constant.174.clone) | copy-start | bytes 9412
  137.3 0.7 copy-start.2
  138.0 0.7 copy-start.3
  138.7 2.4 %collective-permute-start.16 = (bf16[368,384]{1,0:T(8,128)(2,1)}, bf16[368,384]{1,0:T(8,128)(2,1)S(1)}, u32[]{:S(2)}, u32[]{:S(2)}) collective-permute-start(bf16[368,384]{1,0:T(8,128)(2,1)} %get-tuple-element.7.refs_0_), channel_id=1, source_target_pairs={{0,16},{16,0},{1,17},{17,1},{2,18},{18,2},{3,19},{19,3},{4,20},{20... | collective-permute-start | bytes 847880 | tf_op jit(solution)/shard_map/ppermute | solution.py:206
  139.7 1.8 %collective-permute-start.17 = (bf16[368,384]{1,0:T(8,128)(2,1)}, bf16[368,384]{1,0:T(8,128)(2,1)S(1)}, u32[]{:S(2)}, u32[]{:S(2)}) collective-permute-start(bf16[368,384]{1,0:T(8,128)(2,1)} %get-tuple-element.8.refs_1_), channel_id=1, source_target_pairs={{0,16},{16,0},{1,17},{17,1},{2,18},{18,2},{3,19},{19,3},{4,20},{20... | collective-permute-start | bytes 847880 | tf_op jit(solution)/shard_map/ppermute | solution.py:206
  141.1 0.7 copy-start.24
  141.8 0.7 copy-start.25
  149.5 14.6 %all-to-all-start.4 = ((bf16[8,104,384]{2,1,0:T(8,128)(2,1)}), bf16[8,104,384]{2,1,0:T(8,128)(2,1)S(1)}, u32[]{:S(2)}, u32[]{:S(2)}) async-start(bf16[8,104,384]{2,1,0:T(8,128)(2,1)} %bitcast.36), calls=%async_computation.4 | async-start | bytes 1277952 | tf_op jit(solution)/shard_map/all_to_all | solution.py:303
  164.1 0.8 copy-start
Sparse Core Ops, SparseCore 0:
  9.5 85.4 all-gather.2

commit v3 on v2

--- a/solution.py
+++ b/solution.py
@@ -52,13 +52,13 @@
 WIDE = 384
 
 
-def mask_rows(strips, step, wide_ref, at, left):
-    columns = left.shape[1]
+def mask_rows(strips, wides, step, left, first_column):
+    columns = 2 * WIDE
     line = lax.broadcasted_iota(jnp.int32, (8, columns), 0)
-    in_half = wide_ref.shape[1] // 2
+    in_half = wides.shape[1] // 2
 
     def of_atom(half, atom):
-        return jnp.broadcast_to(wide_ref[at, pl.ds(half * in_half + atom, 1), :], (8, columns))
+        return jnp.broadcast_to(wides[step, pl.ds(half * in_half + atom, 1), :], (8, columns))
 
     for start in range(0, left.shape[0], 16):
         masks = []
@@ -72,7 +72,7 @@
             masks.append(mask)
         rows = pl.ds(start, 16)
         both = jnp.concatenate([strips[step, 0, rows], strips[step, 1, rows]], axis=1)
-        left[rows] = (both.astype(F32) * jnp.concatenate(masks, axis=0)).astype(BF)
+        left[rows, first_column : first_column + columns] = (both.astype(F32) * jnp.concatenate(masks, axis=0)).astype(BF)
 
 
 def multiply(panel, wide, scale, index, base, blocks, scaled, epilogue, extra, out_shape, micros, early=()):
@@ -90,8 +90,8 @@
         pieces, refs = refs[: len(flat)], refs[len(flat) :]
         more, refs = refs[: len(extra)], refs[len(extra) + len(early) :]
         outs, refs = refs[: len(out_shape)], refs[len(out_shape) :]
-        acc, held, strips, left, sem, strip_sem, more_sem = refs[:7]
-        kept_more = refs[7:]
+        acc, held, strips, wides, left, sem, strip_sem, more_sem = refs[:8]
+        kept_more = refs[8:]
         by = scale_ref[0, 0]
 
         def fetch(k, j, first, t):
@@ -101,7 +101,11 @@
 
         def fetch_strip(j):
             source = panel_ref.at[pl.ds(2 * index_ref[base + j], 2)]
-            return pltpu.make_async_copy(source, strips.at[j], strip_sem.at[j])
+            return pltpu.make_async_copy(source, strips.at[j], strip_sem.at[j, 0])
+
+        def fetch_wide(j):
+            source = wide_ref.at[index_ref[base + j]]
+            return pltpu.make_async_copy(source, wides.at[j], strip_sem.at[j, 1])
 
         def fetch_more(k):
             return pltpu.make_async_copy(more[k], kept_more[k], more_sem.at[k])
@@ -115,6 +119,7 @@
                     if one[1] == j:
                         fetch(*one).start()
                 fetch_strip(j).start()
+                fetch_wide(j).start()
             for k in range(len(extra)):
                 fetch_more(k).start()
             acc[...] = jnp.zeros_like(acc)
@@ -125,20 +130,22 @@
 
         for j in range(count):
 
-            @pl.when(step == j)
+            @pl.when(step == j // 2)
             def _(j=j):
                 fetch_strip(j).wait()
+                fetch_wide(j).wait()
                 for one in halves:
                     if one[1] == j:
                         fetch(*one).wait()
 
-        mask_rows(strips, step, wide_ref, index_ref[base + step], left)
-        right = held[step]
+        for t in range(2):
+            mask_rows(strips, wides, 2 * step + t, left, 2 * WIDE * t)
+        right = held[pl.ds(2 * step, 2)].reshape(4 * WIDE, WIDE)
         if scaled:
             right = (right.astype(F32) * by).astype(BF)
         acc[...] += jnp.dot(left[...], right, preferred_element_type=F32)
 
-        @pl.when(step == count - 1)
+        @pl.when(step == count // 2 - 1)
         def _():
             for k in range(len(extra)):
                 fetch_more(k).wait()
@@ -151,16 +158,17 @@
     return pl.pallas_call(
         body,
         out_shape=out_shape,
-        grid=(count,),
-        in_specs=[smem, smem, anywhere, whole] + [anywhere] * len(operands),
+        grid=(count // 2,),
+        in_specs=[smem, smem, anywhere, anywhere] + [anywhere] * len(operands),
         out_specs=[whole] * len(out_shape),
         scratch_shapes=[
             pltpu.VMEM((rows, WIDE), F32),
             pltpu.VMEM((count, 2 * WIDE, WIDE), BF),
             pltpu.VMEM((count, 2, rows, WIDE), BF),
-            pltpu.VMEM((rows, 2 * WIDE), BF),
+            pltpu.VMEM((count,) + wide.shape[1:], F32),
+            pltpu.VMEM((rows, 4 * WIDE), BF),
             pltpu.SemaphoreType.DMA((count, 2)),
-            pltpu.SemaphoreType.DMA((count,)),
+            pltpu.SemaphoreType.DMA((count, 2)),
             pltpu.SemaphoreType.DMA((max(len(extra), 1),)),
         ]
         + [pltpu.VMEM(e.shape, e.dtype) for e in extra],
@@ -172,7 +180,9 @@
 
 
 def square_end(acc, by, outs, keep):
-    outs[0][...] = (acc[...] * keep[...].astype(F32)).astype(BF)
+    for half in range(2):
+        rows = slice(half * TALL, (half + 1) * TALL)
+        outs[half][...] = (acc[rows] * keep[rows].astype(F32)).astype(BF)
 
 
 def first_sum(acc, by, outs):
@@ -210,16 +220,29 @@
     return lax.all_to_all(jnp.broadcast_to(array[None], (count,) + array.shape), axes, 0, 0)
 
 
-def column_panel(block, beside=None):
-    before, behind = send(block, "x", 1), send(block, "x", 3)
-    opposite = [send(before[:TALL], "x", 1), send(behind[TALL:], "x", 3)]
-    near = [(one,) for first in (block, before, behind) for one in (first, send(first, "c", 1))]
-    partial = None
-    if beside is not None:
-        partial = beside(near)
-        opposite = after(partial, opposite)
-    far = [tuple(opposite), tuple(send(half, "c", 1) for half in opposite)]
-    return near, far, partial
+PLACES = [(0, 0), (0, 1), (-1, 0), (1, 0), (-1, 1), (1, 1), (2, 0), (2, 1)]
+
+
+def other(pieces):
+    return tuple(send(piece, "c", 1) for piece in pieces)
+
+
+def column_panel(block):
+    before, behind = (send(block, "x", 1),), (send(block, "x", 3),)
+    opposite = (send(before[0][:TALL], "x", 1), send(behind[0][TALL:], "x", 3))
+    own = (block,)
+    return [own, other(own), before, behind, other(before), other(behind), opposite, other(opposite)]
+
+
+def column_panel_beside(top, bottom, beside):
+    before_top, behind_bottom = send(top, "x", 1), send(bottom, "x", 3)
+    before = (before_top, send(bottom, "x", 1))
+    behind = (send(top, "x", 3), behind_bottom)
+    opposite = [send(before_top, "x", 1), send(behind_bottom, "x", 3)]
+    own = (top, bottom)
+    partial = beside([own, other(own), before, behind])
+    opposite = (after(partial, opposite[:1])[0], opposite[1])
+    return [other(before), other(behind), opposite, other(opposite)], partial
 
 
 def on_device(hamiltonian, new_atom, pattern):
@@ -263,7 +286,7 @@
     broad = eq(np.arange(atoms_col)[:, None], jnp.asarray(of_col)[None, :])
     keep = exact(exact(tall[:, :atoms_row], rows_pattern), broad)
     right = moved * keep
-    near, far, _ = column_panel(right)
+    blocks = column_panel(right)
 
     part_sum = jnp.sum(jnp.square(right.astype(F32)))
     sent = jnp.concatenate(
@@ -283,7 +306,7 @@
     def rho(step, other_core):
         return 2 * jnp.mod(x + step, 4) + jnp.mod(c + other_core, 2)
 
-    index = jnp.stack([rho(d, o) for d in (0, -1, 1, 2) for o in range(2)])
+    index = jnp.stack([rho(d, o) for d, o in PLACES])
     sums = jax.ShapeDtypeStruct((2 * TALL, WIDE), F32)
     whole = pl.BlockSpec(memory_space=pltpu.VMEM)
     of_panel = functools.partial(multiply, panel, wide, scale, index)
@@ -291,14 +314,15 @@
     line = (base[:, :, None] * NBF + np.arange(NBF)).reshape(-1)
     row_of = np.where(of_row >= 0, np.arange(2 * TALL) - (np.arange(2 * TALL) // TALL) * (TALL - half), -1)
     pack_rows = eq(line[:, None], jnp.asarray(row_of)[None, :])
-    block = jax.ShapeDtypeStruct((2 * TALL, WIDE), BF)
-    square = of_panel(0, near + far, True, square_end, [keep], [block], 9, [pack_rows])[0]
-    _, far, partial = column_panel(
-        square, lambda near: of_panel(0, near, False, first_sum, [], [sums], 11)[0]
+    half_block = jax.ShapeDtypeStruct((TALL, WIDE), BF)
+    square = of_panel(0, blocks, True, square_end, [keep], [half_block] * 2, 9, [pack_rows])
+    blocks, partial = column_panel_beside(
+        *square,
+        lambda first: of_panel(0, first, False, first_sum, [], [sums], 7)[0],
     )
     sent_rows = of_panel(
-        6, far, False, sign_end, [partial, keep, right, pack_rows],
-        [jax.ShapeDtypeStruct((row_count * slots_row * NBF, WIDE), BF)], 7,
+        4, blocks, False, sign_end, [partial, keep, right, pack_rows],
+        [jax.ShapeDtypeStruct((row_count * slots_row * NBF, WIDE), BF)], 9,
     )[0]
     got_rows = lax.all_to_all(sent_rows.reshape(row_count, slots_row * NBF, WIDE), ROW, 0, 0)
     got_rows = got_rows.reshape(-1, WIDE)

time: 176 us -> 170 us (0.966)
  starting transfers between devices: 46.2 us -> 51.8 us
  waiting for transfers between devices: 54.6 us -> 49.6 us
  Pallas kernels: 31 us -> 27.2 us
  local copies, waits for them, and re-layouts: 14.6 us -> 12.6 us
    ppermute x18 -> x23, starting transfers between devices: 20.3 us -> 26.1 us  [send(): return lax.ppermute(array, axis, shift(2 if axis == 'c' else 4, by))]
    ppermute x18 -> x23, waiting for transfers between devices: 16 us -> 10.9 us  [send(): return lax.ppermute(array, axis, shift(2 if axis == 'c' else 4, by))]
    pallas_call x3, Pallas kernels: 27.7 us -> 23.9 us  [multiply(): pl.pallas_call(body, out_shape=out_shape, grid=(count // 2,), in_specs=[s...]
    unnamed x60 -> x70, local copies, waits for them, and re-layouts: 6.97 us -> 5.11 us
  transfers between devices with their start and end apart: 24 -> 29, of which waited for: 8 -> 10; matrix products, arithmetic and copies ran while one was open for 12% -> 13% of each run, Pallas kernels for 5% -> 4%
where the time goes in v3:
time: 170 us
  starting transfers between devices  51.8 us (30%)
  waiting for transfers between devices  49.6 us (29%)
  Pallas kernels  27.2 us (16%)
  between operations  14.6 us (9%)
  local copies, waits for them, and re-layouts  12.6 us (7%)
  other arithmetic  7.92 us (5%)
  matrix products  6.07 us (4%)
    ppermute x23, starting transfers between devices, send(): return lax.ppermute(array, axis, shift(2 if axis == 'c' else 4, by))  26.1 us
    pallas_call x3, Pallas kernels, multiply(): pl.pallas_call(body, out_shape=out_shape, grid=(count // 2,), in_specs=[s...  23.9 us
    all_to_all x1, waiting for transfers between devices, on_device(): lax.all_to_all(outgoing.reshape(col_count, width, 2 * TALL), COL, 0, 0)  15.3 us
    all_to_all x3, starting transfers between devices, from_all(): lax.all_to_all(jnp.broadcast_to(array[None], (count,) + array.shape), axe...  14.2 us
    ppermute x23, waiting for transfers between devices, send(): return lax.ppermute(array, axis, shift(2 if axis == 'c' else 4, by))  10.9 us
    all_gather x1, waiting for transfers between devices, on_device(): panel = lax.all_gather(padded, COL, axis=0)  10.2 us
    all_to_all x1, waiting for transfers between devices, on_device(): lax.all_to_all(sent_rows.reshape(row_count, slots_row * NBF, WIDE), ROW,...  9.05 us
    all_to_all x1, starting transfers between devices, on_device(): lax.all_to_all(outgoing.reshape(col_count, width, 2 * TALL), COL, 0, 0)  7.9 us
  transfers between devices with their start and end apart: 29, of which 10 were waited for; matrix products, arithmetic and copies ran while one was open for 13% of the time, Pallas kernels for 4%

profile of v3, /device:TPU:1, one launch (start us, length us, event | category | flops | bytes accessed | tf_op | source)
XLA Modules:
  0.0 169.8 jit_solution(13460695984700588025)
XLA Ops:
  6.5 1.1 fusion.35
  7.7 0.9 fusion.14
  8.6 0.7 reshape.319
  9.4 5.8 %all-to-all-start = ((bf16[8,2,784]{2,1,0:T(2,128)(2,1)}), bf16[8,2,784]{2,1,0:T(2,128)(2,1)S(1)}, u32[]{:S(2)}, u32[]{:S(2)}) async-start(bf16[8,2,784]{2,1,0:T(2,128)(2,1)} %reshape.319), calls=%async_computation | async-start | bytes 57344 | tf_op jit(solution)/shard_map/all_to_all | solution.py:220
  15.5 0.6 convert_reduce_fusion.1
  17.2 0.7 fusion.29
  18.0 0.7 convolution_convert_fusion
  18.7 1.2 copy.39
  19.9 7.9 %all-to-all-start.1 = ((bf16[16,32,736]{2,1,0:T(8,128)(2,1)}), bf16[16,32,736]{2,1,0:T(8,128)(2,1)S(1)}, u32[]{:S(2)}, u32[]{:S(2)}) async-start(bf16[16,32,736]{2,1,0:T(8,128)(2,1)} %bitcast.8), calls=%async_computation.1 | async-start | bytes 1572864 | tf_op jit(solution)/shard_map/all_to_all | solution.py:271
  28.0 0.3 convert_reduce_fusion
  28.3 0.2 select_reduce_fusion
  28.9 0.2 convolution_convert_fusion.4
  29.1 0.6 convolution_convert_fusion.2.refs_10_.refs_9_
  29.7 15.3 %all-to-all-done.1 = bf16[16,32,736]{2,1,0:T(8,128)(2,1)S(1)} async-done(((bf16[16,32,736]{2,1,0:T(8,128)(2,1)}), bf16[16,32,736]{2,1,0:T(8,128)(2,1)S(1)}, u32[]{:S(2)}, u32[]{:S(2)}) %all-to-all-start.1) | async-done | bytes 753696 | tf_op jit(solution)/shard_map/all_to_all | solution.py:271
  45.0 1.3 multiply_reduce_fusion
  46.3 1.3 collective-permute-start.1
  47.6 1.4 collective-permute-start.2
  49.2 0.7 concatenate.7
  49.9 0.8 reshape.321
  50.7 5.0 %all-to-all-start.2 = ((f32[16,1,1792]{2,1,0:T(1,128)}), f32[16,1,1792]{2,1,0:T(1,128)S(1)}, u32[]{:S(2)}, u32[]{:S(2)}) async-start(f32[16,1,1792]{2,1,0:T(1,128)} %reshape.321), calls=%async_computation.2 | async-start | bytes 229376 | tf_op jit(solution)/shard_map/all_to_all | solution.py:220
  55.8 3.3 %collective-permute-done.1.refs_2_ = bf16[736,384]{1,0:T(8,128)(2,1)S(1)} collective-permute-done((bf16[736,384]{1,0:T(8,128)(2,1)S(1)}, bf16[736,384]{1,0:T(8,128)(2,1)S(1)}, u32[]{:S(2)}, u32[]{:S(2)}) %collective-permute-start.1) | collective-permute-done | bytes 565280 | tf_op jit(solution)/shard_map/ppermute | solution.py:216
  59.3 2.7 %collective-permute-start.6 = (bf16[368,384]{1,0:T(8,128)(2,1)S(1)}, bf16[368,384]{1,0:T(8,128)(2,1)}, u32[]{:S(2)}, u32[]{:S(2)}) collective-permute-start(bf16[368,384]{1,0:T(8,128)(2,1)S(1)} %slice.36), channel_id=1, source_target_pairs={{0,96},{32,0},{64,32},{96,64},{1,97},{33,1},{65,33},{97,65},{2,98}... | collective-permute-start | bytes 847880 | tf_op jit(solution)/shard_map/ppermute | solution.py:216
  61.9 1.3 compare_convert_fusion.refs_11_
  63.3 0.7 stack.35.index_ref
  63.9 4.3 %collective-permute-start = (bf16[736,384]{1,0:T(8,128)(2,1)S(1)}, bf16[736,384]{1,0:T(8,128)(2,1)S(1)}, u32[]{:S(2)}, u32[]{:S(2)}) collective-permute-start(bf16[736,384]{1,0:T(8,128)(2,1)S(1)} %get-tuple-element.22.refs_0_.refs_10_), channel_id=1, source_target_pairs={{0,16},{16,0},{1,17},{17,1},{2,18},{18,2},{3,19},{19,3},{4,20},{20... | collective-permute-start | bytes 1695752 | tf_op jit(solution)/shard_map/ppermute | solution.py:216
  68.2 0.5 broadcast.371
  68.7 0.9 reduce.3
  69.9 0.5 collective-permute-start.4
  70.4 0.7 slice_reduce_fusion
  71.0 1.2 broadcast_in_dim_broadcast_in_dim_broadcast_in_dim.3
  72.2 3.3 %all-to-all-start.3 = ((f32[8,8,128]{2,1,0:T(8,128)}), f32[8,8,128]{2,1,0:T(8,128)S(1)}, u32[]{:S(2)}, u32[]{:S(2)}) async-start(f32[8,8,128]{2,1,0:T(8,128)} %broadcast_in_dim_broadcast_in_dim_broadcast_in_dim.3), calls=%async_computation.3 | async-start | bytes 65536 | tf_op jit(solution)/shard_map/all_to_all | solution.py:220
  75.5 0.2 collective-permute-start.7
  75.7 0.4 collective-permute-start.8
  76.2 4.1 %all-to-all-done.3 = f32[8,8,128]{2,1,0:T(8,128)S(1)} async-done(((f32[8,8,128]{2,1,0:T(8,128)}), f32[8,8,128]{2,1,0:T(8,128)S(1)}, u32[]{:S(2)}, u32[]{:S(2)}) %all-to-all-start.3) | async-done | bytes 32800 | tf_op jit(solution)/shard_map/all_to_all | solution.py:220
  80.3 0.5 slice.29
  81.5 3.3 %fusion.8.wide_ref = f32[8,56,768]{2,1,0:T(8,128)} fusion(s32[8,768]{1,0:T(8,128)S(1)} %copy-done.31, s32[448]{0:T(512)S(1)} %copy-done.7, f32[]{:T(128)} %bitcast.11, bf16[56,448]{0,1:T(8,128)(2,1)S(1)} %convert_element_type.71), kind=kOutput, calls=%fused_computation.8 | convolution fusion | flops 311377920 | bytes 1452804 | tf_op jit(solution)/shard_map/ia,ran->rin/dot_general | solution.py:302
  84.9 10.2 %all-gather.3.cloned.1.call-done = bf16[11776,384]{1,0:T(8,128)(2,1)} async-done(((bf16[736,384]{1,0:T(8,128)(2,1)}), bf16[11776,384]{1,0:T(8,128)(2,1)}) %all-gather.3.cloned.1.call-update) | async-done | bytes 9043984 | tf_op jit(solution)/shard_map/all_gather | solution.py:263
  95.0 9.5 %shard_map.217 = (bf16[368,384]{1,0:T(8,128)(2,1)}, bf16[368,384]{1,0:T(8,128)(2,1)}) custom-call(s32[8]{0:T(128)} %stack.35.index_ref, f32[1,1]{1,0:T(1,128)} %rsqrt.3.scale_ref, bf16[16,736,384]{2,1,0:T(8,128)(2,1)} %bitcast.40, f32[8,56,768]{2,1,0:T(8,128)} %fusion.8.wide_ref, bf16[736,384]{1,0:T(8,128)(2,1)} %copy-done.14, bf16[736,384]{1,0:T(8,128)(2,1)} %copy-done.15, ...), custom_call_target="tpu_custom_call" | custom-call | flops 10350000128 | bytes 27000000 | tf_op jit(solution)/shard_map/pallas_call | solution.py:158
  104.6 1.3 collective-permute-start.11
  105.8 1.2 collective-permute-start.9
  107.0 1.5 collective-permute-start.13
  108.5 0.3 collective-permute-start.15
  108.8 1.8 %collective-permute-start.17 = (bf16[368,384]{1,0:T(8,128)(2,1)}, bf16[368,384]{1,0:T(8,128)(2,1)S(1)}, u32[]{:S(2)}, u32[]{:S(2)}) collective-permute-start(bf16[368,384]{1,0:T(8,128)(2,1)} %get-tuple-element.7.refs_0_), channel_id=1, source_target_pairs={{0,16},{16,0},{1,17},{17,1},{2,18},{18,2},{3,19},{19,3},{4,20},{20... | collective-permute-start | bytes 847880 | tf_op jit(solution)/shard_map/ppermute | solution.py:216
  110.6 3.1 %collective-permute-done.11.refs_5_ = bf16[368,384]{1,0:T(8,128)(2,1)S(1)} collective-permute-done((bf16[368,384]{1,0:T(8,128)(2,1)}, bf16[368,384]{1,0:T(8,128)(2,1)S(1)}, u32[]{:S(2)}, u32[]{:S(2)}) %collective-permute-start.11) | collective-permute-done | bytes 282656 | tf_op jit(solution)/shard_map/ppermute | solution.py:216
  113.7 2.7 %collective-permute-start.18 = (bf16[368,384]{1,0:T(8,128)(2,1)}, bf16[368,384]{1,0:T(8,128)(2,1)S(1)}, u32[]{:S(2)}, u32[]{:S(2)}) collective-permute-start(bf16[368,384]{1,0:T(8,128)(2,1)} %get-tuple-element.8.refs_1_), channel_id=1, source_target_pairs={{0,16},{16,0},{1,17},{17,1},{2,18},{18,2},{3,19},{19,3},{4,20},{20... | collective-permute-start | bytes 847880 | tf_op jit(solution)/shard_map/ppermute | solution.py:216
  116.4 3.4 %collective-permute-done.9.refs_4_ = bf16[368,384]{1,0:T(8,128)(2,1)S(1)} collective-permute-done((bf16[368,384]{1,0:T(8,128)(2,1)}, bf16[368,384]{1,0:T(8,128)(2,1)S(1)}, u32[]{:S(2)}, u32[]{:S(2)}) %collective-permute-start.9) | collective-permute-done | bytes 282656 | tf_op jit(solution)/shard_map/ppermute | solution.py:216
  119.8 1.8 %collective-permute-start.10 = (bf16[368,384]{1,0:T(8,128)(2,1)S(1)}, bf16[368,384]{1,0:T(8,128)(2,1)S(1)}, u32[]{:S(2)}, u32[]{:S(2)}) collective-permute-start(bf16[368,384]{1,0:T(8,128)(2,1)S(1)} %collective-permute-done.9.refs_4_), channel_id=1, source_target_pairs={{0,16},{16,0},{1,17},{17,1},{2,18},{18,2},{3,19},{19,3},{4,20},{20... | collective-permute-start | bytes 847880 | tf_op jit(solution)/shard_map/ppermute | solution.py:216
  121.5 2.7 %collective-permute-start.20 = (bf16[368,384]{1,0:T(8,128)(2,1)S(1)}, bf16[368,384]{1,0:T(8,128)(2,1)S(1)}, u32[]{:S(2)}, u32[]{:S(2)}) collective-permute-start(bf16[368,384]{1,0:T(8,128)(2,1)S(1)} %collective-permute-done.15.refs_7_), channel_id=1, source_target_pairs={{0,96},{32,0},{64,32},{96,64},{1,97},{33,1},{65,33},{97,65},{2,98}... | collective-permute-start | bytes 847880 | tf_op jit(solution)/shard_map/ppermute | solution.py:216
  124.2 1.2 collective-permute-start.12
  125.6 0.6 copy-done.30
  126.1 6.6 %shard_map.218.refs_0_.refs_8_ = f32[736,384]{1,0:T(8,128)} custom-call(s32[8]{0:T(128)} %stack.35.index_ref, f32[1,1]{1,0:T(1,128)} %rsqrt.3.scale_ref, bf16[16,736,384]{2,1,0:T(8,128)(2,1)} %bitcast.41, f32[8,56,768]{2,1,0:T(8,128)} %fusion.8.wide_ref, bf16[368,384]{1,0:T(8,128)(2,1)} %get-tuple-element.7.refs_0_, ...), custom_call_target="tpu_custom_call" | custom-call | flops 8049999872 | bytes 21000000 | tf_op jit(solution)/shard_map/pallas_call | solution.py:158
  133.0 0.5 copy-done.2
  133.6 0.4 collective-permute-start.22
  134.4 0.3 collective-permute-done.16.refs_3_
  134.7 0.7 collective-permute-done.21.refs_6_
  135.3 0.2 collective-permute-done.22.refs_7_
  135.5 0.5 copy-done.26
  136.0 0.7 copy-done.28
  136.7 7.7 %shard_map.220 = bf16[832,384]{1,0:T(8,128)(2,1)} custom-call(s32[8]{0:T(128)} %stack.35.index_ref, f32[1,1]{1,0:T(1,128)} %rsqrt.3.scale_ref, bf16[16,736,384]{2,1,0:T(8,128)(2,1)} %bitcast.42, f32[8,56,768]{2,1,0:T(8,128)} %fusion.8.wide_ref, bf16[368,384]{1,0:T(8,128)(2,1)} %copy-done.20, bf16[368,384]{1,0:T(8,128)(2,1)} %copy-done.22, ...), custom_call_target="tpu_custom_call" | custom-call | flops 10350000128 | bytes 27000000 | tf_op jit(solution)/shard_map/pallas_call | solution.py:158
  144.5 3.6 %all-to-all-start.4 = ((bf16[8,104,384]{2,1,0:T(8,128)(2,1)}), bf16[8,104,384]{2,1,0:T(8,128)(2,1)S(1)}, u32[]{:S(2)}, u32[]{:S(2)}) async-start(bf16[8,104,384]{2,1,0:T(8,128)(2,1)} %bitcast.36), calls=%async_computation.4 | async-start | bytes 1277952 | tf_op jit(solution)/shard_map/all_to_all | solution.py:327
  148.4 1.4 fusion.4.place_ref
  149.7 9.1 %all-to-all-done.4 = bf16[8,104,384]{2,1,0:T(8,128)(2,1)S(1)} async-done(((bf16[8,104,384]{2,1,0:T(8,128)(2,1)}), bf16[8,104,384]{2,1,0:T(8,128)(2,1)S(1)}, u32[]{:S(2)}, u32[]{:S(2)}) %all-to-all-start.4) | async-done | bytes 639008 | tf_op jit(solution)/shard_map/all_to_all | solution.py:327
  158.8 0.8 copy-done
  159.6 3.3 %shard_map.221 = f32[728,364]{1,0:T(8,128)} custom-call(bf16[728,832]{1,0:T(8,128)(2,1)} %fusion.4.place_ref, bf16[832,384]{1,0:T(8,128)(2,1)} %bitcast.34), custom_call_target="tpu_custom_call" | custom-call | tf_op jit(solution)/shard_map/pallas_call | solution.py:332
  (135 shorter events, 3.8 us)
Async XLA Ops:
  6.5 2.1 %copy-start.5 = (s32[56,28]{0,1:T(8,128)S(1)}, s32[56,28]{0,1:T(8,128)}, u32[]{:S(2)}) copy-start(s32[56,28]{0,1:T(8,128)} %param.25) | copy-start | bytes 18820
  6.5 8.6 %copy-start.7 = (s32[448]{0:T(512)S(1)}, s32[448]{0:T(512)}, u32[]{:S(2)}) copy-start(s32[448]{0:T(512)} %param.24) | copy-start | bytes 5380
  6.5 88.5 %all-gather.3.cloned.1.call-start = ((), (), s32[]{:S(2)}) async-start(), calls=%async_computation.5 | async-start | bytes 9609216 | tf_op jit(solution)/shard_map/all_gather | solution.py:263
  7.7 7.8 %copy-start.12 = (pred[28,28]{1,0:T(8,128)(4,1)S(1)}, pred[28,28]{1,0:T(8,128)(4,1)}, u32[]{:S(2)}) copy-start(pred[28,28]{1,0:T(8,128)(4,1)} %constant.191) | copy-start | bytes 2356
  7.7 9.5 %copy-start.6 = (pred[1,28,28]{2,0,1:T(4,128)(4,1)S(1)}, pred[1,28,28]{2,0,1:T(4,128)(4,1)}, u32[]{:S(2)}) copy-start(pred[1,28,28]{2,0,1:T(4,128)(4,1)} %constant.164.clone) | copy-start | bytes 2356
  9.4 10.5 %all-to-all-start = ((bf16[8,2,784]{2,1,0:T(2,128)(2,1)}), bf16[8,2,784]{2,1,0:T(2,128)(2,1)S(1)}, u32[]{:S(2)}, u32[]{:S(2)}) async-start(bf16[8,2,784]{2,1,0:T(2,128)(2,1)} %reshape.319), calls=%async_computation | async-start | bytes 57344 | tf_op jit(solution)/shard_map/all_to_all | solution.py:220
  18.7 9.3 %copy-start.9 = (pred[56,56]{1,0:T(8,128)(4,1)S(1)}, pred[56,56]{1,0:T(8,128)(4,1)}, u32[]{:S(2)}) copy-start(pred[56,56]{1,0:T(8,128)(4,1)} %constant.199) | copy-start | bytes 9412
  19.9 9.2 %copy-start.11 = (s32[736]{0:T(1024)S(1)}, s32[736]{0:T(1024)}, u32[]{:S(2)}) copy-start(s32[736]{0:T(1024)} %constant.169.clone) | copy-start | bytes 8836
  19.9 9.2 %copy-start.13 = (s32[384]{0:T(512)S(1)}, s32[384]{0:T(512)}, u32[]{:S(2)}) copy-start(s32[384]{0:T(512)} %constant.171.clone) | copy-start | bytes 4612
  19.9 25.1 %all-to-all-start.1 = ((bf16[16,32,736]{2,1,0:T(8,128)(2,1)}), bf16[16,32,736]{2,1,0:T(8,128)(2,1)S(1)}, u32[]{:S(2)}, u32[]{:S(2)}) async-start(bf16[16,32,736]{2,1,0:T(8,128)(2,1)} %bitcast.8), calls=%async_computation.1 | async-start | bytes 1572864 | tf_op jit(solution)/shard_map/all_to_all | solution.py:271
  29.7 16.6 %copy-start.1 = (bf16[736,384]{1,0:T(8,128)(2,1)}, bf16[736,384]{1,0:T(8,128)(2,1)S(1)}, u32[]{:S(2)}) copy-start(bf16[736,384]{1,0:T(8,128)(2,1)S(1)} %convolution_convert_fusion.2.refs_10_.refs_9_) | copy-start | bytes 1695748
  46.3 17.6 %copy-start.14 = (bf16[736,384]{1,0:T(8,128)(2,1)}, bf16[736,384]{1,0:T(8,128)(2,1)S(1)}, u32[]{:S(2)}) copy-start(bf16[736,384]{1,0:T(8,128)(2,1)S(1)} %get-tuple-element.22.refs_0_.refs_10_) | copy-start | bytes 1695748
  46.3 15.6 %copy-start.10 = (s32[736]{0:T(1024)S(1)}, s32[736]{0:T(1024)}, u32[]{:S(2)}) copy-start(s32[736]{0:T(1024)} %constant.176.clone) | copy-start | bytes 8836
  46.3 12.7 %collective-permute-start.1 = (bf16[736,384]{1,0:T(8,128)(2,1)S(1)}, bf16[736,384]{1,0:T(8,128)(2,1)S(1)}, u32[]{:S(2)}, u32[]{:S(2)}) collective-permute-start(bf16[736,384]{1,0:T(8,128)(2,1)S(1)} %get-tuple-element.22.refs_0_.refs_10_), channel_id=1, source_target_pairs={{0,32},{32,64},{64,96},{96,0},{1,33},{33,65},{65,97},{97,1},{2,34}... | collective-permute-start | bytes 1695752 | tf_op jit(solution)/shard_map/ppermute | solution.py:216
  47.6 11.6 %collective-permute-start.2 = (bf16[736,384]{1,0:T(8,128)(2,1)S(1)}, bf16[736,384]{1,0:T(8,128)(2,1)S(1)}, u32[]{:S(2)}, u32[]{:S(2)}) collective-permute-start(bf16[736,384]{1,0:T(8,128)(2,1)S(1)} %get-tuple-element.22.refs_0_.refs_10_), channel_id=1, source_target_pairs={{0,96},{32,0},{64,32},{96,64},{1,97},{33,1},{65,33},{97,65},{2,98}... | collective-permute-start | bytes 1695752 | tf_op jit(solution)/shard_map/ppermute | solution.py:216
  50.7 17.5 %all-to-all-start.2 = ((f32[16,1,1792]{2,1,0:T(1,128)}), f32[16,1,1792]{2,1,0:T(1,128)S(1)}, u32[]{:S(2)}, u32[]{:S(2)}) async-start(f32[16,1,1792]{2,1,0:T(1,128)} %reshape.321), calls=%async_computation.2 | async-start | bytes 229376 | tf_op jit(solution)/shard_map/all_to_all | solution.py:220
  59.0 10.7 %copy-start.3 = (bf16[736,384]{1,0:T(8,128)(2,1)}, bf16[736,384]{1,0:T(8,128)(2,1)S(1)}, u32[]{:S(2)}) copy-start(bf16[736,384]{1,0:T(8,128)(2,1)S(1)} %collective-permute-done.1.refs_2_) | copy-start | bytes 1695748
  59.1 16.5 %collective-permute-start.5 = (bf16[368,384]{1,0:T(8,128)(2,1)S(1)}, bf16[368,384]{1,0:T(8,128)(2,1)S(1)}, u32[]{:S(2)}, u32[]{:S(2)}) collective-permute-start(bf16[368,384]{1,0:T(8,128)(2,1)S(1)} %slice.35), channel_id=1, source_target_pairs={{0,32},{32,64},{64,96},{96,0},{1,33},{33,65},{65,97},{97,1},{2,34}... | collective-permute-start | bytes 847880 | tf_op jit(solution)/shard_map/ppermute | solution.py:216
  59.2 10.7 %copy-start.4 = (bf16[736,384]{1,0:T(8,128)(2,1)}, bf16[736,384]{1,0:T(8,128)(2,1)S(1)}, u32[]{:S(2)}) copy-start(bf16[736,384]{1,0:T(8,128)(2,1)S(1)} %collective-permute-done.2.refs_3_) | copy-start | bytes 1695748
  59.3 22.3 %copy-start.31 = (s32[8,768]{1,0:T(8,128)S(1)}, s32[8,768]{1,0:T(8,128)}, u32[]{:S(2)}) copy-start(s32[8,768]{1,0:T(8,128)} %constant.198) | copy-start | bytes 73732
  59.3 16.5 %collective-permute-start.6 = (bf16[368,384]{1,0:T(8,128)(2,1)S(1)}, bf16[368,384]{1,0:T(8,128)(2,1)}, u32[]{:S(2)}, u32[]{:S(2)}) collective-permute-start(bf16[368,384]{1,0:T(8,128)(2,1)S(1)} %slice.36), channel_id=1, source_target_pairs={{0,96},{32,0},{64,32},{96,64},{1,97},{33,1},{65,33},{97,65},{2,98}... | collective-permute-start | bytes 847880 | tf_op jit(solution)/shard_map/ppermute | solution.py:216
  63.9 20.9 %collective-permute-start = (bf16[736,384]{1,0:T(8,128)(2,1)S(1)}, bf16[736,384]{1,0:T(8,128)(2,1)S(1)}, u32[]{:S(2)}, u32[]{:S(2)}) collective-permute-start(bf16[736,384]{1,0:T(8,128)(2,1)S(1)} %get-tuple-element.22.refs_0_.refs_10_), channel_id=1, source_target_pairs={{0,16},{16,0},{1,17},{17,1},{2,18},{18,2},{3,19},{19,3},{4,20},{20... | collective-permute-start | bytes 1695752 | tf_op jit(solution)/shard_map/ppermute | solution.py:216
  69.8 15.1 %collective-permute-start.3 = (bf16[736,384]{1,0:T(8,128)(2,1)S(1)}, bf16[736,384]{1,0:T(8,128)(2,1)}, u32[]{:S(2)}, u32[]{:S(2)}) collective-permute-start(bf16[736,384]{1,0:T(8,128)(2,1)S(1)} %collective-permute-done.1.refs_2_), channel_id=1, source_target_pairs={{0,16},{16,0},{1,17},{17,1},{2,18},{18,2},{3,19},{19,3},{4,20},{20... | collective-permute-start | bytes 1695752 | tf_op jit(solution)/shard_map/ppermute | solution.py:216
  69.9 15.0 %collective-permute-start.4 = (bf16[736,384]{1,0:T(8,128)(2,1)S(1)}, bf16[736,384]{1,0:T(8,128)(2,1)}, u32[]{:S(2)}, u32[]{:S(2)}) collective-permute-start(bf16[736,384]{1,0:T(8,128)(2,1)S(1)} %collective-permute-done.2.refs_3_), channel_id=1, source_target_pairs={{0,16},{16,0},{1,17},{17,1},{2,18},{18,2},{3,19},{19,3},{4,20},{20... | collective-permute-start | bytes 1695752 | tf_op jit(solution)/shard_map/ppermute | solution.py:216
  72.2 8.1 %all-to-all-start.3 = ((f32[8,8,128]{2,1,0:T(8,128)}), f32[8,8,128]{2,1,0:T(8,128)S(1)}, u32[]{:S(2)}, u32[]{:S(2)}) async-start(f32[8,8,128]{2,1,0:T(8,128)} %broadcast_in_dim_broadcast_in_dim_broadcast_in_dim.3), calls=%async_computation.3 | async-start | bytes 65536 | tf_op jit(solution)/shard_map/all_to_all | solution.py:220
  75.5 9.3 %copy-start.16 = (bf16[368,384]{1,0:T(8,128)(2,1)}, bf16[368,384]{1,0:T(8,128)(2,1)S(1)}, u32[]{:S(2)}) copy-start(bf16[368,384]{1,0:T(8,128)(2,1)S(1)} %collective-permute-done.5.refs_6_) | copy-start | bytes 847876
  75.5 9.3 %collective-permute-start.7 = (bf16[368,384]{1,0:T(8,128)(2,1)S(1)}, bf16[368,384]{1,0:T(8,128)(2,1)}, u32[]{:S(2)}, u32[]{:S(2)}) collective-permute-start(bf16[368,384]{1,0:T(8,128)(2,1)S(1)} %collective-permute-done.5.refs_6_), channel_id=1, source_target_pairs={{0,16},{16,0},{1,17},{17,1},{2,18},{18,2},{3,19},{19,3},{4,20},{20... | collective-permute-start | bytes 847880 | tf_op jit(solution)/shard_map/ppermute | solution.py:216
  75.7 9.1 %collective-permute-start.8 = (bf16[368,384]{1,0:T(8,128)(2,1)}, bf16[368,384]{1,0:T(8,128)(2,1)S(1)}, u32[]{:S(2)}, u32[]{:S(2)}) collective-permute-start(bf16[368,384]{1,0:T(8,128)(2,1)} %collective-permute-done.6.refs_7_), channel_id=1, source_target_pairs={{0,16},{16,0},{1,17},{17,1},{2,18},{18,2},{3,19},{19,3},{4,20},{20... | collective-permute-start | bytes 847880 | tf_op jit(solution)/shard_map/ppermute | solution.py:216
  84.8 10.2 %copy-start.15 = (bf16[736,384]{1,0:T(8,128)(2,1)}, bf16[736,384]{1,0:T(8,128)(2,1)S(1)}, u32[]{:S(2)}) copy-start(bf16[736,384]{1,0:T(8,128)(2,1)S(1)} %collective-permute-done.refs_1_) | copy-start | bytes 1695748
  84.8 10.2 %copy-start.27 = (bf16[368,384]{1,0:T(8,128)(2,1)}, bf16[368,384]{1,0:T(8,128)(2,1)S(1)}, u32[]{:S(2)}) copy-start(bf16[368,384]{1,0:T(8,128)(2,1)S(1)} %collective-permute-done.8.refs_9_) | copy-start | bytes 847876
  104.6 9.1 %collective-permute-start.11 = (bf16[368,384]{1,0:T(8,128)(2,1)}, bf16[368,384]{1,0:T(8,128)(2,1)S(1)}, u32[]{:S(2)}, u32[]{:S(2)}) collective-permute-start(bf16[368,384]{1,0:T(8,128)(2,1)} %get-tuple-element.8.refs_1_), channel_id=1, source_target_pairs={{0,32},{32,64},{64,96},{96,0},{1,33},{33,65},{65,97},{97,1},{2,34}... | collective-permute-start | bytes 847880 | tf_op jit(solution)/shard_map/ppermute | solution.py:216
  105.8 13.9 %collective-permute-start.9 = (bf16[368,384]{1,0:T(8,128)(2,1)}, bf16[368,384]{1,0:T(8,128)(2,1)S(1)}, u32[]{:S(2)}, u32[]{:S(2)}) collective-permute-start(bf16[368,384]{1,0:T(8,128)(2,1)} %get-tuple-element.7.refs_0_), channel_id=1, source_target_pairs={{0,32},{32,64},{64,96},{96,0},{1,33},{33,65},{65,97},{97,1},{2,34}... | collective-permute-start | bytes 847880 | tf_op jit(solution)/shard_map/ppermute | solution.py:216
  107.0 12.7 %collective-permute-start.13 = (bf16[368,384]{1,0:T(8,128)(2,1)}, bf16[368,384]{1,0:T(8,128)(2,1)S(1)}, u32[]{:S(2)}, u32[]{:S(2)}) collective-permute-start(bf16[368,384]{1,0:T(8,128)(2,1)} %get-tuple-element.7.refs_0_), channel_id=1, source_target_pairs={{0,96},{32,0},{64,32},{96,64},{1,97},{33,1},{65,33},{97,65},{2,98}... | collective-permute-start | bytes 847880 | tf_op jit(solution)/shard_map/ppermute | solution.py:216
  108.5 13.0 %collective-permute-start.15 = (bf16[368,384]{1,0:T(8,128)(2,1)}, bf16[368,384]{1,0:T(8,128)(2,1)S(1)}, u32[]{:S(2)}, u32[]{:S(2)}) collective-permute-start(bf16[368,384]{1,0:T(8,128)(2,1)} %get-tuple-element.8.refs_1_), channel_id=1, source_target_pairs={{0,96},{32,0},{64,32},{96,64},{1,97},{33,1},{65,33},{97,65},{2,98}... | collective-permute-start | bytes 847880 | tf_op jit(solution)/shard_map/ppermute | solution.py:216
  108.8 15.5 %collective-permute-start.17 = (bf16[368,384]{1,0:T(8,128)(2,1)}, bf16[368,384]{1,0:T(8,128)(2,1)S(1)}, u32[]{:S(2)}, u32[]{:S(2)}) collective-permute-start(bf16[368,384]{1,0:T(8,128)(2,1)} %get-tuple-element.7.refs_0_), channel_id=1, source_target_pairs={{0,16},{16,0},{1,17},{17,1},{2,18},{18,2},{3,19},{19,3},{4,20},{20... | collective-permute-start | bytes 847880 | tf_op jit(solution)/shard_map/ppermute | solution.py:216
  113.7 11.9 %copy-start.17 = (bf16[368,384]{1,0:T(8,128)(2,1)}, bf16[368,384]{1,0:T(8,128)(2,1)S(1)}, u32[]{:S(2)}) copy-start(bf16[368,384]{1,0:T(8,128)(2,1)S(1)} %collective-permute-done.11.refs_5_) | copy-start | bytes 847876
  113.7 11.8 %collective-permute-start.18 = (bf16[368,384]{1,0:T(8,128)(2,1)}, bf16[368,384]{1,0:T(8,128)(2,1)S(1)}, u32[]{:S(2)}, u32[]{:S(2)}) collective-permute-start(bf16[368,384]{1,0:T(8,128)(2,1)} %get-tuple-element.8.refs_1_), channel_id=1, source_target_pairs={{0,16},{16,0},{1,17},{17,1},{2,18},{18,2},{3,19},{19,3},{4,20},{20... | collective-permute-start | bytes 847880 | tf_op jit(solution)/shard_map/ppermute | solution.py:216
  119.7 5.8 %copy-start.23 = (bf16[368,384]{1,0:T(8,128)(2,1)}, bf16[368,384]{1,0:T(8,128)(2,1)S(1)}, u32[]{:S(2)}) copy-start(bf16[368,384]{1,0:T(8,128)(2,1)S(1)} %collective-permute-done.9.refs_4_) | copy-start | bytes 847876
  119.7 13.0 %collective-permute-start.19 = (bf16[368,384]{1,0:T(8,128)(2,1)S(1)}, bf16[368,384]{1,0:T(8,128)(2,1)S(1)}, u32[]{:S(2)}, u32[]{:S(2)}) collective-permute-start(bf16[368,384]{1,0:T(8,128)(2,1)S(1)} %collective-permute-done.9.refs_4_), channel_id=1, source_target_pairs={{0,32},{32,64},{64,96},{96,0},{1,33},{33,65},{65,97},{97,1},{2,34}... | collective-permute-start | bytes 847880 | tf_op jit(solution)/shard_map/ppermute | solution.py:216
  119.7 5.8 %copy-start.18 = (bf16[368,384]{1,0:T(8,128)(2,1)}, bf16[368,384]{1,0:T(8,128)(2,1)S(1)}, u32[]{:S(2)}) copy-start(bf16[368,384]{1,0:T(8,128)(2,1)S(1)} %collective-permute-done.13.refs_6_) | copy-start | bytes 847876
  119.8 13.9 %collective-permute-start.10 = (bf16[368,384]{1,0:T(8,128)(2,1)S(1)}, bf16[368,384]{1,0:T(8,128)(2,1)S(1)}, u32[]{:S(2)}, u32[]{:S(2)}) collective-permute-start(bf16[368,384]{1,0:T(8,128)(2,1)S(1)} %collective-permute-done.9.refs_4_), channel_id=1, source_target_pairs={{0,16},{16,0},{1,17},{17,1},{2,18},{18,2},{3,19},{19,3},{4,20},{20... | collective-permute-start | bytes 847880 | tf_op jit(solution)/shard_map/ppermute | solution.py:216
  121.5 4.0 %copy-start.19 = (bf16[368,384]{1,0:T(8,128)(2,1)}, bf16[368,384]{1,0:T(8,128)(2,1)S(1)}, u32[]{:S(2)}) copy-start(bf16[368,384]{1,0:T(8,128)(2,1)S(1)} %collective-permute-done.15.refs_7_) | copy-start | bytes 847876
  121.5 12.0 %collective-permute-start.20 = (bf16[368,384]{1,0:T(8,128)(2,1)S(1)}, bf16[368,384]{1,0:T(8,128)(2,1)S(1)}, u32[]{:S(2)}, u32[]{:S(2)}) collective-permute-start(bf16[368,384]{1,0:T(8,128)(2,1)S(1)} %collective-permute-done.15.refs_7_), channel_id=1, source_target_pairs={{0,96},{32,0},{64,32},{96,64},{1,97},{33,1},{65,33},{97,65},{2,98}... | collective-permute-start | bytes 847880 | tf_op jit(solution)/shard_map/ppermute | solution.py:216
  124.2 1.3 copy-start.29
  124.2 10.1 %collective-permute-start.12 = (bf16[368,384]{1,0:T(8,128)(2,1)S(1)}, bf16[368,384]{1,0:T(8,128)(2,1)S(1)}, u32[]{:S(2)}, u32[]{:S(2)}) collective-permute-start(bf16[368,384]{1,0:T(8,128)(2,1)S(1)} %collective-permute-done.11.refs_5_), channel_id=1, source_target_pairs={{0,16},{16,0},{1,17},{17,1},{2,18},{18,2},{3,19},{19,3},{4,20},{20... | collective-permute-start | bytes 847880 | tf_op jit(solution)/shard_map/ppermute | solution.py:216
  125.4 0.7 copy-start.30
  125.4 8.9 %collective-permute-start.14 = (bf16[368,384]{1,0:T(8,128)(2,1)S(1)}, bf16[368,384]{1,0:T(8,128)(2,1)S(1)}, u32[]{:S(2)}, u32[]{:S(2)}) collective-permute-start(bf16[368,384]{1,0:T(8,128)(2,1)S(1)} %collective-permute-done.13.refs_6_), channel_id=1, source_target_pairs={{0,16},{16,0},{1,17},{17,1},{2,18},{18,2},{3,19},{19,3},{4,20},{20... | collective-permute-start | bytes 847880 | tf_op jit(solution)/shard_map/ppermute | solution.py:216
  132.8 1.4 copy-start.8
  132.8 0.7 copy-start.2
  132.8 1.9 %collective-permute-start.16 = (bf16[368,384]{1,0:T(8,128)(2,1)}, bf16[368,384]{1,0:T(8,128)(2,1)S(1)}, u32[]{:S(2)}, u32[]{:S(2)}) collective-permute-start(bf16[368,384]{1,0:T(8,128)(2,1)} %copy-done.19), channel_id=1, source_target_pairs={{0,16},{16,0},{1,17},{17,1},{2,18},{18,2},{3,19},{19,3},{4,20},{20... | collective-permute-start | bytes 847880 | tf_op jit(solution)/shard_map/ppermute | solution.py:216
  133.5 2.0 %copy-start.21 = (bf16[368,384]{1,0:T(8,128)(2,1)}, bf16[368,384]{1,0:T(8,128)(2,1)S(1)}, u32[]{:S(2)}) copy-start(bf16[368,384]{1,0:T(8,128)(2,1)S(1)} %collective-permute-done.20.refs_5_) | copy-start | bytes 847876
  133.5 1.8 %collective-permute-start.21 = (bf16[368,384]{1,0:T(8,128)(2,1)}, bf16[368,384]{1,0:T(8,128)(2,1)S(1)}, u32[]{:S(2)}, u32[]{:S(2)}) collective-permute-start(bf16[368,384]{1,0:T(8,128)(2,1)} %shard_map.219.refs_4_), channel_id=1, source_target_pairs={{0,16},{16,0},{1,17},{17,1},{2,18},{18,2},{3,19},{19,3},{4,20},{20... | collective-permute-start | bytes 847880 | tf_op jit(solution)/shard_map/ppermute | solution.py:216
  133.6 1.9 %copy-start.20 = (bf16[368,384]{1,0:T(8,128)(2,1)}, bf16[368,384]{1,0:T(8,128)(2,1)S(1)}, u32[]{:S(2)}) copy-start(bf16[368,384]{1,0:T(8,128)(2,1)S(1)} %collective-permute-done.10.refs_0_) | copy-start | bytes 847876
  133.6 1.9 %collective-permute-start.22 = (bf16[368,384]{1,0:T(8,128)(2,1)S(1)}, bf16[368,384]{1,0:T(8,128)(2,1)S(1)}, u32[]{:S(2)}, u32[]{:S(2)}) collective-permute-start(bf16[368,384]{1,0:T(8,128)(2,1)S(1)} %collective-permute-done.20.refs_5_), channel_id=1, source_target_pairs={{0,16},{16,0},{1,17},{17,1},{2,18},{18,2},{3,19},{19,3},{4,20},{20... | collective-permute-start | bytes 847880 | tf_op jit(solution)/shard_map/ppermute | solution.py:216
  134.3 1.2 copy-start.22
  134.3 1.2 copy-start.24
  134.7 0.9 copy-start.25
  135.3 0.7 copy-start.26
  136.0 0.7 copy-start.28
  144.5 14.3 %all-to-all-start.4 = ((bf16[8,104,384]{2,1,0:T(8,128)(2,1)}), bf16[8,104,384]{2,1,0:T(8,128)(2,1)S(1)}, u32[]{:S(2)}, u32[]{:S(2)}) async-start(bf16[8,104,384]{2,1,0:T(8,128)(2,1)} %bitcast.36), calls=%async_computation.4 | async-start | bytes 1277952 | tf_op jit(solution)/shard_map/all_to_all | solution.py:327
  158.8 0.8 copy-start
Sparse Core Ops, SparseCore 0:
  9.5 85.4 all-gather.2

commit v4 on v3

--- a/solution.py
+++ b/solution.py
@@ -196,11 +196,6 @@
     outs[0][...] = jnp.dot(pack[...], value, preferred_element_type=F32).astype(BF)
 
 
-def unpack_body(place_ref, arrived_ref, out_ref):
-    value = jnp.dot(place_ref[...], arrived_ref[...], preferred_element_type=F32)
-    out_ref[...] = value[:, : out_ref.shape[1]]
-
-
 def after(ready, arrays):
     anywhere = pl.BlockSpec(memory_space=pl.ANY)
     return pl.pallas_call(
@@ -329,12 +324,7 @@
     source, rank = arrivals(new_atom, row_here, atoms_row)
     spot = (((source * slots_row + rank) * NBF)[:, None] + np.arange(NBF)).reshape(-1)
     place_rows = eq(spot[:, None], np.arange(row_count * slots_row * NBF)[None, :])
-    return pl.pallas_call(
-        unpack_body,
-        out_shape=jax.ShapeDtypeStruct((rows_here, cols_here), F32),
-        in_specs=[whole, whole],
-        out_specs=whole,
-    )(place_rows, got_rows)
+    return jnp.dot(place_rows, got_rows[:, :cols_here], preferred_element_type=F32)
 
 
 def solution(mesh):

time: 170 us -> 168 us (0.988)
  Pallas kernels: 27.2 us -> 23.9 us
  matrix products: 6.07 us -> 8.01 us
    pallas_call x1 -> x0, Pallas kernels: 3.35 us -> none  [on_device(): pl.pallas_call(unpack_body, out_shape=jax.ShapeDtypeStruct((rows_here, co...]
    dot_general x0 -> x1, matrix products: none -> 1.98 us  [on_device(): jnp.dot(place_rows, got_rows[:, :cols_here], preferred_element_type=F32)]
    unnamed x70 -> x68, local copies, waits for them, and re-layouts: 5.11 us -> 4.26 us
  transfers between devices with their start and end apart: 29 -> 29, of which waited for: 10 -> 10; matrix products, arithmetic and copies ran while one was open for 13% -> 12% of each run, Pallas kernels for 4% -> 4%
where the time goes in v4:
time: 168 us
  starting transfers between devices  51.8 us (31%)
  waiting for transfers between devices  51 us (30%)
  Pallas kernels  23.9 us (14%)
  between operations  14.6 us (9%)
  local copies, waits for them, and re-layouts  11.8 us (7%)
  matrix products  8.01 us (5%)
  other arithmetic  6.58 us (4%)
    ppermute x23, starting transfers between devices, send(): return lax.ppermute(array, axis, shift(2 if axis == 'c' else 4, by))  26.1 us
    pallas_call x3, Pallas kernels, multiply(): pl.pallas_call(body, out_shape=out_shape, grid=(count // 2,), in_specs=[s...  23.9 us
    all_to_all x1, waiting for transfers between devices, on_device(): lax.all_to_all(outgoing.reshape(col_count, width, 2 * TALL), COL, 0, 0)  15.3 us
    all_to_all x3, starting transfers between devices, from_all(): lax.all_to_all(jnp.broadcast_to(array[None], (count,) + array.shape), axe...  14.2 us
    ppermute x23, waiting for transfers between devices, send(): return lax.ppermute(array, axis, shift(2 if axis == 'c' else 4, by))  11.1 us
    all_to_all x1, waiting for transfers between devices, on_device(): lax.all_to_all(sent_rows.reshape(row_count, slots_row * NBF, WIDE), ROW,...  10.2 us
    all_gather x1, waiting for transfers between devices, on_device(): panel = lax.all_gather(padded, COL, axis=0)  10.2 us
    all_to_all x1, starting transfers between devices, on_device(): lax.all_to_all(outgoing.reshape(col_count, width, 2 * TALL), COL, 0, 0)  7.91 us
  transfers between devices with their start and end apart: 29, of which 10 were waited for; matrix products, arithmetic and copies ran while one was open for 12% of the time, Pallas kernels for 4%

profile of v4, /device:TPU:1, one launch (start us, length us, event | category | flops | bytes accessed | tf_op | source)
XLA Modules:
  0.0 167.6 jit_solution(4224217392986699382)
XLA Ops:
  6.5 1.1 fusion.37
  7.7 0.9 fusion.16
  8.6 0.7 reshape.319
  9.4 5.8 %all-to-all-start = ((bf16[8,2,784]{2,1,0:T(2,128)(2,1)}), bf16[8,2,784]{2,1,0:T(2,128)(2,1)S(1)}, u32[]{:S(2)}, u32[]{:S(2)}) async-start(bf16[8,2,784]{2,1,0:T(2,128)(2,1)} %reshape.319), calls=%async_computation | async-start | bytes 57344 | tf_op jit(solution)/shard_map/all_to_all | solution.py:215
  15.5 0.6 convert_reduce_fusion.1
  17.2 0.7 fusion.31
  18.0 0.7 convolution_convert_fusion
  18.7 1.2 copy.39
  19.9 7.9 %all-to-all-start.1 = ((bf16[16,32,736]{2,1,0:T(8,128)(2,1)}), bf16[16,32,736]{2,1,0:T(8,128)(2,1)S(1)}, u32[]{:S(2)}, u32[]{:S(2)}) async-start(bf16[16,32,736]{2,1,0:T(8,128)(2,1)} %bitcast.8), calls=%async_computation.1 | async-start | bytes 1572864 | tf_op jit(solution)/shard_map/all_to_all | solution.py:266
  28.0 0.3 convert_reduce_fusion
  28.3 0.2 select_reduce_fusion
  28.9 0.2 convolution_convert_fusion.4
  29.1 0.6 convolution_convert_fusion.2.refs_10_.refs_9_
  29.7 15.3 %all-to-all-done.1 = bf16[16,32,736]{2,1,0:T(8,128)(2,1)S(1)} async-done(((bf16[16,32,736]{2,1,0:T(8,128)(2,1)}), bf16[16,32,736]{2,1,0:T(8,128)(2,1)S(1)}, u32[]{:S(2)}, u32[]{:S(2)}) %all-to-all-start.1) | async-done | bytes 753696 | tf_op jit(solution)/shard_map/all_to_all | solution.py:266
  45.0 1.3 multiply_reduce_fusion
  46.3 1.3 collective-permute-start.1
  47.6 1.4 collective-permute-start.2
  49.2 0.7 concatenate.7
  49.9 0.8 reshape.321
  50.7 5.0 %all-to-all-start.2 = ((f32[16,1,1792]{2,1,0:T(1,128)}), f32[16,1,1792]{2,1,0:T(1,128)S(1)}, u32[]{:S(2)}, u32[]{:S(2)}) async-start(f32[16,1,1792]{2,1,0:T(1,128)} %reshape.321), calls=%async_computation.2 | async-start | bytes 229376 | tf_op jit(solution)/shard_map/all_to_all | solution.py:215
  55.8 3.2 %collective-permute-done.1.refs_2_ = bf16[736,384]{1,0:T(8,128)(2,1)S(1)} collective-permute-done((bf16[736,384]{1,0:T(8,128)(2,1)S(1)}, bf16[736,384]{1,0:T(8,128)(2,1)S(1)}, u32[]{:S(2)}, u32[]{:S(2)}) %collective-permute-start.1) | collective-permute-done | bytes 565280 | tf_op jit(solution)/shard_map/ppermute | solution.py:211
  59.3 2.7 %collective-permute-start.6 = (bf16[368,384]{1,0:T(8,128)(2,1)S(1)}, bf16[368,384]{1,0:T(8,128)(2,1)}, u32[]{:S(2)}, u32[]{:S(2)}) collective-permute-start(bf16[368,384]{1,0:T(8,128)(2,1)S(1)} %slice.40), channel_id=1, source_target_pairs={{0,96},{32,0},{64,32},{96,64},{1,97},{33,1},{65,33},{97,65},{2,98}... | collective-permute-start | bytes 847880 | tf_op jit(solution)/shard_map/ppermute | solution.py:211
  61.9 1.3 compare_convert_fusion.refs_11_
  63.3 0.6 stack.35.index_ref
  63.9 4.3 %collective-permute-start = (bf16[736,384]{1,0:T(8,128)(2,1)S(1)}, bf16[736,384]{1,0:T(8,128)(2,1)S(1)}, u32[]{:S(2)}, u32[]{:S(2)}) collective-permute-start(bf16[736,384]{1,0:T(8,128)(2,1)S(1)} %get-tuple-element.22.refs_0_.refs_10_), channel_id=1, source_target_pairs={{0,16},{16,0},{1,17},{17,1},{2,18},{18,2},{3,19},{19,3},{4,20},{20... | collective-permute-start | bytes 1695752 | tf_op jit(solution)/shard_map/ppermute | solution.py:211
  68.2 0.5 broadcast.371
  68.7 0.9 reduce.3
  69.8 0.5 collective-permute-start.4
  70.3 0.7 slice_reduce_fusion
  71.0 1.2 broadcast_in_dim_broadcast_in_dim_broadcast_in_dim.3
  72.2 3.3 %all-to-all-start.3 = ((f32[8,8,128]{2,1,0:T(8,128)}), f32[8,8,128]{2,1,0:T(8,128)S(1)}, u32[]{:S(2)}, u32[]{:S(2)}) async-start(f32[8,8,128]{2,1,0:T(8,128)} %broadcast_in_dim_broadcast_in_dim_broadcast_in_dim.3), calls=%async_computation.3 | async-start | bytes 65536 | tf_op jit(solution)/shard_map/all_to_all | solution.py:215
  75.6 0.2 collective-permute-start.7
  75.8 0.4 collective-permute-start.8
  76.2 4.1 %all-to-all-done.3 = f32[8,8,128]{2,1,0:T(8,128)S(1)} async-done(((f32[8,8,128]{2,1,0:T(8,128)}), f32[8,8,128]{2,1,0:T(8,128)S(1)}, u32[]{:S(2)}, u32[]{:S(2)}) %all-to-all-start.3) | async-done | bytes 32800 | tf_op jit(solution)/shard_map/all_to_all | solution.py:215
  80.4 0.5 slice.32
  81.6 3.2 %fusion.8.wide_ref = f32[8,56,768]{2,1,0:T(8,128)} fusion(s32[8,768]{1,0:T(8,128)S(1)} %copy-done.30, s32[448]{0:T(512)S(1)} %copy-done.6, f32[]{:T(128)} %bitcast.11, bf16[56,448]{0,1:T(8,128)(2,1)S(1)} %convert_element_type.68), kind=kOutput, calls=%fused_computation.8 | convolution fusion | flops 311377920 | bytes 1452804 | tf_op jit(solution)/shard_map/ia,ran->rin/dot_general | solution.py:297
  84.9 10.2 %all-gather.3.cloned.1.call-done = bf16[11776,384]{1,0:T(8,128)(2,1)} async-done(((bf16[736,384]{1,0:T(8,128)(2,1)}), bf16[11776,384]{1,0:T(8,128)(2,1)}) %all-gather.3.cloned.1.call-update) | async-done | bytes 9043984 | tf_op jit(solution)/shard_map/all_gather | solution.py:258
  95.0 9.5 %shard_map.217 = (bf16[368,384]{1,0:T(8,128)(2,1)}, bf16[368,384]{1,0:T(8,128)(2,1)}) custom-call(s32[8]{0:T(128)} %stack.35.index_ref, f32[1,1]{1,0:T(1,128)} %rsqrt.3.scale_ref, bf16[16,736,384]{2,1,0:T(8,128)(2,1)} %bitcast.40, f32[8,56,768]{2,1,0:T(8,128)} %fusion.8.wide_ref, bf16[736,384]{1,0:T(8,128)(2,1)} %copy-done.13, bf16[736,384]{1,0:T(8,128)(2,1)} %copy-done.14, ...), custom_call_target="tpu_custom_call" | custom-call | flops 10350000128 | bytes 27000000 | tf_op jit(solution)/shard_map/pallas_call | solution.py:158
  104.6 1.3 collective-permute-start.11
  105.8 1.2 collective-permute-start.9
  107.0 1.5 collective-permute-start.13
  108.5 0.3 collective-permute-start.15
  108.8 1.8 %collective-permute-start.17 = (bf16[368,384]{1,0:T(8,128)(2,1)}, bf16[368,384]{1,0:T(8,128)(2,1)S(1)}, u32[]{:S(2)}, u32[]{:S(2)}) collective-permute-start(bf16[368,384]{1,0:T(8,128)(2,1)} %get-tuple-element.7.refs_0_), channel_id=1, source_target_pairs={{0,16},{16,0},{1,17},{17,1},{2,18},{18,2},{3,19},{19,3},{4,20},{20... | collective-permute-start | bytes 847880 | tf_op jit(solution)/shard_map/ppermute | solution.py:211
  110.6 3.1 %collective-permute-done.11.refs_5_ = bf16[368,384]{1,0:T(8,128)(2,1)S(1)} collective-permute-done((bf16[368,384]{1,0:T(8,128)(2,1)}, bf16[368,384]{1,0:T(8,128)(2,1)S(1)}, u32[]{:S(2)}, u32[]{:S(2)}) %collective-permute-start.11) | collective-permute-done | bytes 282656 | tf_op jit(solution)/shard_map/ppermute | solution.py:211
  113.7 2.7 %collective-permute-start.18 = (bf16[368,384]{1,0:T(8,128)(2,1)}, bf16[368,384]{1,0:T(8,128)(2,1)S(1)}, u32[]{:S(2)}, u32[]{:S(2)}) collective-permute-start(bf16[368,384]{1,0:T(8,128)(2,1)} %get-tuple-element.8.refs_1_), channel_id=1, source_target_pairs={{0,16},{16,0},{1,17},{17,1},{2,18},{18,2},{3,19},{19,3},{4,20},{20... | collective-permute-start | bytes 847880 | tf_op jit(solution)/shard_map/ppermute | solution.py:211
  116.4 3.4 %collective-permute-done.9.refs_4_ = bf16[368,384]{1,0:T(8,128)(2,1)S(1)} collective-permute-done((bf16[368,384]{1,0:T(8,128)(2,1)}, bf16[368,384]{1,0:T(8,128)(2,1)S(1)}, u32[]{:S(2)}, u32[]{:S(2)}) %collective-permute-start.9) | collective-permute-done | bytes 282656 | tf_op jit(solution)/shard_map/ppermute | solution.py:211
  119.7 1.8 %collective-permute-start.10 = (bf16[368,384]{1,0:T(8,128)(2,1)S(1)}, bf16[368,384]{1,0:T(8,128)(2,1)S(1)}, u32[]{:S(2)}, u32[]{:S(2)}) collective-permute-start(bf16[368,384]{1,0:T(8,128)(2,1)S(1)} %collective-permute-done.9.refs_4_), channel_id=1, source_target_pairs={{0,16},{16,0},{1,17},{17,1},{2,18},{18,2},{3,19},{19,3},{4,20},{20... | collective-permute-start | bytes 847880 | tf_op jit(solution)/shard_map/ppermute | solution.py:211
  121.5 2.7 %collective-permute-start.20 = (bf16[368,384]{1,0:T(8,128)(2,1)S(1)}, bf16[368,384]{1,0:T(8,128)(2,1)S(1)}, u32[]{:S(2)}, u32[]{:S(2)}) collective-permute-start(bf16[368,384]{1,0:T(8,128)(2,1)S(1)} %collective-permute-done.15.refs_7_), channel_id=1, source_target_pairs={{0,96},{32,0},{64,32},{96,64},{1,97},{33,1},{65,33},{97,65},{2,98}... | collective-permute-start | bytes 847880 | tf_op jit(solution)/shard_map/ppermute | solution.py:211
  124.2 1.2 collective-permute-start.12
  125.5 0.6 copy-done.29
  126.1 6.6 %shard_map.218.refs_0_.refs_8_ = f32[736,384]{1,0:T(8,128)} custom-call(s32[8]{0:T(128)} %stack.35.index_ref, f32[1,1]{1,0:T(1,128)} %rsqrt.3.scale_ref, bf16[16,736,384]{2,1,0:T(8,128)(2,1)} %bitcast.41, f32[8,56,768]{2,1,0:T(8,128)} %fusion.8.wide_ref, bf16[368,384]{1,0:T(8,128)(2,1)} %get-tuple-element.7.refs_0_, ...), custom_call_target="tpu_custom_call" | custom-call | flops 8049999872 | bytes 21000000 | tf_op jit(solution)/shard_map/pallas_call | solution.py:158
  132.8 0.2 collective-permute-start.16
  133.0 0.5 copy-done.1
  133.6 0.4 collective-permute-start.22
  134.2 0.5 collective-permute-done.16.refs_3_
  134.6 0.7 collective-permute-done.21.refs_6_
  135.3 0.2 collective-permute-done.22.refs_7_
  135.5 0.5 copy-done.26
  136.0 0.7 copy-done.28
  136.7 7.7 %shard_map.220 = bf16[832,384]{1,0:T(8,128)(2,1)} custom-call(s32[8]{0:T(128)} %stack.35.index_ref, f32[1,1]{1,0:T(1,128)} %rsqrt.3.scale_ref, bf16[16,736,384]{2,1,0:T(8,128)(2,1)} %bitcast.42, f32[8,56,768]{2,1,0:T(8,128)} %fusion.8.wide_ref, bf16[368,384]{1,0:T(8,128)(2,1)} %copy-done.19, bf16[368,384]{1,0:T(8,128)(2,1)} %copy-done.22, ...), custom_call_target="tpu_custom_call" | custom-call | flops 10350000128 | bytes 27000000 | tf_op jit(solution)/shard_map/pallas_call | solution.py:158
  144.5 3.6 %all-to-all-start.4 = ((bf16[8,104,384]{2,1,0:T(8,128)(2,1)}), bf16[8,104,384]{2,1,0:T(8,128)(2,1)S(1)}, u32[]{:S(2)}, u32[]{:S(2)}) async-start(bf16[8,104,384]{2,1,0:T(8,128)(2,1)} %bitcast.35), calls=%async_computation.4 | async-start | bytes 1277952 | tf_op jit(solution)/shard_map/all_to_all | solution.py:322
  148.1 0.2 convert_reduce_fusion.2
  148.5 10.2 %all-to-all-done.4 = bf16[8,104,384]{2,1,0:T(8,128)(2,1)S(1)} async-done(((bf16[8,104,384]{2,1,0:T(8,128)(2,1)}), bf16[8,104,384]{2,1,0:T(8,128)(2,1)S(1)}, u32[]{:S(2)}, u32[]{:S(2)}) %all-to-all-start.4) | async-done | bytes 639008 | tf_op jit(solution)/shard_map/all_to_all | solution.py:322
  158.8 2.0 %fusion.4 = f32[728,364]{1,0:T(8,128)} fusion(s32[728]{0:T(1024)S(1)} %add.252, bf16[832,384]{1,0:T(8,128)(2,1)S(1)} %bitcast.36), kind=kOutput, calls=%fused_computation.5 | convolution fusion | flops 441552384 | bytes 1701856 | tf_op jit(solution)/shard_map/dot_general | solution.py:327
  (132 shorter events, 3.5 us)
Async XLA Ops:
  6.5 88.5 %all-gather.3.cloned.1.call-start = ((), (), s32[]{:S(2)}) async-start(), calls=%async_computation.5 | async-start | bytes 9609216 | tf_op jit(solution)/shard_map/all_gather | solution.py:258
  7.7 0.9 copy-start.4
  7.7 7.5 %copy-start.6 = (s32[448]{0:T(512)S(1)}, s32[448]{0:T(512)}, u32[]{:S(2)}) copy-start(s32[448]{0:T(512)} %param.24) | copy-start | bytes 5380
  7.7 7.8 %copy-start.11 = (pred[28,28]{1,0:T(8,128)(4,1)S(1)}, pred[28,28]{1,0:T(8,128)(4,1)}, u32[]{:S(2)}) copy-start(pred[28,28]{1,0:T(8,128)(4,1)} %constant.191) | copy-start | bytes 2356
  7.7 9.5 %copy-start.5 = (pred[1,28,28]{2,0,1:T(4,128)(4,1)S(1)}, pred[1,28,28]{2,0,1:T(4,128)(4,1)}, u32[]{:S(2)}) copy-start(pred[1,28,28]{2,0,1:T(4,128)(4,1)} %constant.164.clone) | copy-start | bytes 2356
  9.4 10.5 %all-to-all-start = ((bf16[8,2,784]{2,1,0:T(2,128)(2,1)}), bf16[8,2,784]{2,1,0:T(2,128)(2,1)S(1)}, u32[]{:S(2)}, u32[]{:S(2)}) async-start(bf16[8,2,784]{2,1,0:T(2,128)(2,1)} %reshape.319), calls=%async_computation | async-start | bytes 57344 | tf_op jit(solution)/shard_map/all_to_all | solution.py:215
  19.9 8.1 %copy-start.8 = (pred[56,56]{1,0:T(8,128)(4,1)S(1)}, pred[56,56]{1,0:T(8,128)(4,1)}, u32[]{:S(2)}) copy-start(pred[56,56]{1,0:T(8,128)(4,1)} %constant.199) | copy-start | bytes 9412
  19.9 9.2 %copy-start.10 = (s32[736]{0:T(1024)S(1)}, s32[736]{0:T(1024)}, u32[]{:S(2)}) copy-start(s32[736]{0:T(1024)} %constant.169.clone) | copy-start | bytes 8836
  19.9 9.2 %copy-start.12 = (s32[384]{0:T(512)S(1)}, s32[384]{0:T(512)}, u32[]{:S(2)}) copy-start(s32[384]{0:T(512)} %constant.171.clone) | copy-start | bytes 4612
  19.9 25.1 %all-to-all-start.1 = ((bf16[16,32,736]{2,1,0:T(8,128)(2,1)}), bf16[16,32,736]{2,1,0:T(8,128)(2,1)S(1)}, u32[]{:S(2)}, u32[]{:S(2)}) async-start(bf16[16,32,736]{2,1,0:T(8,128)(2,1)} %bitcast.8), calls=%async_computation.1 | async-start | bytes 1572864 | tf_op jit(solution)/shard_map/all_to_all | solution.py:266
  29.7 16.6 %copy-start = (bf16[736,384]{1,0:T(8,128)(2,1)}, bf16[736,384]{1,0:T(8,128)(2,1)S(1)}, u32[]{:S(2)}) copy-start(bf16[736,384]{1,0:T(8,128)(2,1)S(1)} %convolution_convert_fusion.2.refs_10_.refs_9_) | copy-start | bytes 1695748
  46.3 17.5 %copy-start.13 = (bf16[736,384]{1,0:T(8,128)(2,1)}, bf16[736,384]{1,0:T(8,128)(2,1)S(1)}, u32[]{:S(2)}) copy-start(bf16[736,384]{1,0:T(8,128)(2,1)S(1)} %get-tuple-element.22.refs_0_.refs_10_) | copy-start | bytes 1695748
  46.3 15.6 %copy-start.9 = (s32[736]{0:T(1024)S(1)}, s32[736]{0:T(1024)}, u32[]{:S(2)}) copy-start(s32[736]{0:T(1024)} %constant.176.clone) | copy-start | bytes 8836
  46.3 12.7 %collective-permute-start.1 = (bf16[736,384]{1,0:T(8,128)(2,1)S(1)}, bf16[736,384]{1,0:T(8,128)(2,1)S(1)}, u32[]{:S(2)}, u32[]{:S(2)}) collective-permute-start(bf16[736,384]{1,0:T(8,128)(2,1)S(1)} %get-tuple-element.22.refs_0_.refs_10_), channel_id=1, source_target_pairs={{0,32},{32,64},{64,96},{96,0},{1,33},{33,65},{65,97},{97,1},{2,34}... | collective-permute-start | bytes 1695752 | tf_op jit(solution)/shard_map/ppermute | solution.py:211
  47.6 11.6 %collective-permute-start.2 = (bf16[736,384]{1,0:T(8,128)(2,1)S(1)}, bf16[736,384]{1,0:T(8,128)(2,1)S(1)}, u32[]{:S(2)}, u32[]{:S(2)}) collective-permute-start(bf16[736,384]{1,0:T(8,128)(2,1)S(1)} %get-tuple-element.22.refs_0_.refs_10_), channel_id=1, source_target_pairs={{0,96},{32,0},{64,32},{96,64},{1,97},{33,1},{65,33},{97,65},{2,98}... | collective-permute-start | bytes 1695752 | tf_op jit(solution)/shard_map/ppermute | solution.py:211
  50.7 17.4 %all-to-all-start.2 = ((f32[16,1,1792]{2,1,0:T(1,128)}), f32[16,1,1792]{2,1,0:T(1,128)S(1)}, u32[]{:S(2)}, u32[]{:S(2)}) async-start(f32[16,1,1792]{2,1,0:T(1,128)} %reshape.321), calls=%async_computation.2 | async-start | bytes 229376 | tf_op jit(solution)/shard_map/all_to_all | solution.py:215
  59.0 10.7 %copy-start.2 = (bf16[736,384]{1,0:T(8,128)(2,1)}, bf16[736,384]{1,0:T(8,128)(2,1)S(1)}, u32[]{:S(2)}) copy-start(bf16[736,384]{1,0:T(8,128)(2,1)S(1)} %collective-permute-done.1.refs_2_) | copy-start | bytes 1695748
  59.0 16.5 %collective-permute-start.5 = (bf16[368,384]{1,0:T(8,128)(2,1)S(1)}, bf16[368,384]{1,0:T(8,128)(2,1)S(1)}, u32[]{:S(2)}, u32[]{:S(2)}) collective-permute-start(bf16[368,384]{1,0:T(8,128)(2,1)S(1)} %slice.39), channel_id=1, source_target_pairs={{0,32},{32,64},{64,96},{96,0},{1,33},{33,65},{65,97},{97,1},{2,34}... | collective-permute-start | bytes 847880 | tf_op jit(solution)/shard_map/ppermute | solution.py:211
  59.2 10.6 %copy-start.3 = (bf16[736,384]{1,0:T(8,128)(2,1)}, bf16[736,384]{1,0:T(8,128)(2,1)S(1)}, u32[]{:S(2)}) copy-start(bf16[736,384]{1,0:T(8,128)(2,1)S(1)} %collective-permute-done.2.refs_3_) | copy-start | bytes 1695748
  59.3 22.3 %copy-start.30 = (s32[8,768]{1,0:T(8,128)S(1)}, s32[8,768]{1,0:T(8,128)}, u32[]{:S(2)}) copy-start(s32[8,768]{1,0:T(8,128)} %constant.198) | copy-start | bytes 73732
  59.3 16.5 %collective-permute-start.6 = (bf16[368,384]{1,0:T(8,128)(2,1)S(1)}, bf16[368,384]{1,0:T(8,128)(2,1)}, u32[]{:S(2)}, u32[]{:S(2)}) collective-permute-start(bf16[368,384]{1,0:T(8,128)(2,1)S(1)} %slice.40), channel_id=1, source_target_pairs={{0,96},{32,0},{64,32},{96,64},{1,97},{33,1},{65,33},{97,65},{2,98}... | collective-permute-start | bytes 847880 | tf_op jit(solution)/shard_map/ppermute | solution.py:211
  63.9 21.0 %collective-permute-start = (bf16[736,384]{1,0:T(8,128)(2,1)S(1)}, bf16[736,384]{1,0:T(8,128)(2,1)S(1)}, u32[]{:S(2)}, u32[]{:S(2)}) collective-permute-start(bf16[736,384]{1,0:T(8,128)(2,1)S(1)} %get-tuple-element.22.refs_0_.refs_10_), channel_id=1, source_target_pairs={{0,16},{16,0},{1,17},{17,1},{2,18},{18,2},{3,19},{19,3},{4,20},{20... | collective-permute-start | bytes 1695752 | tf_op jit(solution)/shard_map/ppermute | solution.py:211
  69.7 15.1 %collective-permute-start.3 = (bf16[736,384]{1,0:T(8,128)(2,1)S(1)}, bf16[736,384]{1,0:T(8,128)(2,1)}, u32[]{:S(2)}, u32[]{:S(2)}) collective-permute-start(bf16[736,384]{1,0:T(8,128)(2,1)S(1)} %collective-permute-done.1.refs_2_), channel_id=1, source_target_pairs={{0,16},{16,0},{1,17},{17,1},{2,18},{18,2},{3,19},{19,3},{4,20},{20... | collective-permute-start | bytes 1695752 | tf_op jit(solution)/shard_map/ppermute | solution.py:211
  69.8 15.1 %collective-permute-start.4 = (bf16[736,384]{1,0:T(8,128)(2,1)S(1)}, bf16[736,384]{1,0:T(8,128)(2,1)}, u32[]{:S(2)}, u32[]{:S(2)}) collective-permute-start(bf16[736,384]{1,0:T(8,128)(2,1)S(1)} %collective-permute-done.2.refs_3_), channel_id=1, source_target_pairs={{0,16},{16,0},{1,17},{17,1},{2,18},{18,2},{3,19},{19,3},{4,20},{20... | collective-permute-start | bytes 1695752 | tf_op jit(solution)/shard_map/ppermute | solution.py:211
  72.2 8.1 %all-to-all-start.3 = ((f32[8,8,128]{2,1,0:T(8,128)}), f32[8,8,128]{2,1,0:T(8,128)S(1)}, u32[]{:S(2)}, u32[]{:S(2)}) async-start(f32[8,8,128]{2,1,0:T(8,128)} %broadcast_in_dim_broadcast_in_dim_broadcast_in_dim.3), calls=%async_computation.3 | async-start | bytes 65536 | tf_op jit(solution)/shard_map/all_to_all | solution.py:215
  75.6 9.2 %copy-start.15 = (bf16[368,384]{1,0:T(8,128)(2,1)}, bf16[368,384]{1,0:T(8,128)(2,1)S(1)}, u32[]{:S(2)}) copy-start(bf16[368,384]{1,0:T(8,128)(2,1)S(1)} %collective-permute-done.5.refs_6_) | copy-start | bytes 847876
  75.6 9.3 %collective-permute-start.7 = (bf16[368,384]{1,0:T(8,128)(2,1)S(1)}, bf16[368,384]{1,0:T(8,128)(2,1)}, u32[]{:S(2)}, u32[]{:S(2)}) collective-permute-start(bf16[368,384]{1,0:T(8,128)(2,1)S(1)} %collective-permute-done.5.refs_6_), channel_id=1, source_target_pairs={{0,16},{16,0},{1,17},{17,1},{2,18},{18,2},{3,19},{19,3},{4,20},{20... | collective-permute-start | bytes 847880 | tf_op jit(solution)/shard_map/ppermute | solution.py:211
  75.8 9.1 %collective-permute-start.8 = (bf16[368,384]{1,0:T(8,128)(2,1)}, bf16[368,384]{1,0:T(8,128)(2,1)S(1)}, u32[]{:S(2)}, u32[]{:S(2)}) collective-permute-start(bf16[368,384]{1,0:T(8,128)(2,1)} %collective-permute-done.6.refs_7_), channel_id=1, source_target_pairs={{0,16},{16,0},{1,17},{17,1},{2,18},{18,2},{3,19},{19,3},{4,20},{20... | collective-permute-start | bytes 847880 | tf_op jit(solution)/shard_map/ppermute | solution.py:211
  84.8 10.2 %copy-start.14 = (bf16[736,384]{1,0:T(8,128)(2,1)}, bf16[736,384]{1,0:T(8,128)(2,1)S(1)}, u32[]{:S(2)}) copy-start(bf16[736,384]{1,0:T(8,128)(2,1)S(1)} %collective-permute-done.refs_1_) | copy-start | bytes 1695748
  84.8 10.2 %copy-start.25 = (bf16[368,384]{1,0:T(8,128)(2,1)}, bf16[368,384]{1,0:T(8,128)(2,1)S(1)}, u32[]{:S(2)}) copy-start(bf16[368,384]{1,0:T(8,128)(2,1)S(1)} %collective-permute-done.8.refs_9_) | copy-start | bytes 847876
  104.6 9.1 %collective-permute-start.11 = (bf16[368,384]{1,0:T(8,128)(2,1)}, bf16[368,384]{1,0:T(8,128)(2,1)S(1)}, u32[]{:S(2)}, u32[]{:S(2)}) collective-permute-start(bf16[368,384]{1,0:T(8,128)(2,1)} %get-tuple-element.8.refs_1_), channel_id=1, source_target_pairs={{0,32},{32,64},{64,96},{96,0},{1,33},{33,65},{65,97},{97,1},{2,34}... | collective-permute-start | bytes 847880 | tf_op jit(solution)/shard_map/ppermute | solution.py:211
  105.8 13.9 %collective-permute-start.9 = (bf16[368,384]{1,0:T(8,128)(2,1)}, bf16[368,384]{1,0:T(8,128)(2,1)S(1)}, u32[]{:S(2)}, u32[]{:S(2)}) collective-permute-start(bf16[368,384]{1,0:T(8,128)(2,1)} %get-tuple-element.7.refs_0_), channel_id=1, source_target_pairs={{0,32},{32,64},{64,96},{96,0},{1,33},{33,65},{65,97},{97,1},{2,34}... | collective-permute-start | bytes 847880 | tf_op jit(solution)/shard_map/ppermute | solution.py:211
  107.0 12.7 %collective-permute-start.13 = (bf16[368,384]{1,0:T(8,128)(2,1)}, bf16[368,384]{1,0:T(8,128)(2,1)S(1)}, u32[]{:S(2)}, u32[]{:S(2)}) collective-permute-start(bf16[368,384]{1,0:T(8,128)(2,1)} %get-tuple-element.7.refs_0_), channel_id=1, source_target_pairs={{0,96},{32,0},{64,32},{96,64},{1,97},{33,1},{65,33},{97,65},{2,98}... | collective-permute-start | bytes 847880 | tf_op jit(solution)/shard_map/ppermute | solution.py:211
  108.5 13.0 %collective-permute-start.15 = (bf16[368,384]{1,0:T(8,128)(2,1)}, bf16[368,384]{1,0:T(8,128)(2,1)S(1)}, u32[]{:S(2)}, u32[]{:S(2)}) collective-permute-start(bf16[368,384]{1,0:T(8,128)(2,1)} %get-tuple-element.8.refs_1_), channel_id=1, source_target_pairs={{0,96},{32,0},{64,32},{96,64},{1,97},{33,1},{65,33},{97,65},{2,98}... | collective-permute-start | bytes 847880 | tf_op jit(solution)/shard_map/ppermute | solution.py:211
  108.8 15.5 %collective-permute-start.17 = (bf16[368,384]{1,0:T(8,128)(2,1)}, bf16[368,384]{1,0:T(8,128)(2,1)S(1)}, u32[]{:S(2)}, u32[]{:S(2)}) collective-permute-start(bf16[368,384]{1,0:T(8,128)(2,1)} %get-tuple-element.7.refs_0_), channel_id=1, source_target_pairs={{0,16},{16,0},{1,17},{17,1},{2,18},{18,2},{3,19},{19,3},{4,20},{20... | collective-permute-start | bytes 847880 | tf_op jit(solution)/shard_map/ppermute | solution.py:211
  113.7 11.9 %copy-start.16 = (bf16[368,384]{1,0:T(8,128)(2,1)}, bf16[368,384]{1,0:T(8,128)(2,1)S(1)}, u32[]{:S(2)}) copy-start(bf16[368,384]{1,0:T(8,128)(2,1)S(1)} %collective-permute-done.11.refs_5_) | copy-start | bytes 847876
  113.7 11.8 %collective-permute-start.18 = (bf16[368,384]{1,0:T(8,128)(2,1)}, bf16[368,384]{1,0:T(8,128)(2,1)S(1)}, u32[]{:S(2)}, u32[]{:S(2)}) collective-permute-start(bf16[368,384]{1,0:T(8,128)(2,1)} %get-tuple-element.8.refs_1_), channel_id=1, source_target_pairs={{0,16},{16,0},{1,17},{17,1},{2,18},{18,2},{3,19},{19,3},{4,20},{20... | collective-permute-start | bytes 847880 | tf_op jit(solution)/shard_map/ppermute | solution.py:211
  119.7 5.8 %copy-start.21 = (bf16[368,384]{1,0:T(8,128)(2,1)}, bf16[368,384]{1,0:T(8,128)(2,1)S(1)}, u32[]{:S(2)}) copy-start(bf16[368,384]{1,0:T(8,128)(2,1)S(1)} %collective-permute-done.9.refs_4_) | copy-start | bytes 847876
  119.7 13.0 %collective-permute-start.19 = (bf16[368,384]{1,0:T(8,128)(2,1)S(1)}, bf16[368,384]{1,0:T(8,128)(2,1)S(1)}, u32[]{:S(2)}, u32[]{:S(2)}) collective-permute-start(bf16[368,384]{1,0:T(8,128)(2,1)S(1)} %collective-permute-done.9.refs_4_), channel_id=1, source_target_pairs={{0,32},{32,64},{64,96},{96,0},{1,33},{33,65},{65,97},{97,1},{2,34}... | collective-permute-start | bytes 847880 | tf_op jit(solution)/shard_map/ppermute | solution.py:211
  119.7 5.8 %copy-start.17 = (bf16[368,384]{1,0:T(8,128)(2,1)}, bf16[368,384]{1,0:T(8,128)(2,1)S(1)}, u32[]{:S(2)}) copy-start(bf16[368,384]{1,0:T(8,128)(2,1)S(1)} %collective-permute-done.13.refs_6_) | copy-start | bytes 847876
  119.7 13.9 %collective-permute-start.10 = (bf16[368,384]{1,0:T(8,128)(2,1)S(1)}, bf16[368,384]{1,0:T(8,128)(2,1)S(1)}, u32[]{:S(2)}, u32[]{:S(2)}) collective-permute-start(bf16[368,384]{1,0:T(8,128)(2,1)S(1)} %collective-permute-done.9.refs_4_), channel_id=1, source_target_pairs={{0,16},{16,0},{1,17},{17,1},{2,18},{18,2},{3,19},{19,3},{4,20},{20... | collective-permute-start | bytes 847880 | tf_op jit(solution)/shard_map/ppermute | solution.py:211
  121.5 4.0 %copy-start.18 = (bf16[368,384]{1,0:T(8,128)(2,1)}, bf16[368,384]{1,0:T(8,128)(2,1)S(1)}, u32[]{:S(2)}) copy-start(bf16[368,384]{1,0:T(8,128)(2,1)S(1)} %collective-permute-done.15.refs_7_) | copy-start | bytes 847876
  121.5 12.0 %collective-permute-start.20 = (bf16[368,384]{1,0:T(8,128)(2,1)S(1)}, bf16[368,384]{1,0:T(8,128)(2,1)S(1)}, u32[]{:S(2)}, u32[]{:S(2)}) collective-permute-start(bf16[368,384]{1,0:T(8,128)(2,1)S(1)} %collective-permute-done.15.refs_7_), channel_id=1, source_target_pairs={{0,96},{32,0},{64,32},{96,64},{1,97},{33,1},{65,33},{97,65},{2,98}... | collective-permute-start | bytes 847880 | tf_op jit(solution)/shard_map/ppermute | solution.py:211
  124.2 1.3 copy-start.27
  124.2 9.9 %collective-permute-start.12 = (bf16[368,384]{1,0:T(8,128)(2,1)S(1)}, bf16[368,384]{1,0:T(8,128)(2,1)S(1)}, u32[]{:S(2)}, u32[]{:S(2)}) collective-permute-start(bf16[368,384]{1,0:T(8,128)(2,1)S(1)} %collective-permute-done.11.refs_5_), channel_id=1, source_target_pairs={{0,16},{16,0},{1,17},{17,1},{2,18},{18,2},{3,19},{19,3},{4,20},{20... | collective-permute-start | bytes 847880 | tf_op jit(solution)/shard_map/ppermute | solution.py:211
  125.4 0.7 copy-start.29
  125.4 8.7 %collective-permute-start.14 = (bf16[368,384]{1,0:T(8,128)(2,1)S(1)}, bf16[368,384]{1,0:T(8,128)(2,1)S(1)}, u32[]{:S(2)}, u32[]{:S(2)}) collective-permute-start(bf16[368,384]{1,0:T(8,128)(2,1)S(1)} %collective-permute-done.13.refs_6_), channel_id=1, source_target_pairs={{0,16},{16,0},{1,17},{17,1},{2,18},{18,2},{3,19},{19,3},{4,20},{20... | collective-permute-start | bytes 847880 | tf_op jit(solution)/shard_map/ppermute | solution.py:211
  132.8 0.7 copy-start.1
  132.8 1.9 %collective-permute-start.16 = (bf16[368,384]{1,0:T(8,128)(2,1)}, bf16[368,384]{1,0:T(8,128)(2,1)S(1)}, u32[]{:S(2)}, u32[]{:S(2)}) collective-permute-start(bf16[368,384]{1,0:T(8,128)(2,1)} %copy-done.18), channel_id=1, source_target_pairs={{0,16},{16,0},{1,17},{17,1},{2,18},{18,2},{3,19},{19,3},{4,20},{20... | collective-permute-start | bytes 847880 | tf_op jit(solution)/shard_map/ppermute | solution.py:211
  133.5 2.0 %copy-start.20 = (bf16[368,384]{1,0:T(8,128)(2,1)}, bf16[368,384]{1,0:T(8,128)(2,1)S(1)}, u32[]{:S(2)}) copy-start(bf16[368,384]{1,0:T(8,128)(2,1)S(1)} %collective-permute-done.20.refs_5_) | copy-start | bytes 847876
  133.5 1.8 %collective-permute-start.21 = (bf16[368,384]{1,0:T(8,128)(2,1)}, bf16[368,384]{1,0:T(8,128)(2,1)S(1)}, u32[]{:S(2)}, u32[]{:S(2)}) collective-permute-start(bf16[368,384]{1,0:T(8,128)(2,1)} %shard_map.219.refs_4_), channel_id=1, source_target_pairs={{0,16},{16,0},{1,17},{17,1},{2,18},{18,2},{3,19},{19,3},{4,20},{20... | collective-permute-start | bytes 847880 | tf_op jit(solution)/shard_map/ppermute | solution.py:211
  133.6 1.8 %copy-start.19 = (bf16[368,384]{1,0:T(8,128)(2,1)}, bf16[368,384]{1,0:T(8,128)(2,1)S(1)}, u32[]{:S(2)}) copy-start(bf16[368,384]{1,0:T(8,128)(2,1)S(1)} %collective-permute-done.10.refs_0_) | copy-start | bytes 847876
  133.6 1.8 %collective-permute-start.22 = (bf16[368,384]{1,0:T(8,128)(2,1)S(1)}, bf16[368,384]{1,0:T(8,128)(2,1)S(1)}, u32[]{:S(2)}, u32[]{:S(2)}) collective-permute-start(bf16[368,384]{1,0:T(8,128)(2,1)S(1)} %collective-permute-done.20.refs_5_), channel_id=1, source_target_pairs={{0,16},{16,0},{1,17},{17,1},{2,18},{18,2},{3,19},{19,3},{4,20},{20... | collective-permute-start | bytes 847880 | tf_op jit(solution)/shard_map/ppermute | solution.py:211
  134.1 1.4 copy-start.22
  134.1 1.3 copy-start.23
  134.6 0.9 copy-start.24
  135.3 0.7 copy-start.26
  136.0 0.7 copy-start.28
  144.4 3.6 %copy-start.7 = (pred[1,56,56]{2,1,0:T(8,128)(4,1)S(1)}, pred[1,56,56]{2,1,0:T(8,128)(4,1)}, u32[]{:S(2)}) copy-start(pred[1,56,56]{2,1,0:T(8,128)(4,1)} %constant.174.clone) | copy-start | bytes 9412
  144.5 14.3 %all-to-all-start.4 = ((bf16[8,104,384]{2,1,0:T(8,128)(2,1)}), bf16[8,104,384]{2,1,0:T(8,128)(2,1)S(1)}, u32[]{:S(2)}, u32[]{:S(2)}) async-start(bf16[8,104,384]{2,1,0:T(8,128)(2,1)} %bitcast.35), calls=%async_computation.4 | async-start | bytes 1277952 | tf_op jit(solution)/shard_map/all_to_all | solution.py:322
Sparse Core Ops, SparseCore 0:
  9.5 85.4 all-gather.2
